TPU v7x, 512 devices: a whole 4x4x16 slice. The times are simulated.
512 devices in a mesh: prompt: 16 (over z_hi, y), tp: 32 (over x, z_lo, core).
Axes of the slice: x: 4, y: 4, z: 16 (z_hi: 4, z_lo: 4; z = z_hi * 4 + z_lo), core: 2. Of those that a mesh axis runs over, the one named last changes fastest.
Arguments:
- prompt_keys: bfloat16 [16, 8, 8192, 128], P('prompt', None, 'tp'), may hold values from -13 to 13
- prompt_values: bfloat16 [16, 8, 8192, 128], P('prompt', None, 'tp'), may hold values from -24 to 24
- queries: bfloat16 [16, 3, 64, 16384], P('prompt', None, None, 'tp'), may hold values from -80 to 80
- sample_step_keys: bfloat16 [16, 3, 64, 8, 128], P('prompt', None, 'tp'), may hold values from -9 to 9
- suffix_values: bfloat16 [16, 3, 64, 8, 128], P('prompt', None, 'tp'), may hold values from -24 to 24
- suffix_lengths: int32 [16, 64], P('prompt'), may hold values from 1 to 3, as said below
- assignment: int32 [16], replicated, may hold values from 0 to 15, each once
Outputs:
- attended: bfloat16 [16, 3, 64, 16384], P('prompt', None, None, 'tp')
Inputs may be any that keep to these rules, and one draw needn't show every extreme that they name: `suffix_lengths`: in every rollout group some sample generates 3 tokens and some sample generates 1.
All inputs are finite; a program needn't handle non-finite values.
Results may differ from a plain program's by a relative error of at most 0.0038.
Values may be sent and summed in bfloat16 or wider, within the bound.
No kernel may reach another device: no remote copies, remote signals or barrier semaphores. Data moves between devices by JAX's collectives and lax.ppermute only.
A program may use at most 64 MiB of HBM per device.

v0:
```python
import jax
import jax.numpy as jnp
from jax import lax
from jax.sharding import PartitionSpec as P


def local(
    prompt_keys, prompt_values, queries, sample_step_keys, suffix_values, suffix_lengths, assignment
):
    n_tp = lax.axis_size("tp")
    n_prompt = lax.axis_size("prompt")
    kv_heads = prompt_keys.shape[1]
    block_len = prompt_keys.shape[2]
    head_size = prompt_keys.shape[3]
    sample_group = n_tp // kv_heads
    steps = queries.shape[1]
    samples = queries.shape[2]
    local_heads = queries.shape[3] // head_size
    score_scale = head_size ** (-0.5)
    piece = block_len // n_prompt
    split_keys = prompt_keys.reshape(kv_heads, n_prompt, piece, head_size)
    split_values = prompt_values.reshape(kv_heads, n_prompt, piece, head_size)
    spread_keys, spread_values = (
        lax.all_to_all(split_keys, "prompt", split_axis=1, concat_axis=1, tiled=True),
        lax.all_to_all(split_values, "prompt", split_axis=1, concat_axis=1, tiled=True),
    )
    chosen_keys = jnp.take(spread_keys, assignment, axis=1)
    chosen_values = jnp.take(spread_values, assignment, axis=1)
    keys_block, values_block = (
        lax.all_to_all(chosen_keys, "prompt", split_axis=1, concat_axis=1, tiled=True),
        lax.all_to_all(chosen_values, "prompt", split_axis=1, concat_axis=1, tiled=True),
    )
    keys_block = keys_block.reshape(kv_heads, block_len, head_size)
    values_block = values_block.reshape(kv_heads, block_len, head_size)
    relayed = (
        jnp.repeat(keys_block, sample_group, axis=0),
        jnp.repeat(values_block, sample_group, axis=0),
    )
    head_keys, head_values = (
        lax.all_to_all(relayed[0], "tp", split_axis=0, concat_axis=1, tiled=True),
        lax.all_to_all(relayed[1], "tp", split_axis=0, concat_axis=1, tiled=True),
    )
    head_keys = head_keys.reshape(-1, head_size)
    head_values = head_values.reshape(-1, head_size)
    length = head_keys.shape[0]
    tile = min(512, length)
    count = length // tile
    keys_tiles = head_keys.reshape(count, tile, head_size)
    values_tiles = head_values.reshape(count, tile, head_size)
    rows = queries.reshape(steps * samples * local_heads, head_size)
    n_rows = rows.shape[0]

    def tile_scores(keys_tile):
        return (
            lax.dot_general(
                rows, keys_tile, (((1,), (1,)), ((), ())), preferred_element_type=jnp.float32
            )
            * score_scale
        )

    def tile_max(carry, keys_tile):
        return (jnp.maximum(carry, jnp.max(tile_scores(keys_tile), axis=-1)), None)

    prefix_top, unused = lax.scan(tile_max, jnp.full((n_rows,), -jnp.inf, jnp.float32), keys_tiles)
    fresh = (
        jnp.repeat(sample_step_keys, sample_group, axis=3),
        jnp.repeat(suffix_values, sample_group, axis=3),
    )
    fresh_keys, fresh_values = (
        lax.all_to_all(fresh[0], "tp", split_axis=3, concat_axis=2, tiled=True),
        lax.all_to_all(fresh[1], "tp", split_axis=3, concat_axis=2, tiled=True),
    )
    fresh_keys = fresh_keys.reshape(steps, samples, head_size)
    fresh_values = fresh_values.reshape(steps, samples, head_size)
    query_four = queries.reshape(steps, samples, local_heads, head_size)
    suffix_tokens = (
        jnp.einsum("evyc,wvc->evyw", query_four, fresh_keys, preferred_element_type=jnp.float32)
        * score_scale
    )
    step_now = lax.broadcasted_iota(jnp.int32, (steps, 1, 1, steps), 0)
    step_key = lax.broadcasted_iota(jnp.int32, (steps, 1, 1, steps), 3)
    causal = step_key <= step_now
    suffix_tokens = jnp.where(causal, suffix_tokens, -jnp.inf)
    top = jnp.maximum(prefix_top, jnp.max(suffix_tokens, axis=-1).reshape(-1))
    weight_suf = jnp.where(
        causal, jnp.exp(suffix_tokens - top.reshape(steps, samples, local_heads)[..., None]), 0.0
    )

    def tile_sum(carry, pair):
        weights = jnp.exp(tile_scores(pair[0]) - top[:, None])
        total_now = carry[0] + jnp.sum(weights, axis=-1)
        numer_now = carry[1] + jnp.dot(
            weights.astype(jnp.bfloat16), pair[1], preferred_element_type=jnp.float32
        )
        return ((total_now, numer_now), None)

    start = (jnp.zeros((n_rows,), jnp.float32), jnp.zeros((n_rows, head_size), jnp.float32))
    (prefix_total, prefix_numer), unused = lax.scan(tile_sum, start, (keys_tiles, values_tiles))
    total = prefix_total + jnp.sum(weight_suf, axis=-1).reshape(-1)
    numer = prefix_numer + jnp.einsum(
        "siht,tid->sihd",
        weight_suf.astype(jnp.bfloat16),
        fresh_values,
        preferred_element_type=jnp.float32,
    ).reshape(-1, head_size)
    result = (numer / total[:, None]).reshape(steps, samples, local_heads, head_size)
    live_samples = jnp.arange(steps, dtype=jnp.int32)[:, None] < suffix_lengths[0][None, :]
    result = jnp.where(live_samples[:, :, None, None], result, 0.0)
    return result.reshape(1, steps, samples, local_heads * head_size).astype(jnp.bfloat16)


def solution(mesh):
    in_specs = (
        P("prompt", None, "tp", None),
        P("prompt", None, "tp", None),
        P("prompt", None, None, "tp"),
        P("prompt", None, "tp", None, None),
        P("prompt", None, "tp", None, None),
        P("prompt", None),
        P(),
    )
    out_specs = P("prompt", None, None, "tp")
    return jax.shard_map(local, mesh=mesh, in_specs=in_specs, out_specs=out_specs, check_vma=False)
```

profile of v0, /device:TPU:1, one launch (start us, length us, event | category | flops | bytes accessed | tf_op | source)
XLA Modules:
  0.0 336.1 jit_solution(7033155962234818548)
XLA Ops:
  0.0 2.0 copy.56
  2.0 18.4 %all-to-all-start = ((bf16[8,16,16,128]{3,2,0,1:T(8,128)(2,1)}), bf16[8,16,16,128]{3,2,0,1:T(8,128)(2,1)S(1)}, u32[]{:S(2)}, u32[]{:S(2)}) async-start(bf16[8,16,16,128]{3,2,0,1:T(8,128)(2,1)} %copy.56), calls=%async_computation | async-start | bytes 1048576 | tf_op jit(solution)/shard_map/all_to_all | solution.py:24
  21.2 18.6 %all-to-all-done = bf16[8,16,16,128]{3,2,0,1:T(8,128)(2,1)S(1)} async-done(((bf16[8,16,16,128]{3,2,0,1:T(8,128)(2,1)}), bf16[8,16,16,128]{3,2,0,1:T(8,128)(2,1)S(1)}, u32[]{:S(2)}, u32[]{:S(2)}) %all-to-all-start) | async-done | bytes 524320 | tf_op jit(solution)/shard_map/all_to_all | solution.py:24
  39.9 16.8 %all-to-all-start.4 = ((bf16[8,16,16,128]{3,2,0,1:T(8,128)(2,1)}), bf16[8,16,16,128]{3,2,0,1:T(8,128)(2,1)S(1)}, u32[]{:S(2)}, u32[]{:S(2)}) async-start(bf16[8,16,16,128]{3,2,0,1:T(8,128)(2,1)} %copy.65), calls=%async_computation.4 | async-start | bytes 1048576 | tf_op jit(solution)/shard_map/all_to_all | solution.py:25
  56.8 17.3 %all-to-all-done.4 = bf16[8,16,16,128]{3,2,0,1:T(8,128)(2,1)S(1)} async-done(((bf16[8,16,16,128]{3,2,0,1:T(8,128)(2,1)}), bf16[8,16,16,128]{3,2,0,1:T(8,128)(2,1)S(1)}, u32[]{:S(2)}, u32[]{:S(2)}) %all-to-all-start.4) | async-done | bytes 524320 | tf_op jit(solution)/shard_map/all_to_all | solution.py:25
  74.8 21.7 %all-to-all-start.3 = ((bf16[1,3,2,32,128]{4,2,1,0,3:T(2,128)(2,1)}), bf16[1,3,2,32,128]{4,2,1,0,3:T(2,128)(2,1)S(1)}, u32[]{:S(2)}, u32[]{:S(2)}) async-start(bf16[1,3,2,32,128]{4,2,1,0,3:T(2,128)(2,1)} %bitcast.7), calls=%async_computation.3 | async-start | bytes 98304 | tf_op jit(solution)/shard_map/all_to_all | solution.py:70
  98.0 6.2 %all-to-all-done.3 = bf16[1,3,2,32,128]{4,2,1,0,3:T(2,128)(2,1)S(1)} async-done(((bf16[1,3,2,32,128]{4,2,1,0,3:T(2,128)(2,1)}), bf16[1,3,2,32,128]{4,2,1,0,3:T(2,128)(2,1)S(1)}, u32[]{:S(2)}, u32[]{:S(2)}) %all-to-all-start.3) | async-done | bytes 49184 | tf_op jit(solution)/shard_map/all_to_all | solution.py:70
  104.8 4.0 %all-to-all-start.7 = ((bf16[1,3,2,32,128]{4,2,1,0,3:T(2,128)(2,1)}), bf16[1,3,2,32,128]{4,2,1,0,3:T(2,128)(2,1)S(1)}, u32[]{:S(2)}, u32[]{:S(2)}) async-start(bf16[1,3,2,32,128]{4,2,1,0,3:T(2,128)(2,1)} %bitcast.20), calls=%async_computation.7 | async-start | bytes 98304 | tf_op jit(solution)/shard_map/all_to_all | solution.py:71
  109.8 6.8 %all-to-all-done.7 = bf16[1,3,2,32,128]{4,2,1,0,3:T(2,128)(2,1)S(1)} async-done(((bf16[1,3,2,32,128]{4,2,1,0,3:T(2,128)(2,1)}), bf16[1,3,2,32,128]{4,2,1,0,3:T(2,128)(2,1)S(1)}, u32[]{:S(2)}, u32[]{:S(2)}) %all-to-all-start.7) | async-done | bytes 49184 | tf_op jit(solution)/shard_map/all_to_all | solution.py:71
  116.6 33.2 %all_to_all.68 = bf16[8,16,16,128]{3,2,0,1:T(8,128)(2,1)S(1)} all-to-all(bf16[8,16,16,128]{3,2,0,1:T(8,128)(2,1)S(1)} %get-tuple-element.135), channel_id=1, replica_groups=mesh['prompt'=16,'tp'=32] {'prompt'}, dimensions={1} | all-to-all | bytes 1048576 | tf_op jit(solution)/shard_map/all_to_all | solution.py:30
  149.8 9.4 %all-to-all-start.5 = ((bf16[8,16,16,128]{3,2,0,1:T(8,128)(2,1)}), bf16[8,16,16,128]{3,2,0,1:T(8,128)(2,1)S(1)}, u32[]{:S(2)}, u32[]{:S(2)}) async-start(bf16[8,16,16,128]{3,2,0,1:T(8,128)(2,1)} %get-tuple-element.134), calls=%async_computation.5 | async-start | bytes 1048576 | tf_op jit(solution)/shard_map/all_to_all | solution.py:31
  159.3 27.7 %all-to-all-done.5 = bf16[8,16,16,128]{3,2,0,1:T(8,128)(2,1)S(1)} async-done(((bf16[8,16,16,128]{3,2,0,1:T(8,128)(2,1)}), bf16[8,16,16,128]{3,2,0,1:T(8,128)(2,1)S(1)}, u32[]{:S(2)}, u32[]{:S(2)}) %all-to-all-start.5) | async-done | bytes 524320 | tf_op jit(solution)/shard_map/all_to_all | solution.py:31
  187.0 1.9 broadcast_in_dim.73
  188.9 6.8 %all-to-all-start.2 = ((bf16[32,256,128]{2,1,0:T(8,128)(2,1)}), bf16[32,256,128]{2,1,0:T(8,128)(2,1)S(1)}, u32[]{:S(2)}, u32[]{:S(2)}) async-start(bf16[32,256,128]{2,1,0:T(8,128)(2,1)} %bitcast.4), calls=%async_computation.2 | async-start | bytes 4194304 | tf_op jit(solution)/shard_map/all_to_all | solution.py:40
  195.7 49.8 %all-to-all-done.2 = bf16[32,256,128]{2,1,0:T(8,128)(2,1)S(1)} async-done(((bf16[32,256,128]{2,1,0:T(8,128)(2,1)}), bf16[32,256,128]{2,1,0:T(8,128)(2,1)S(1)}, u32[]{:S(2)}, u32[]{:S(2)}) %all-to-all-start.2) | async-done | bytes 2097184 | tf_op jit(solution)/shard_map/all_to_all | solution.py:40
  245.6 2.0 broadcast_in_dim.79
  247.5 4.7 %all-to-all-start.6 = ((bf16[32,256,128]{2,1,0:T(8,128)(2,1)}), bf16[32,256,128]{2,1,0:T(8,128)(2,1)S(1)}, u32[]{:S(2)}, u32[]{:S(2)}) async-start(bf16[32,256,128]{2,1,0:T(8,128)(2,1)} %bitcast.17), calls=%async_computation.6 | async-start | bytes 4194304 | tf_op jit(solution)/shard_map/all_to_all | solution.py:41
  255.1 22.5 %while.24 = (s32[]{:T(128)}, f32[768]{0:T(1024)S(1)}, bf16[16,512,128]{2,1,0:T(8,128)(2,1)}, bf16[768,128]{1,0:T(8,128)(2,1)}, s32[]{:T(128)}, /*index=5*/s32[]{:T(128)}) while((s32[]{:T(128)}, f32[768]{0:T(1024)S(1)}, bf16[16,512,128]{2,1,0:T(8,128)(2,1)}, bf16[768,128]{1,0:T(8,128)(2,1)}, s32[]{:T(128)}, ...), condition=%wide.region_2.4_spmd.clone, body=%wide.region_0.3_spmd.clone.sunk | while | flops 101450496 | bytes 340559 | solution.py:64
  277.7 24.4 %all-to-all-done.6 = bf16[32,256,128]{2,1,0:T(8,128)(2,1)S(1)} async-done(((bf16[32,256,128]{2,1,0:T(8,128)(2,1)}), bf16[32,256,128]{2,1,0:T(8,128)(2,1)S(1)}, u32[]{:S(2)}, u32[]{:S(2)}) %all-to-all-start.6) | async-done | bytes 2097184 | tf_op jit(solution)/shard_map/all_to_all | solution.py:41
  302.1 31.9 %while.25 = (s32[]{:T(128)}, f32[768]{0:T(1024)S(1)}, f32[768,128]{1,0:T(8,128)S(1)}, bf16[16,512,128]{2,1,0:T(8,128)(2,1)}, bf16[768,128]{1,0:T(8,128)(2,1)}, /...) while((s32[]{:T(128)}, f32[768]{0:T(1024)S(1)}, ...), condition=%wide.region_6.8_spmd.clone, body=%wide.region_4.7_spmd.clone.sunk | while | flops 203096832 | bytes 2834028 | solution.py:98
  304.1 1.5 fusion.33
  306.1 1.5 fusion.33
  308.1 1.5 fusion.33
  310.1 1.5 fusion.33
  312.1 1.5 fusion.33
  314.1 1.5 fusion.33
  316.1 1.5 fusion.33
  318.1 1.5 fusion.33
  320.1 1.5 fusion.33
  322.1 1.5 fusion.33
  328.0 1.5 fusion.33
  332.0 1.5 fusion.33
  (132 shorter events, 45.2 us)
Async XLA Ops:
  0.0 20.4 %copy-start.2 = (bf16[1,8,256,128]{3,2,1,0:T(8,128)(2,1)S(1)}, bf16[1,8,256,128]{3,2,1,0:T(8,128)(2,1)}, u32[]{:S(2)}) copy-start(bf16[1,8,256,128]{3,2,1,0:T(8,128)(2,1)} %param.14) | copy-start | bytes 1572868
  0.0 56.7 %copy-start.7 = (bf16[1,3,2,8,128]{4,3,2,1,0:T(8,128)(2,1)S(1)}, bf16[1,3,2,8,128]{4,3,2,1,0:T(8,128)(2,1)}, u32[]{:S(2)}) copy-start(bf16[1,3,2,8,128]{4,3,2,1,0:T(8,128)(2,1)} %param.16) | copy-start | bytes 36868
  0.0 56.7 %copy-start.8 = (bf16[1,3,2,8,128]{4,3,2,1,0:T(8,128)(2,1)S(1)}, bf16[1,3,2,8,128]{4,3,2,1,0:T(8,128)(2,1)}, u32[]{:S(2)}) copy-start(bf16[1,3,2,8,128]{4,3,2,1,0:T(8,128)(2,1)} %param.17) | copy-start | bytes 36868
  0.0 56.7 %copy-start.9 = (s32[16]{0:T(128)S(1)}, s32[16]{0:T(128)}, u32[]{:S(2)}) copy-start(s32[16]{0:T(128)} %param.19) | copy-start | bytes 196
  2.0 37.9 %all-to-all-start = ((bf16[8,16,16,128]{3,2,0,1:T(8,128)(2,1)}), bf16[8,16,16,128]{3,2,0,1:T(8,128)(2,1)S(1)}, u32[]{:S(2)}, u32[]{:S(2)}) async-start(bf16[8,16,16,128]{3,2,0,1:T(8,128)(2,1)} %copy.56), calls=%async_computation | async-start | bytes 1048576 | tf_op jit(solution)/shard_map/all_to_all | solution.py:24
  39.9 34.3 %all-to-all-start.4 = ((bf16[8,16,16,128]{3,2,0,1:T(8,128)(2,1)}), bf16[8,16,16,128]{3,2,0,1:T(8,128)(2,1)S(1)}, u32[]{:S(2)}, u32[]{:S(2)}) async-start(bf16[8,16,16,128]{3,2,0,1:T(8,128)(2,1)} %copy.65), calls=%async_computation.4 | async-start | bytes 1048576 | tf_op jit(solution)/shard_map/all_to_all | solution.py:25
  74.8 29.4 %all-to-all-start.3 = ((bf16[1,3,2,32,128]{4,2,1,0,3:T(2,128)(2,1)}), bf16[1,3,2,32,128]{4,2,1,0,3:T(2,128)(2,1)S(1)}, u32[]{:S(2)}, u32[]{:S(2)}) async-start(bf16[1,3,2,32,128]{4,2,1,0,3:T(2,128)(2,1)} %bitcast.7), calls=%async_computation.3 | async-start | bytes 98304 | tf_op jit(solution)/shard_map/all_to_all | solution.py:70
  104.2 45.6 %copy-start.3 = (bf16[1,3,2,32,128]{4,2,1,0,3:T(2,128)(2,1)}, bf16[1,3,2,32,128]{4,2,1,0,3:T(2,128)(2,1)S(1)}, u32[]{:S(2)}) copy-start(bf16[1,3,2,32,128]{4,2,1,0,3:T(2,128)(2,1)S(1)} %all-to-all-done.3) | copy-start | bytes 147460
  104.8 11.8 %all-to-all-start.7 = ((bf16[1,3,2,32,128]{4,2,1,0,3:T(2,128)(2,1)}), bf16[1,3,2,32,128]{4,2,1,0,3:T(2,128)(2,1)S(1)}, u32[]{:S(2)}, u32[]{:S(2)}) async-start(bf16[1,3,2,32,128]{4,2,1,0,3:T(2,128)(2,1)} %bitcast.20), calls=%async_computation.7 | async-start | bytes 98304 | tf_op jit(solution)/shard_map/all_to_all | solution.py:71
  116.6 72.3 %copy-start.5 = (bf16[1,3,2,32,128]{4,2,1,0,3:T(2,128)(2,1)}, bf16[1,3,2,32,128]{4,2,1,0,3:T(2,128)(2,1)S(1)}, u32[]{:S(2)}) copy-start(bf16[1,3,2,32,128]{4,2,1,0,3:T(2,128)(2,1)S(1)} %all-to-all-done.7) | copy-start | bytes 147460
  149.8 37.2 %all-to-all-start.5 = ((bf16[8,16,16,128]{3,2,0,1:T(8,128)(2,1)}), bf16[8,16,16,128]{3,2,0,1:T(8,128)(2,1)S(1)}, u32[]{:S(2)}, u32[]{:S(2)}) async-start(bf16[8,16,16,128]{3,2,0,1:T(8,128)(2,1)} %get-tuple-element.134), calls=%async_computation.5 | async-start | bytes 1048576 | tf_op jit(solution)/shard_map/all_to_all | solution.py:31
  188.9 56.7 %all-to-all-start.2 = ((bf16[32,256,128]{2,1,0:T(8,128)(2,1)}), bf16[32,256,128]{2,1,0:T(8,128)(2,1)S(1)}, u32[]{:S(2)}, u32[]{:S(2)}) async-start(bf16[32,256,128]{2,1,0:T(8,128)(2,1)} %bitcast.4), calls=%async_computation.2 | async-start | bytes 4194304 | tf_op jit(solution)/shard_map/all_to_all | solution.py:40
  245.6 2.0 copy-start
  247.5 4.7 %copy-start.1 = (bf16[1,3,64,512]{3,2,1,0:T(8,128)(2,1)S(1)}, bf16[1,3,64,512]{3,2,1,0:T(8,128)(2,1)}, u32[]{:S(2)}) copy-start(bf16[1,3,64,512]{3,2,1,0:T(8,128)(2,1)} %param.15) | copy-start | bytes 589828
  247.5 5.6 %copy-start.10 = (s32[1,64]{1,0:T(1,128)S(1)}, s32[1,64]{1,0:T(1,128)}, u32[]{:S(2)}) copy-start(s32[1,64]{1,0:T(1,128)} %param.18) | copy-start | bytes 772
  247.5 5.7 %copy-start.4 = (bf16[1,3,2,32,128]{4,2,1,0,3:T(2,128)(2,1)S(1)}, bf16[1,3,2,32,128]{4,2,1,0,3:T(2,128)(2,1)}, u32[]{:S(2)}) copy-start(bf16[1,3,2,32,128]{4,2,1,0,3:T(2,128)(2,1)} %copy-done.3) | copy-start | bytes 147460
  247.5 54.6 %all-to-all-start.6 = ((bf16[32,256,128]{2,1,0:T(8,128)(2,1)}), bf16[32,256,128]{2,1,0:T(8,128)(2,1)S(1)}, u32[]{:S(2)}, u32[]{:S(2)}) async-start(bf16[32,256,128]{2,1,0:T(8,128)(2,1)} %bitcast.17), calls=%async_computation.6 | async-start | bytes 4194304 | tf_op jit(solution)/shard_map/all_to_all | solution.py:41
  252.2 2.8 copy-start.6
where the time goes:
time: 337 us; the launch traced here: 336 us
  waiting for transfers between devices  151 us (45%)
  starting transfers between devices  81.9 us (24%)
  matrix products  54.6 us (16%)
  blocking collectives  33.2 us (10%)
  local copies, waits for them, and re-layouts  11.6 us (3%)
    all_to_all x1, waiting for transfers between devices, local(): lax.all_to_all(relayed[0], 'tp', split_axis=0, concat_axis=1, tiled=True)  49.8 us
    dot_general x32, matrix products, tile_scores(): lax.dot_general(rows, keys_tile, (((1,), (1,)), ((), ())), preferred_elem...  45.3 us
    all_to_all x1, blocking collectives, local(): lax.all_to_all(chosen_keys, 'prompt', split_axis=1, concat_axis=1, tiled=...  33.2 us
    all_to_all x1, waiting for transfers between devices, local(): lax.all_to_all(chosen_values, 'prompt', split_axis=1, concat_axis=1, tile...  27.7 us
    all_to_all x1, waiting for transfers between devices, local(): lax.all_to_all(relayed[1], 'tp', split_axis=0, concat_axis=1, tiled=True)  24.4 us
    all_to_all x1, starting transfers between devices, local(): lax.all_to_all(fresh[0], 'tp', split_axis=3, concat_axis=2, tiled=True)  21.7 us
    all_to_all x1, waiting for transfers between devices, local(): lax.all_to_all(split_keys, 'prompt', split_axis=1, concat_axis=1, tiled=T...  18.6 us
    all_to_all x1, starting transfers between devices, local(): lax.all_to_all(split_keys, 'prompt', split_axis=1, concat_axis=1, tiled=T...  18.4 us
  transfers between devices with their start and end apart: 7, of which 7 were waited for; matrix products, arithmetic and copies ran while one was open for 8% of the time, Pallas kernels for 0%

commit v1 on v0

v1 whole, which is shorter than its diff:
```python
import functools
import math

import jax
import jax.numpy as jnp
from jax import lax
from jax.experimental import pallas as pl
from jax.experimental.pallas import tpu as pltpu
from jax.sharding import PartitionSpec as P

F32 = jnp.float32
BF16 = jnp.bfloat16
NEG = -1e30
VMEM = pl.BlockSpec(memory_space=pltpu.VMEM)

STEPS, SAMPLES, HD = 3, 64, 128
HEADS = 4
TOKENS = STEPS * SAMPLES
ROWS = HEADS * TOKENS
BLOCK = 256
SUF = 16
PART = 2 * BLOCK + SUF
PIECES = 16
PIECE = ROWS // PIECES
EXTRA = 16
SCALE2 = HD ** (-0.5) * math.log2(math.e)
TILE = 256


def dot_t(a, b):
    return lax.dot_general(a, b, (((1,), (1,)), ((), ())), preferred_element_type=F32)


def dot(a, b):
    return lax.dot_general(a, b, (((1,), (0,)), ((), ())), preferred_element_type=F32)


def split3(x):
    hi = x.astype(BF16)
    rest = x - hi.astype(F32)
    mid = rest.astype(BF16)
    low = (rest - mid.astype(F32)).astype(BF16)
    return hi, mid, low


def attend_tile(q, blocks, m, l, acc):
    scores = [dot_t(q, k[...]) for k, _ in blocks]
    top = functools.reduce(jnp.maximum, scores)
    m_new = jnp.maximum(m, jnp.max(top, axis=-1, keepdims=True) * SCALE2)
    fade = jnp.exp2(m - m_new)
    l = l * fade
    acc = acc * fade
    for s, (_, v) in zip(scores, blocks):
        w = jnp.exp2(s * SCALE2 - m_new)
        l = l + jnp.sum(w, axis=-1, keepdims=True)
        acc = acc + dot(w.astype(BF16), v[...])
    return m_new, l, acc


def views(ref):
    return [
        (ref.at[i, pl.ds(0, BLOCK)], ref.at[i, pl.ds(BLOCK, BLOCK)]) for i in range(ref.shape[0])
    ]


def first_kernel(q_ref, a, b, c, d, m_ref, l_ref, acc_ref):
    def body(r, carry):
        at = pl.ds(pl.multiple_of(r * TILE, TILE), TILE)
        q = q_ref[at]
        m = jnp.full((TILE, 1), NEG, F32)
        l = jnp.zeros((TILE, 1), F32)
        acc = jnp.zeros((TILE, HD), F32)
        for ref in (a, b, c, d):
            m, l, acc = attend_tile(q, views(ref), m, l, acc)
        m_ref[at] = jnp.broadcast_to(m, (TILE, HD))
        l_ref[at] = jnp.broadcast_to(l, (TILE, HD))
        acc_ref[at] = acc
        return carry

    lax.fori_loop(0, ROWS // TILE, body, 0)


def second_kernel(q_ref, a, b, c, d, m_ref, l_ref, acc_ref, out_ref, o_sc, lse_sc):
    def body(r, carry):
        at = pl.ds(pl.multiple_of(r * TILE, TILE), TILE)
        q = q_ref[at]
        m, l, acc = m_ref[at][:, :1], l_ref[at][:, :1], acc_ref[at]
        for ref in (a, b, c, d):
            m, l, acc = attend_tile(q, views(ref), m, l, acc)
        o_sc[at] = (acc / l).astype(BF16)
        hi, mid, low = split3(m + jnp.log2(l))
        lane = lax.broadcasted_iota(jnp.int32, (TILE, HD), 1)
        zero = jnp.zeros((TILE, HD), BF16)
        lse_sc[at] = jnp.where(
            lane == 0, hi, jnp.where(lane == 1, mid, jnp.where(lane == 2, low, zero))
        )
        return carry

    lax.fori_loop(0, ROWS // TILE, body, 0)
    row = lax.broadcasted_iota(jnp.int32, (PIECE, HD), 0)
    lane = lax.broadcasted_iota(jnp.int32, (PIECE, HD), 1)
    eye = (row == lane).astype(BF16)
    for p in range(PIECES):
        out_ref[p, pl.ds(0, PIECE)] = o_sc[pl.ds(p * PIECE, PIECE)]
        turned = lax.dot_general(
            lse_sc[pl.ds(p * PIECE, PIECE)],
            eye,
            (((0,), (0,)), ((), ())),
            preferred_element_type=F32,
        )
        out_ref[p, pl.ds(PIECE, EXTRA)] = turned[:EXTRA].astype(BF16)


def suffix_kernel(q_ref, k_ref, v_ref, step_ref, sample_ref, o_ref, lse_ref):
    row = lax.broadcasted_iota(jnp.int32, (TOKENS, TOKENS), 0)
    keep = (sample_ref[...] == row % SAMPLES) & (step_ref[...] <= row // SAMPLES)
    for j in range(HEADS):
        at = pl.ds(j * TOKENS, TOKENS)
        t = jnp.where(keep, dot_t(q_ref[at], k_ref[...]) * SCALE2, NEG)
        m = jnp.max(t, axis=-1, keepdims=True)
        w = jnp.where(keep, jnp.exp2(t - m), 0.0)
        l = jnp.sum(w, axis=-1, keepdims=True)
        o_ref[at] = dot(w.astype(BF16), v_ref[...]) / l
        lse_ref[at] = jnp.broadcast_to(m + jnp.log2(l), (TOKENS, HD))


def merge_kernel(r_ref, o_ref, lse_ref, live_ref, out_ref):
    row = lax.broadcasted_iota(jnp.int32, (PIECE, HD), 0)
    lane = lax.broadcasted_iota(jnp.int32, (PIECE, HD), 1)
    eye = (row == lane).astype(BF16)
    per_head = PIECES // HEADS
    for p in range(PIECES):
        parts = dot_t(eye, r_ref[p, pl.ds(PIECE, EXTRA)])
        lse_p = parts[:, 0:1] + parts[:, 1:2] + parts[:, 2:3]
        at = pl.ds(p * PIECE, PIECE)
        lse_s = lse_ref[at]
        top = jnp.maximum(lse_p, lse_s)
        w_p = jnp.exp2(lse_p - top)
        w_s = jnp.exp2(lse_s - top)
        o_p = r_ref[p, pl.ds(0, PIECE)].astype(F32)
        merged = (w_p * o_p + w_s * o_ref[at]) / (w_p + w_s)
        tok = pl.ds((p % per_head) * PIECE, PIECE)
        merged = jnp.where(live_ref[tok] > 0, merged, 0.0)
        out_ref[tok, pl.ds((p // per_head) * HD, HD)] = merged.astype(BF16)


def call(kernel, outs, args, scratch=(), flops=0, exps=0):
    moved = sum(math.prod(a.shape) * a.dtype.itemsize for a in (*args, *outs))
    many = len(outs) > 1
    return pl.pallas_call(
        kernel,
        out_shape=tuple(outs) if many else outs[0],
        in_specs=[VMEM] * len(args),
        out_specs=(VMEM,) * len(outs) if many else VMEM,
        scratch_shapes=list(scratch),
        compiler_params=pltpu.CompilerParams(vmem_limit_bytes=40 * 2**20),
        cost_estimate=pl.CostEstimate(flops=flops, bytes_accessed=moved, transcendentals=exps),
    )(*args)


def sds(*shape, dtype=F32):
    return jax.ShapeDtypeStruct(shape, dtype)


def local(
    prompt_keys, prompt_values, queries, sample_step_keys, suffix_values, suffix_lengths, assignment
):
    tp = lax.axis_index("tp")
    x, side = tp // 8, (tp // 4) % 2
    keys, values = prompt_keys[0], prompt_values[0]

    def by_head(a):
        return jnp.transpose(a[0], (2, 0, 1, 3)).reshape(8, STEPS * 2, HD)

    fresh = jnp.concatenate(
        [by_head(sample_step_keys), by_head(suffix_values), jnp.zeros((8, 4, HD), BF16)], axis=1
    )

    def payload(to):
        own, other = 2 * to + side, 2 * to + 1 - side
        parts = [
            lax.dynamic_index_in_dim(a, h, 0, keepdims=False)
            for h in (own, other)
            for a in (keys, values, fresh)
        ]
        return jnp.concatenate(parts, axis=0).reshape(2, PART, HD)

    def shift_x(k):
        return [(t, (t + 8 * k) % 32) for t in range(32)]

    def swap(bit):
        return [(t, t ^ bit) for t in range(32)]

    got = [payload(x)] + [
        lax.ppermute(payload((x + k) % 4), "tp", shift_x(k)) for k in (1, 2, 3)
    ]
    mine = jnp.stack([g[0] for g in got])
    others = jnp.stack([g[1] for g in got])

    rows = jnp.transpose(queries[0].reshape(TOKENS, HEADS, HD), (1, 0, 2))
    pieces = rows.reshape(PIECES, PIECE, HD)
    spread = lax.all_to_all(pieces, "prompt", 0, 0, tiled=True)
    index = jnp.arange(PIECES, dtype=jnp.int32)
    server = jnp.sum(jnp.where(assignment[None, :] == index[:, None], index[None, :], 0), axis=1)
    sorted_in = jnp.take(spread, server, axis=0, mode="clip")
    home = lax.all_to_all(sorted_in, "prompt", 0, 0, tiled=True).reshape(ROWS, HD)

    part_c = lax.ppermute(others, "tp", swap(4))
    part_b = lax.ppermute(mine, "tp", swap(2))
    part_d = lax.ppermute(part_c, "tp", swap(2))
    far_a = lax.ppermute(mine, "tp", swap(1))
    far_b = lax.ppermute(part_b, "tp", swap(1))
    far_c = lax.ppermute(part_c, "tp", swap(1))
    far_d = lax.ppermute(part_d, "tp", swap(1))

    half = ROWS * 4096
    m, l, acc = call(
        first_kernel,
        [sds(ROWS, HD)] * 3,
        [home, mine, far_a, part_b, far_b],
        flops=4 * half * HD,
        exps=half,
    )
    done = call(
        second_kernel,
        [sds(PIECES, PIECE + EXTRA, HD, dtype=BF16)],
        [home, part_c, far_c, part_d, far_d, m, l, acc],
        scratch=[pltpu.VMEM((ROWS, HD), BF16), pltpu.VMEM((ROWS, HD), BF16)],
        flops=4 * half * HD,
        exps=half,
    )

    every = (mine, far_a, part_b, far_b, part_c, far_c, part_d, far_d)
    offsets = (0, 1, 2, 3, 4, 5, 6, 7)
    tail = jnp.stack([e[:, 2 * BLOCK :] for e in every])
    suf_k = tail[:, :, : 2 * STEPS].reshape(TOKENS, HD)
    suf_v = tail[:, :, 2 * STEPS : 4 * STEPS].reshape(TOKENS, HD)
    source = (
        8 * ((x - jnp.arange(4, dtype=jnp.int32)) % 4)[None, :]
        + ((tp % 8) ^ jnp.array(offsets, jnp.int32))[:, None]
    )
    shape = (8, 4, STEPS, 2)
    sample = 2 * source[:, :, None, None] + lax.broadcasted_iota(jnp.int32, shape, 3)
    step = lax.broadcasted_iota(jnp.int32, shape, 2)
    wide = (TOKENS, TOKENS)
    o_s, lse_s = call(
        suffix_kernel,
        [sds(ROWS, HD)] * 2,
        [
            rows.reshape(ROWS, HD),
            suf_k,
            suf_v,
            jnp.broadcast_to(step.reshape(1, TOKENS), wide),
            jnp.broadcast_to(sample.reshape(1, TOKENS), wide),
        ],
        flops=4 * ROWS * TOKENS * HD,
        exps=ROWS * TOKENS,
    )
    live = jnp.arange(STEPS, dtype=jnp.int32)[:, None] < suffix_lengths[0][None, :]
    live = jnp.broadcast_to(live.reshape(TOKENS, 1), (TOKENS, HD)).astype(jnp.int32)

    gone = lax.all_to_all(done, "prompt", 0, 0, tiled=True)
    sorted_out = jnp.take(gone, assignment, axis=0, mode="clip")
    back = lax.all_to_all(sorted_out, "prompt", 0, 0, tiled=True)
    out = call(
        merge_kernel, [sds(TOKENS, HEADS * HD, dtype=BF16)], [back, o_s, lse_s, live]
    )
    return out.reshape(1, STEPS, SAMPLES, HEADS * HD)


def solution(mesh):
    in_specs = (
        P("prompt", None, "tp", None),
        P("prompt", None, "tp", None),
        P("prompt", None, None, "tp"),
        P("prompt", None, "tp", None, None),
        P("prompt", None, "tp", None, None),
        P("prompt", None),
        P(),
    )
    out_specs = P("prompt", None, None, "tp")
    return jax.shard_map(local, mesh=mesh, in_specs=in_specs, out_specs=out_specs, check_vma=False)
```

time: 337 us -> 179 us (0.53)
  the two profiles are of different devices: /device:TPU:1 before, /device:TPU:32 now
where the time goes in v1:
time: 179 us; the launch traced here: 178 us
  waiting for transfers between devices  81.7 us (46%)
  starting transfers between devices  64.7 us (36%)
  Pallas kernels  18.9 us (11%)
  local copies, waits for them, and re-layouts  11.2 us (6%)
    all_to_all x1, waiting for transfers between devices, local(): gone = lax.all_to_all(done, 'prompt', 0, 0, tiled=True)  19.9 us
    pallas_call x4, Pallas kernels, call(): pl.pallas_call(kernel, out_shape=tuple(outs) if many else outs[0], in_spe...  18.9 us
    all_to_all x1, waiting for transfers between devices, local(): back = lax.all_to_all(sorted_out, 'prompt', 0, 0, tiled=True)  17.6 us
    all_to_all x1, starting transfers between devices, local(): spread = lax.all_to_all(pieces, 'prompt', 0, 0, tiled=True)  15.1 us
    all_to_all x1, waiting for transfers between devices, local(): lax.all_to_all(sorted_in, 'prompt', 0, 0, tiled=True).reshape(ROWS, HD)  13.9 us
    ppermute x3, waiting for transfers between devices, local(): lax.ppermute(payload((x + k) % 4), 'tp', shift_x(k))  11.5 us
    all_to_all x1, waiting for transfers between devices, local(): spread = lax.all_to_all(pieces, 'prompt', 0, 0, tiled=True)  11.2 us
    ppermute x3, starting transfers between devices, local(): lax.ppermute(payload((x + k) % 4), 'tp', shift_x(k))  10.2 us
  transfers between devices with their start and end apart: 14, of which 8 were waited for; matrix products, arithmetic and copies ran while one was open for 3% of the time, Pallas kernels for 5%

profile of v1, /device:TPU:32, one launch (start us, length us, event | category | flops | bytes accessed | tf_op | source)
XLA Modules:
  0.0 177.6 jit_solution(18150253020924073663)
XLA Ops:
  0.0 0.8 copy.17
  1.6 0.9 bitcast_dynamic-update-slice_fusion.11
  2.5 0.9 bitcast_dynamic-update-slice_fusion.10
  3.7 4.7 %collective-permute-start.2 = (bf16[2,528,128]{2,1,0:T(8,128)(2,1)S(1)}, bf16[2,528,128]{2,1,0:T(8,128)(2,1)S(1)}, u32[]{:S(2)}, u32[]{:S(2)}) collective-permute-start(bf16[2,528,128]{2,1,0:T(8,128)(2,1)S(1)} %bitcast.121), channel_id=1, source_target_pairs={{0,24},{1,25},{2,26},{3,27},{4,28},{5,29},{6,30},{7,31},{8,0},{9,1... | collective-permute-start | bytes 811016 | tf_op jit(solution)/shard_map/ppermute | solution.py:195
  8.4 2.7 %collective-permute-start.1 = (bf16[2,528,128]{2,1,0:T(8,128)(2,1)S(1)}, bf16[2,528,128]{2,1,0:T(8,128)(2,1)S(1)}, u32[]{:S(2)}, u32[]{:S(2)}) collective-permute-start(bf16[2,528,128]{2,1,0:T(8,128)(2,1)S(1)} %bitcast.123), channel_id=1, source_target_pairs={{0,16},{1,17},{2,18},{3,19},{4,20},{5,21},{6,22},{7,23},{8,24},{9,... | collective-permute-start | bytes 811016 | tf_op jit(solution)/shard_map/ppermute | solution.py:195
  11.1 2.8 %collective-permute-start = (bf16[2,528,128]{2,1,0:T(8,128)(2,1)S(1)}, bf16[2,528,128]{2,1,0:T(8,128)(2,1)S(1)}, u32[]{:S(2)}, u32[]{:S(2)}) collective-permute-start(bf16[2,528,128]{2,1,0:T(8,128)(2,1)S(1)} %bitcast.122), channel_id=1, source_target_pairs={{0,8},{1,9},{2,10},{3,11},{4,12},{5,13},{6,14},{7,15},{8,16},{9,17... | collective-permute-start | bytes 811016 | tf_op jit(solution)/shard_map/ppermute | solution.py:195
  14.0 5.9 %collective-permute-done.2 = bf16[2,528,128]{2,1,0:T(8,128)(2,1)S(1)} collective-permute-done((bf16[2,528,128]{2,1,0:T(8,128)(2,1)S(1)}, bf16[2,528,128]{2,1,0:T(8,128)(2,1)S(1)}, u32[]{:S(2)}, u32[]{:S(2)}) %collective-permute-start.2) | collective-permute-done | bytes 270368 | tf_op jit(solution)/shard_map/ppermute | solution.py:195
  19.9 1.3 collective-permute-done.1
  21.2 4.3 %collective-permute-done = bf16[2,528,128]{2,1,0:T(8,128)(2,1)S(1)} collective-permute-done((bf16[2,528,128]{2,1,0:T(8,128)(2,1)S(1)}, bf16[2,528,128]{2,1,0:T(8,128)(2,1)S(1)}, u32[]{:S(2)}, u32[]{:S(2)}) %collective-permute-start) | collective-permute-done | bytes 270368 | tf_op jit(solution)/shard_map/ppermute | solution.py:195
  25.6 5.2 %collective-permute-start.3 = (bf16[4,528,128]{2,1,0:T(8,128)(2,1)S(1)}, bf16[4,528,128]{2,1,0:T(8,128)(2,1)S(1)}, u32[]{:S(2)}, u32[]{:S(2)}) collective-permute-start(bf16[4,528,128]{2,1,0:T(8,128)(2,1)S(1)} %pad_maximum_fusion), channel_id=1, source_target_pairs={{0,4},{1,5},{2,6},{3,7},{4,0},{5,1},{6,2},{7,3},{8,12},{9,13},{10,... | collective-permute-start | bytes 1622024 | tf_op jit(solution)/shard_map/ppermute | solution.py:208
  31.6 15.1 %all-to-all-start = ((bf16[16,48,128]{2,1,0:T(8,128)(2,1)}), bf16[16,48,128]{2,1,0:T(8,128)(2,1)S(1)}, u32[]{:S(2)}, u32[]{:S(2)}) async-start(bf16[16,48,128]{2,1,0:T(8,128)(2,1)} %bitcast.1), calls=%async_computation | async-start | bytes 393216 | tf_op jit(solution)/shard_map/all_to_all | solution.py:202
  46.8 2.9 %collective-permute-start.8 = (bf16[4,528,128]{2,1,0:T(8,128)(2,1)S(1)}, bf16[4,528,128]{2,1,0:T(8,128)(2,1)S(1)}, u32[]{:S(2)}, u32[]{:S(2)}) collective-permute-start(bf16[4,528,128]{2,1,0:T(8,128)(2,1)S(1)} %pad_maximum_fusion.1.a), channel_id=1, source_target_pairs={{0,2},{1,3},{2,0},{3,1},{4,6},{5,7},{6,4},{7,5},{8,10},{9,11},{10,... | collective-permute-start | bytes 1622024 | tf_op jit(solution)/shard_map/ppermute | solution.py:209
  50.5 7.6 %collective-permute-done.3.a = bf16[4,528,128]{2,1,0:T(8,128)(2,1)S(1)} collective-permute-done((bf16[4,528,128]{2,1,0:T(8,128)(2,1)S(1)}, bf16[4,528,128]{2,1,0:T(8,128)(2,1)S(1)}, u32[]{:S(2)}, u32[]{:S(2)}) %collective-permute-start.3) | collective-permute-done | bytes 540704 | tf_op jit(solution)/shard_map/ppermute | solution.py:208
  58.1 3.7 %collective-permute-start.5 = (bf16[4,528,128]{2,1,0:T(8,128)(2,1)S(1)}, bf16[4,528,128]{2,1,0:T(8,128)(2,1)S(1)}, u32[]{:S(2)}, u32[]{:S(2)}) collective-permute-start(bf16[4,528,128]{2,1,0:T(8,128)(2,1)S(1)} %collective-permute-done.3.a), channel_id=1, source_target_pairs={{0,2},{1,3},{2,0},{3,1},{4,6},{5,7},{6,4},{7,5},{8,10},{9,11},{10,... | collective-permute-start | bytes 1622024 | tf_op jit(solution)/shard_map/ppermute | solution.py:210
  61.9 11.2 %all-to-all-done = bf16[16,48,128]{2,1,0:T(8,128)(2,1)S(1)} async-done(((bf16[16,48,128]{2,1,0:T(8,128)(2,1)}), bf16[16,48,128]{2,1,0:T(8,128)(2,1)S(1)}, u32[]{:S(2)}, u32[]{:S(2)}) %all-to-all-start) | async-done | bytes 196640 | tf_op jit(solution)/shard_map/all_to_all | solution.py:202
  73.0 1.3 gather_fusion
  74.3 8.7 %all-to-all-start.1 = ((bf16[16,48,128]{2,1,0:T(8,128)(2,1)}), bf16[16,48,128]{2,1,0:T(8,128)(2,1)S(1)}, u32[]{:S(2)}, u32[]{:S(2)}) async-start(bf16[16,48,128]{2,1,0:T(8,128)(2,1)} %gather_fusion), calls=%async_computation.1 | async-start | bytes 393216 | tf_op jit(solution)/shard_map/all_to_all | solution.py:206
  83.0 1.9 %collective-permute-start.7 = (bf16[4,528,128]{2,1,0:T(8,128)(2,1)S(1)}, bf16[4,528,128]{2,1,0:T(8,128)(2,1)}, u32[]{:S(2)}, u32[]{:S(2)}) collective-permute-start(bf16[4,528,128]{2,1,0:T(8,128)(2,1)S(1)} %pad_maximum_fusion.1.a), channel_id=1, source_target_pairs={{0,1},{1,0},{2,3},{3,2},{4,5},{5,4},{6,7},{7,6},{8,9},{9,8},{10,11... | collective-permute-start | bytes 1622024 | tf_op jit(solution)/shard_map/ppermute | solution.py:211
  85.0 2.4 %collective-permute-start.9 = (bf16[4,528,128]{2,1,0:T(8,128)(2,1)S(1)}, bf16[4,528,128]{2,1,0:T(8,128)(2,1)}, u32[]{:S(2)}, u32[]{:S(2)}) collective-permute-start(bf16[4,528,128]{2,1,0:T(8,128)(2,1)S(1)} %collective-permute-done.8.c), channel_id=1, source_target_pairs={{0,1},{1,0},{2,3},{3,2},{4,5},{5,4},{6,7},{7,6},{8,9},{9,8},{10,11... | collective-permute-start | bytes 1622024 | tf_op jit(solution)/shard_map/ppermute | solution.py:212
  87.6 1.9 %collective-permute-start.4 = (bf16[4,528,128]{2,1,0:T(8,128)(2,1)S(1)}, bf16[4,528,128]{2,1,0:T(8,128)(2,1)S(1)}, u32[]{:S(2)}, u32[]{:S(2)}) collective-permute-start(bf16[4,528,128]{2,1,0:T(8,128)(2,1)S(1)} %collective-permute-done.3.a), channel_id=1, source_target_pairs={{0,1},{1,0},{2,3},{3,2},{4,5},{5,4},{6,7},{7,6},{8,9},{9,8},{10,11... | collective-permute-start | bytes 1622024 | tf_op jit(solution)/shard_map/ppermute | solution.py:213
  89.5 2.4 %collective-permute-start.6 = (bf16[4,528,128]{2,1,0:T(8,128)(2,1)S(1)}, bf16[4,528,128]{2,1,0:T(8,128)(2,1)S(1)}, u32[]{:S(2)}, u32[]{:S(2)}) collective-permute-start(bf16[4,528,128]{2,1,0:T(8,128)(2,1)S(1)} %collective-permute-done.5.c), channel_id=1, source_target_pairs={{0,1},{1,0},{2,3},{3,2},{4,5},{5,4},{6,7},{7,6},{8,9},{9,8},{10,11... | collective-permute-start | bytes 1622024 | tf_op jit(solution)/shard_map/ppermute | solution.py:214
  93.0 13.9 %all-to-all-done.1 = bf16[16,48,128]{2,1,0:T(8,128)(2,1)S(1)} async-done(((bf16[16,48,128]{2,1,0:T(8,128)(2,1)}), bf16[16,48,128]{2,1,0:T(8,128)(2,1)S(1)}, u32[]{:S(2)}, u32[]{:S(2)}) %all-to-all-start.1) | async-done | bytes 196640 | tf_op jit(solution)/shard_map/all_to_all | solution.py:206
  106.8 7.3 %shard_map.82 = (f32[768,128]{1,0:T(8,128)S(1)}, f32[768,128]{1,0:T(8,128)S(1)}, f32[768,128]{1,0:T(8,128)S(1)}) custom-call(bf16[768,128]{1,0:T(8,128)(2,1)S(1)} %bitcast.119, bf16[4,528,128]{2,1,0:T(8,128)(2,1)S(1)} %pad_maximum_fusion.1.a, bf16[4,528,128]{2,1,0:T(8,128)(2,1)} %collective-permute-done.7.b, ...), custom_call_target="tpu_custom_call" | custom-call | flops 1610612736 | bytes 3538944 | tf_op jit(solution)/shard_map/pallas_call | solution.py:150
  114.1 8.7 %shard_map.83 = bf16[16,64,128]{2,1,0:T(8,128)(2,1)} custom-call(bf16[768,128]{1,0:T(8,128)(2,1)S(1)} %bitcast.120, bf16[4,528,128]{2,1,0:T(8,128)(2,1)S(1)} %collective-permute-done.3.a, bf16[4,528,128]{2,1,0:T(8,128)(2,1)S(1)} %collective-permute-done.4.b, bf16[4,528,128]{2,1,0:T(8,128)(2,1)S(1)} %collective-permute-done.5.c, ...), custom_call_target="tpu_custom_call" | custom-call | flops 1610612736 | bytes 3801088 | tf_op jit(solution)/shard_map/pallas_call | solution.py:150
  122.8 6.5 %all-to-all-start.2 = ((bf16[16,64,128]{2,1,0:T(8,128)(2,1)}), bf16[16,64,128]{2,1,0:T(8,128)(2,1)}, u32[]{:S(2)}, u32[]{:S(2)}) async-start(bf16[16,64,128]{2,1,0:T(8,128)(2,1)} %shard_map.83), calls=%async_computation.2 | async-start | bytes 524288 | tf_op jit(solution)/shard_map/all_to_all | solution.py:262
  129.3 0.7 constant_dynamic-update-slice_fusion.12
  130.7 19.9 %all-to-all-done.2 = bf16[16,64,128]{2,1,0:T(8,128)(2,1)} async-done(((bf16[16,64,128]{2,1,0:T(8,128)(2,1)}), bf16[16,64,128]{2,1,0:T(8,128)(2,1)}, u32[]{:S(2)}, u32[]{:S(2)}) %all-to-all-start.2) | async-done | bytes 262176 | tf_op jit(solution)/shard_map/all_to_all | solution.py:262
  150.7 2.2 %gather_fusion.1 = bf16[16,64,128]{2,1,0:T(8,128)(2,1)} fusion(bf16[16,64,128]{2,1,0:T(8,128)(2,1)} %all-to-all-done.2, s32[1024]{0:T(1024)S(1)} %pad_clamp_fusion), kind=kCustom, calls=%fused_computation.1 | custom fusion | bytes 524352 | tf_op jit(solution)/shard_map/jit(_take)/gather | solution.py:263
  152.9 3.8 %all-to-all-start.3 = ((bf16[16,64,128]{2,1,0:T(8,128)(2,1)}), bf16[16,64,128]{2,1,0:T(8,128)(2,1)S(1)}, u32[]{:S(2)}, u32[]{:S(2)}) async-start(bf16[16,64,128]{2,1,0:T(8,128)(2,1)} %gather_fusion.1), calls=%async_computation.3 | async-start | bytes 524288 | tf_op jit(solution)/shard_map/all_to_all | solution.py:264
  156.9 1.7 shard_map.84
  158.6 17.6 %all-to-all-done.3.r_ref = bf16[16,64,128]{2,1,0:T(8,128)(2,1)S(1)} async-done(((bf16[16,64,128]{2,1,0:T(8,128)(2,1)}), bf16[16,64,128]{2,1,0:T(8,128)(2,1)S(1)}, u32[]{:S(2)}, u32[]{:S(2)}) %all-to-all-start.3) | async-done | bytes 262176 | tf_op jit(solution)/shard_map/all_to_all | solution.py:264
  176.3 1.3 shard_map.85
  (63 shorter events, 5.0 us)
Async XLA Ops:
  0.0 3.5 %copy-start = (bf16[1,8,256,128]{3,2,1,0:T(8,128)(2,1)S(1)}, bf16[1,8,256,128]{3,2,1,0:T(8,128)(2,1)}, u32[]{:S(2)}) copy-start(bf16[1,8,256,128]{3,2,1,0:T(8,128)(2,1)} %param.8) | copy-start | bytes 1572868
  1.5 2.1 %copy-start.1 = (bf16[1,8,256,128]{3,2,1,0:T(8,128)(2,1)S(1)}, bf16[1,8,256,128]{3,2,1,0:T(8,128)(2,1)}, u32[]{:S(2)}) copy-start(bf16[1,8,256,128]{3,2,1,0:T(8,128)(2,1)} %param.9) | copy-start | bytes 1572868
  3.7 16.2 %collective-permute-start.2 = (bf16[2,528,128]{2,1,0:T(8,128)(2,1)S(1)}, bf16[2,528,128]{2,1,0:T(8,128)(2,1)S(1)}, u32[]{:S(2)}, u32[]{:S(2)}) collective-permute-start(bf16[2,528,128]{2,1,0:T(8,128)(2,1)S(1)} %bitcast.121), channel_id=1, source_target_pairs={{0,24},{1,25},{2,26},{3,27},{4,28},{5,29},{6,30},{7,31},{8,0},{9,1... | collective-permute-start | bytes 811016 | tf_op jit(solution)/shard_map/ppermute | solution.py:195
  8.4 12.8 %collective-permute-start.1 = (bf16[2,528,128]{2,1,0:T(8,128)(2,1)S(1)}, bf16[2,528,128]{2,1,0:T(8,128)(2,1)S(1)}, u32[]{:S(2)}, u32[]{:S(2)}) collective-permute-start(bf16[2,528,128]{2,1,0:T(8,128)(2,1)S(1)} %bitcast.123), channel_id=1, source_target_pairs={{0,16},{1,17},{2,18},{3,19},{4,20},{5,21},{6,22},{7,23},{8,24},{9,... | collective-permute-start | bytes 811016 | tf_op jit(solution)/shard_map/ppermute | solution.py:195
  11.1 14.4 %collective-permute-start = (bf16[2,528,128]{2,1,0:T(8,128)(2,1)S(1)}, bf16[2,528,128]{2,1,0:T(8,128)(2,1)S(1)}, u32[]{:S(2)}, u32[]{:S(2)}) collective-permute-start(bf16[2,528,128]{2,1,0:T(8,128)(2,1)S(1)} %bitcast.122), channel_id=1, source_target_pairs={{0,8},{1,9},{2,10},{3,11},{4,12},{5,13},{6,14},{7,15},{8,16},{9,17... | collective-permute-start | bytes 811016 | tf_op jit(solution)/shard_map/ppermute | solution.py:195
  25.5 5.3 %copy-start.2 = (bf16[1,3,64,512]{3,2,1,0:T(8,128)(2,1)S(1)}, bf16[1,3,64,512]{3,2,1,0:T(8,128)(2,1)}, u32[]{:S(2)}) copy-start(bf16[1,3,64,512]{3,2,1,0:T(8,128)(2,1)} %param.10) | copy-start | bytes 589828
  25.6 32.5 %collective-permute-start.3 = (bf16[4,528,128]{2,1,0:T(8,128)(2,1)S(1)}, bf16[4,528,128]{2,1,0:T(8,128)(2,1)S(1)}, u32[]{:S(2)}, u32[]{:S(2)}) collective-permute-start(bf16[4,528,128]{2,1,0:T(8,128)(2,1)S(1)} %pad_maximum_fusion), channel_id=1, source_target_pairs={{0,4},{1,5},{2,6},{3,7},{4,0},{5,1},{6,2},{7,3},{8,12},{9,13},{10,... | collective-permute-start | bytes 1622024 | tf_op jit(solution)/shard_map/ppermute | solution.py:208
  31.6 41.5 %all-to-all-start = ((bf16[16,48,128]{2,1,0:T(8,128)(2,1)}), bf16[16,48,128]{2,1,0:T(8,128)(2,1)S(1)}, u32[]{:S(2)}, u32[]{:S(2)}) async-start(bf16[16,48,128]{2,1,0:T(8,128)(2,1)} %bitcast.1), calls=%async_computation | async-start | bytes 393216 | tf_op jit(solution)/shard_map/all_to_all | solution.py:202
  46.8 38.1 %collective-permute-start.8 = (bf16[4,528,128]{2,1,0:T(8,128)(2,1)S(1)}, bf16[4,528,128]{2,1,0:T(8,128)(2,1)S(1)}, u32[]{:S(2)}, u32[]{:S(2)}) collective-permute-start(bf16[4,528,128]{2,1,0:T(8,128)(2,1)S(1)} %pad_maximum_fusion.1.a), channel_id=1, source_target_pairs={{0,2},{1,3},{2,0},{3,1},{4,6},{5,7},{6,4},{7,5},{8,10},{9,11},{10,... | collective-permute-start | bytes 1622024 | tf_op jit(solution)/shard_map/ppermute | solution.py:209
  49.7 0.7 copy-start.4
  58.1 31.4 %collective-permute-start.5 = (bf16[4,528,128]{2,1,0:T(8,128)(2,1)S(1)}, bf16[4,528,128]{2,1,0:T(8,128)(2,1)S(1)}, u32[]{:S(2)}, u32[]{:S(2)}) collective-permute-start(bf16[4,528,128]{2,1,0:T(8,128)(2,1)S(1)} %collective-permute-done.3.a), channel_id=1, source_target_pairs={{0,2},{1,3},{2,0},{3,1},{4,6},{5,7},{6,4},{7,5},{8,10},{9,11},{10,... | collective-permute-start | bytes 1622024 | tf_op jit(solution)/shard_map/ppermute | solution.py:210
  74.3 32.5 %all-to-all-start.1 = ((bf16[16,48,128]{2,1,0:T(8,128)(2,1)}), bf16[16,48,128]{2,1,0:T(8,128)(2,1)S(1)}, u32[]{:S(2)}, u32[]{:S(2)}) async-start(bf16[16,48,128]{2,1,0:T(8,128)(2,1)} %gather_fusion), calls=%async_computation.1 | async-start | bytes 393216 | tf_op jit(solution)/shard_map/all_to_all | solution.py:206
  83.0 9.9 %collective-permute-start.7 = (bf16[4,528,128]{2,1,0:T(8,128)(2,1)S(1)}, bf16[4,528,128]{2,1,0:T(8,128)(2,1)}, u32[]{:S(2)}, u32[]{:S(2)}) collective-permute-start(bf16[4,528,128]{2,1,0:T(8,128)(2,1)S(1)} %pad_maximum_fusion.1.a), channel_id=1, source_target_pairs={{0,1},{1,0},{2,3},{3,2},{4,5},{5,4},{6,7},{7,6},{8,9},{9,8},{10,11... | collective-permute-start | bytes 1622024 | tf_op jit(solution)/shard_map/ppermute | solution.py:211
  85.0 8.0 %collective-permute-start.9 = (bf16[4,528,128]{2,1,0:T(8,128)(2,1)S(1)}, bf16[4,528,128]{2,1,0:T(8,128)(2,1)}, u32[]{:S(2)}, u32[]{:S(2)}) collective-permute-start(bf16[4,528,128]{2,1,0:T(8,128)(2,1)S(1)} %collective-permute-done.8.c), channel_id=1, source_target_pairs={{0,1},{1,0},{2,3},{3,2},{4,5},{5,4},{6,7},{7,6},{8,9},{9,8},{10,11... | collective-permute-start | bytes 1622024 | tf_op jit(solution)/shard_map/ppermute | solution.py:212
  87.6 26.5 %collective-permute-start.4 = (bf16[4,528,128]{2,1,0:T(8,128)(2,1)S(1)}, bf16[4,528,128]{2,1,0:T(8,128)(2,1)S(1)}, u32[]{:S(2)}, u32[]{:S(2)}) collective-permute-start(bf16[4,528,128]{2,1,0:T(8,128)(2,1)S(1)} %collective-permute-done.3.a), channel_id=1, source_target_pairs={{0,1},{1,0},{2,3},{3,2},{4,5},{5,4},{6,7},{7,6},{8,9},{9,8},{10,11... | collective-permute-start | bytes 1622024 | tf_op jit(solution)/shard_map/ppermute | solution.py:213
  89.5 24.6 %collective-permute-start.6 = (bf16[4,528,128]{2,1,0:T(8,128)(2,1)S(1)}, bf16[4,528,128]{2,1,0:T(8,128)(2,1)S(1)}, u32[]{:S(2)}, u32[]{:S(2)}) collective-permute-start(bf16[4,528,128]{2,1,0:T(8,128)(2,1)S(1)} %collective-permute-done.5.c), channel_id=1, source_target_pairs={{0,1},{1,0},{2,3},{3,2},{4,5},{5,4},{6,7},{7,6},{8,9},{9,8},{10,11... | collective-permute-start | bytes 1622024 | tf_op jit(solution)/shard_map/ppermute | solution.py:214
  92.2 0.7 copy-start.3
  122.8 27.9 %all-to-all-start.2 = ((bf16[16,64,128]{2,1,0:T(8,128)(2,1)}), bf16[16,64,128]{2,1,0:T(8,128)(2,1)}, u32[]{:S(2)}, u32[]{:S(2)}) async-start(bf16[16,64,128]{2,1,0:T(8,128)(2,1)} %shard_map.83), calls=%async_computation.2 | async-start | bytes 524288 | tf_op jit(solution)/shard_map/all_to_all | solution.py:262
  152.9 23.3 %all-to-all-start.3 = ((bf16[16,64,128]{2,1,0:T(8,128)(2,1)}), bf16[16,64,128]{2,1,0:T(8,128)(2,1)S(1)}, u32[]{:S(2)}, u32[]{:S(2)}) async-start(bf16[16,64,128]{2,1,0:T(8,128)(2,1)} %gather_fusion.1), calls=%async_computation.3 | async-start | bytes 524288 | tf_op jit(solution)/shard_map/all_to_all | solution.py:264

commit v2 on v1

v2 whole, which is shorter than its diff:
```python
import functools
import math

import jax
import jax.numpy as jnp
from jax import lax
from jax.experimental import pallas as pl
from jax.experimental.pallas import tpu as pltpu
from jax.sharding import PartitionSpec as P

F32 = jnp.float32
BF16 = jnp.bfloat16
NEG = -1e30
VMEM = pl.BlockSpec(memory_space=pltpu.VMEM)

STEPS, SAMPLES, HD = 3, 64, 128
HEADS = 4
TOKENS = STEPS * SAMPLES
ROWS = HEADS * TOKENS
BLOCK = 256
SUF = 16
PART = 2 * BLOCK + SUF
HALF = 8 * BLOCK
HELD = 8 * PART
SORT_FLOPS = 40 * 10**9
PIECES = 16
PIECE = ROWS // PIECES
EXTRA = 8
SCALE2 = HD ** (-0.5) * math.log2(math.e)
TILE = 256


def dot_t(a, b):
    return lax.dot_general(a, b, (((1,), (1,)), ((), ())), preferred_element_type=F32)


def dot(a, b):
    return lax.dot_general(a, b, (((1,), (0,)), ((), ())), preferred_element_type=F32)


def split3(x):
    hi = x.astype(BF16)
    rest = x - hi.astype(F32)
    mid = rest.astype(BF16)
    low = (rest - mid.astype(F32)).astype(BF16)
    return hi, mid, low


def attend_tile(q, blocks, m, l, acc):
    scores = [dot_t(q, k[...]) for k, _ in blocks]
    top = functools.reduce(jnp.maximum, scores)
    m_new = jnp.maximum(m, jnp.max(top, axis=-1, keepdims=True) * SCALE2)
    fade = jnp.exp2(m - m_new)
    l = l * fade
    acc = acc * fade
    for s, (_, v) in zip(scores, blocks):
        w = jnp.exp2(s * SCALE2 - m_new)
        l = l + jnp.sum(w, axis=-1, keepdims=True)
        acc = acc + dot(w.astype(BF16), v[...])
    return m_new, l, acc


def sort_kernel(*refs):
    out = refs[-1]
    for n, (got, i) in enumerate((got, i) for got in refs[:-1] for i in range(2)):
        out[pl.ds(n * BLOCK, BLOCK)] = got[i, pl.ds(0, BLOCK)]
        out[pl.ds(HALF + n * BLOCK, BLOCK)] = got[i, pl.ds(BLOCK, BLOCK)]
        out[pl.ds(2 * HALF + n * SUF, SUF)] = got[i, pl.ds(2 * BLOCK, SUF)]


def views(ref):
    return [
        (ref.at[pl.ds(i, BLOCK)], ref.at[pl.ds(HALF + i, BLOCK)]) for i in range(0, HALF, BLOCK)
    ]


def attend(q, refs, state):
    blocks = [view for ref in refs for view in views(ref)]
    for i in range(0, len(blocks), 4):
        state = attend_tile(q, blocks[i : i + 4], *state)
    return state


def fresh_state():
    return (
        jnp.full((TILE, 1), NEG, F32),
        jnp.zeros((TILE, 1), F32),
        jnp.zeros((TILE, HD), F32),
    )


def tiles(body):
    def step(r, carry):
        body(pl.ds(pl.multiple_of(r * TILE, TILE), TILE))
        return carry

    lax.fori_loop(0, ROWS // TILE, step, 0)


def spread_out(column):
    return jnp.broadcast_to(column, (TILE, HD))


def result(m, l, acc):
    return acc / l, spread_out(m + jnp.log2(l))


def on_diagonal():
    row = lax.broadcasted_iota(jnp.int32, (PIECE, HD), 0)
    lane = lax.broadcasted_iota(jnp.int32, (PIECE, HD), 1)
    return row == lane


def pack(o, lse):
    line = jnp.sum(jnp.where(on_diagonal(), lse, 0.0), axis=0, keepdims=True)
    hi, mid, low = (jnp.broadcast_to(part.astype(F32), (EXTRA, HD)) for part in split3(line))
    row = lax.broadcasted_iota(jnp.int32, (EXTRA, HD), 0)
    parts = jnp.where(row == 0, hi, jnp.where(row == 1, mid, jnp.where(row == 2, low, 0.0)))
    return jnp.concatenate([o, parts], axis=0).astype(BF16)


def unpack(piece):
    piece = piece.astype(F32)
    line = jnp.sum(piece[PIECE:], axis=0, keepdims=True)
    lse = jnp.sum(jnp.where(on_diagonal(), line, 0.0), axis=1, keepdims=True)
    return piece[:PIECE], lse


def attend_kernel(q_ref, a, b, out_ref, o_sc, lse_sc):
    def body(at):
        o_sc[at], lse_sc[at] = result(*attend(q_ref[at], (a, b), fresh_state()))

    tiles(body)
    for p in range(PIECES):
        at = pl.ds(p * PIECE, PIECE)
        out_ref[p] = pack(o_sc[at], lse_sc[at])


def join(o1, lse1, o2, lse2):
    top = jnp.maximum(lse1, lse2)
    w1, w2 = jnp.exp2(lse1 - top), jnp.exp2(lse2 - top)
    total = w1 + w2
    return (w1 * o1 + w2 * o2) / total, top + jnp.log2(total)


def join_kernel(a_ref, b_ref, out_ref):
    for p in range(PIECES):
        out_ref[p] = pack(*join(*unpack(a_ref[p]), *unpack(b_ref[p])))


def suffix_kernel(q_ref, k_ref, v_ref, step_ref, sample_ref, o_ref, lse_ref):
    row = lax.broadcasted_iota(jnp.int32, (TOKENS, TOKENS), 0)
    keep = (sample_ref[...] == row % SAMPLES) & (step_ref[...] <= row // SAMPLES)
    for j in range(HEADS):
        at = pl.ds(j * TOKENS, TOKENS)
        t = jnp.where(keep, dot_t(q_ref[at], k_ref[...]) * SCALE2, NEG)
        m = jnp.max(t, axis=-1, keepdims=True)
        w = jnp.where(keep, jnp.exp2(t - m), 0.0)
        l = jnp.sum(w, axis=-1, keepdims=True)
        o_ref[at] = dot(w.astype(BF16), v_ref[...]) / l
        lse_ref[at] = jnp.broadcast_to(m + jnp.log2(l), (TOKENS, HD))


def merge_kernel(r_ref, o_ref, lse_ref, live_ref, out_ref):
    per_head = PIECES // HEADS
    for p in range(PIECES):
        at = pl.ds(p * PIECE, PIECE)
        tok = pl.ds((p % per_head) * PIECE, PIECE)
        merged, _ = join(o_ref[at], lse_ref[at], *unpack(r_ref[p]))
        merged = jnp.where(live_ref[tok] > 0, merged, 0.0)
        out_ref[tok, pl.ds((p // per_head) * HD, HD)] = merged.astype(BF16)


def call(kernel, outs, args, scratch=(), flops=0, exps=0):
    moved = sum(math.prod(a.shape) * a.dtype.itemsize for a in (*args, *outs))
    many = len(outs) > 1
    return pl.pallas_call(
        kernel,
        out_shape=tuple(outs) if many else outs[0],
        in_specs=[VMEM] * len(args),
        out_specs=(VMEM,) * len(outs) if many else VMEM,
        scratch_shapes=list(scratch),
        compiler_params=pltpu.CompilerParams(vmem_limit_bytes=40 * 2**20),
        cost_estimate=pl.CostEstimate(flops=flops, bytes_accessed=moved, transcendentals=exps),
    )(*args)


def sds(*shape, dtype=F32):
    return jax.ShapeDtypeStruct(shape, dtype)


def local(
    prompt_keys, prompt_values, queries, sample_step_keys, suffix_values, suffix_lengths, assignment
):
    tp = lax.axis_index("tp")
    x, z, core = tp // 8, (tp // 2) % 4, tp % 2
    keys, values = prompt_keys[0], prompt_values[0]

    def turn(zz):
        return (zz % 2) * 2 + zz // 2

    def permute(a, target):
        pairs = []
        for t in range(32):
            to_x, to_z, to_core = target(t // 8, (t // 2) % 4, t % 2)
            pairs.append((t, 8 * to_x + 2 * to_z + to_core))
        return lax.ppermute(a, "tp", pairs)

    def there_0(xx, zz, cc):
        return xx, turn(zz), cc

    def there_1(xx, zz, cc):
        return xx, turn(zz) ^ 2, cc

    def back_1(xx, zz, cc):
        return xx, turn(zz ^ 2), cc

    fresh = jnp.stack([sample_step_keys[0], suffix_values[0]])
    fresh = jnp.transpose(fresh, (3, 0, 1, 2, 4)).reshape(8, 4 * STEPS, HD)
    fresh = jnp.pad(fresh, ((0, 0), (0, SUF - 4 * STEPS), (0, 0)))

    def of_parity(which):
        parts = [
            lax.dynamic_index_in_dim(a.reshape(4, 2, -1, HD), which, 1, keepdims=False)
            for a in (keys, values, fresh)
        ]
        return jnp.concatenate(parts, axis=1)

    rows = jnp.transpose(queries[0].reshape(TOKENS, HEADS, HD), (1, 0, 2))
    pieces = rows.reshape(PIECES, PIECE, HD)
    spread = lax.all_to_all(pieces, "prompt", 0, 0, tiled=True)
    index = jnp.arange(PIECES, dtype=jnp.int32)
    server = jnp.sum(jnp.where(assignment[None, :] == index[:, None], index[None, :], 0), axis=1)
    sorted_in = jnp.take(spread, server, axis=0, mode="clip")
    kept = of_parity(z % 2)
    came = permute(of_parity(1 - z % 2), lambda xx, zz, cc: (xx, zz ^ 1, cc))

    def payload(to):
        return jnp.stack(
            [lax.dynamic_index_in_dim(a, to, 0, keepdims=False) for a in (kept, came)]
        )

    got = [payload(x)]
    for k in (1, 2, 3):
        shift = lambda xx, zz, cc, k=k: ((xx + k) % 4, zz, cc)
        got.append(permute(payload((x + k) % 4), shift))
    mine = call(sort_kernel, [sds(HELD, HD, dtype=BF16)], got, flops=SORT_FLOPS)
    home = lax.all_to_all(sorted_in, "prompt", 0, 0, tiled=True).reshape(ROWS, HD)
    mine, home = lax.optimization_barrier((mine, home))
    far = permute(mine, lambda xx, zz, cc: (xx, zz, cc ^ 1))

    def cost(positions):
        return dict(flops=4 * ROWS * positions * HD, exps=ROWS * positions)

    held = [mine, far]
    packed = sds(PIECES, PIECE + EXTRA, HD, dtype=BF16)
    wide = pltpu.VMEM((ROWS, HD), F32)
    partial = []
    for there, back in ((there_0, there_0), (there_1, back_1)):
        part = call(
            attend_kernel,
            [packed],
            [permute(home, there), *held],
            scratch=[wide, wide],
            **cost(4096),
        )
        partial.append(permute(part, back))
    done = call(join_kernel, [packed], partial)

    done, held = lax.optimization_barrier((done, held))
    tail = jnp.stack([e[2 * HALF :].reshape(8, SUF, HD) for e in held])
    tail = jnp.stack([permute(tail, there_0), permute(tail, back_1)])
    live = jnp.arange(STEPS, dtype=jnp.int32)[:, None] < suffix_lengths[0][None, :]
    live = jnp.broadcast_to(live.reshape(TOKENS, 1), (TOKENS, HD)).astype(jnp.int32)

    gone = lax.all_to_all(done, "prompt", 0, 0, tiled=True)
    gone, tail = lax.optimization_barrier((gone, tail))
    sorted_out = jnp.take(gone, assignment, axis=0, mode="clip")
    sorted_out, tail = lax.optimization_barrier((sorted_out, tail))
    suf_k = tail[:, :, :, : 2 * STEPS].reshape(TOKENS, HD)
    suf_v = tail[:, :, :, 2 * STEPS : 4 * STEPS].reshape(TOKENS, HD)
    shape = (2, 2, 4, 2, STEPS, 2)
    at = [lax.broadcasted_iota(jnp.int32, shape, d) for d in range(6)]
    origin = turn(z) ^ (2 * at[0])
    source = 8 * ((x - at[2]) % 4) + 2 * (origin ^ at[3]) + (core ^ at[1])
    sample, step = 2 * source + at[5], at[4]
    wide = (TOKENS, TOKENS)
    o_s, lse_s = call(
        suffix_kernel,
        [sds(ROWS, HD)] * 2,
        [
            rows.reshape(ROWS, HD),
            suf_k,
            suf_v,
            jnp.broadcast_to(step.reshape(1, TOKENS), wide),
            jnp.broadcast_to(sample.reshape(1, TOKENS), wide),
        ],
        flops=4 * ROWS * TOKENS * HD,
        exps=ROWS * TOKENS,
    )
    back = lax.all_to_all(sorted_out, "prompt", 0, 0, tiled=True)
    out = call(
        merge_kernel, [sds(TOKENS, HEADS * HD, dtype=BF16)], [back, o_s, lse_s, live]
    )
    return out.reshape(1, STEPS, SAMPLES, HEADS * HD)


def solution(mesh):
    in_specs = (
        P("prompt", None, "tp", None),
        P("prompt", None, "tp", None),
        P("prompt", None, None, "tp"),
        P("prompt", None, "tp", None, None),
        P("prompt", None, "tp", None, None),
        P("prompt", None),
        P(),
    )
    out_specs = P("prompt", None, None, "tp")
    return jax.shard_map(local, mesh=mesh, in_specs=in_specs, out_specs=out_specs, check_vma=False)
```

time: 179 us -> 156 us (0.87)
  the two profiles are of different devices: /device:TPU:32 before, /device:TPU:2 now
where the time goes in v2:
time: 156 us; the launch traced here: 155 us
  starting transfers between devices  83.7 us (54%)
  waiting for transfers between devices  47 us (30%)
  Pallas kernels  16.2 us (10%)
  local copies, waits for them, and re-layouts  5.89 us (4%)
    ppermute x11, starting transfers between devices, permute(): return lax.ppermute(a, 'tp', pairs)  42.7 us
    all_to_all x1, waiting for transfers between devices, local(): lax.all_to_all(sorted_in, 'prompt', 0, 0, tiled=True).reshape(ROWS, HD)  17.3 us
    all_to_all x1, starting transfers between devices, local(): spread = lax.all_to_all(pieces, 'prompt', 0, 0, tiled=True)  16.9 us
    pallas_call x6, Pallas kernels, call(): pl.pallas_call(kernel, out_shape=tuple(outs) if many else outs[0], in_spe...  16.2 us
    all_to_all x1, waiting for transfers between devices, local(): back = lax.all_to_all(sorted_out, 'prompt', 0, 0, tiled=True)  14.8 us
    all_to_all x1, starting transfers between devices, local(): back = lax.all_to_all(sorted_out, 'prompt', 0, 0, tiled=True)  13.5 us
    all_to_all x1, waiting for transfers between devices, local(): spread = lax.all_to_all(pieces, 'prompt', 0, 0, tiled=True)  7.53 us
    ppermute x11, waiting for transfers between devices, permute(): return lax.ppermute(a, 'tp', pairs)  7.41 us
  transfers between devices with their start and end apart: 15, of which 5 were waited for; matrix products, arithmetic and copies ran while one was open for 2% of the time, Pallas kernels for 9%

profile of v2, /device:TPU:2, one launch (start us, length us, event | category | flops | bytes accessed | tf_op | source)
XLA Modules:
  0.0 154.6 jit_solution(168872708683329497)
XLA Ops:
  0.0 0.7 pad_maximum_fusion.8
  0.8 1.3 dynamic-slice_bitcast_fusion.2
  2.2 3.8 %collective-permute-start = (bf16[4,528,128]{2,1,0:T(8,128)(2,1)S(1)}, bf16[4,528,128]{2,1,0:T(8,128)(2,1)S(1)}, u32[]{:S(2)}, u32[]{:S(2)}) collective-permute-start(bf16[4,528,128]{2,1,0:T(8,128)(2,1)S(1)} %pad_maximum_fusion.1), channel_id=1, source_target_pairs={{0,2},{1,3},{2,0},{3,1},{4,6},{5,7},{6,4},{7,5},{8,10},{9,11},{10,... | collective-permute-start | bytes 1622024 | tf_op jit(solution)/shard_map/ppermute | solution.py:207
  6.1 0.7 copy.30
  6.8 16.9 %all-to-all-start = ((bf16[16,48,128]{2,1,0:T(8,128)(2,1)}), bf16[16,48,128]{2,1,0:T(8,128)(2,1)S(1)}, u32[]{:S(2)}, u32[]{:S(2)}) async-start(bf16[16,48,128]{2,1,0:T(8,128)(2,1)} %bitcast.12), calls=%async_computation | async-start | bytes 393216 | tf_op jit(solution)/shard_map/all_to_all | solution.py:231
  24.0 2.4 %collective-permute-start.3 = (bf16[2,528,128]{2,1,0:T(8,128)(2,1)S(1)}, bf16[2,528,128]{2,1,0:T(8,128)(2,1)S(1)}, u32[]{:S(2)}, u32[]{:S(2)}) collective-permute-start(bf16[2,528,128]{2,1,0:T(8,128)(2,1)S(1)} %pad_maximum_fusion.5), channel_id=1, source_target_pairs={{0,24},{1,25},{2,26},{3,27},{4,28},{5,29},{6,30},{7,31},{8,0},{9,1... | collective-permute-start | bytes 811016 | tf_op jit(solution)/shard_map/ppermute | solution.py:207
  26.5 4.3 %collective-permute-start.2 = (bf16[2,528,128]{2,1,0:T(8,128)(2,1)S(1)}, bf16[2,528,128]{2,1,0:T(8,128)(2,1)S(1)}, u32[]{:S(2)}, u32[]{:S(2)}) collective-permute-start(bf16[2,528,128]{2,1,0:T(8,128)(2,1)S(1)} %pad_maximum_fusion.4), channel_id=1, source_target_pairs={{0,16},{1,17},{2,18},{3,19},{4,20},{5,21},{6,22},{7,23},{8,24},{9,... | collective-permute-start | bytes 811016 | tf_op jit(solution)/shard_map/ppermute | solution.py:207
  30.9 3.7 %collective-permute-start.1 = (bf16[2,528,128]{2,1,0:T(8,128)(2,1)S(1)}, bf16[2,528,128]{2,1,0:T(8,128)(2,1)S(1)}, u32[]{:S(2)}, u32[]{:S(2)}) collective-permute-start(bf16[2,528,128]{2,1,0:T(8,128)(2,1)S(1)} %pad_maximum_fusion.3), channel_id=1, source_target_pairs={{0,8},{1,9},{2,10},{3,11},{4,12},{5,13},{6,14},{7,15},{8,16},{9,17... | collective-permute-start | bytes 811016 | tf_op jit(solution)/shard_map/ppermute | solution.py:207
  34.7 7.5 %all-to-all-done = bf16[16,48,128]{2,1,0:T(8,128)(2,1)S(1)} async-done(((bf16[16,48,128]{2,1,0:T(8,128)(2,1)}), bf16[16,48,128]{2,1,0:T(8,128)(2,1)S(1)}, u32[]{:S(2)}, u32[]{:S(2)}) %all-to-all-start) | async-done | bytes 196640 | tf_op jit(solution)/shard_map/all_to_all | solution.py:231
  42.3 1.2 gather_fusion
  43.5 6.8 %all-to-all-start.1 = ((bf16[16,48,128]{2,1,0:T(8,128)(2,1)}), bf16[16,48,128]{2,1,0:T(8,128)(2,1)S(1)}, u32[]{:S(2)}, u32[]{:S(2)}) async-start(bf16[16,48,128]{2,1,0:T(8,128)(2,1)} %gather_fusion), calls=%async_computation.1 | async-start | bytes 393216 | tf_op jit(solution)/shard_map/all_to_all | solution.py:248
  50.5 17.3 %all-to-all-done.1 = bf16[16,48,128]{2,1,0:T(8,128)(2,1)S(1)} async-done(((bf16[16,48,128]{2,1,0:T(8,128)(2,1)}), bf16[16,48,128]{2,1,0:T(8,128)(2,1)S(1)}, u32[]{:S(2)}, u32[]{:S(2)}) %all-to-all-start.1) | async-done | bytes 196640 | tf_op jit(solution)/shard_map/all_to_all | solution.py:248
  67.8 1.9 %collective-permute-start.5 = (bf16[4224,128]{1,0:T(8,128)(2,1)S(1)}, bf16[4224,128]{1,0:T(8,128)(2,1)S(1)}, u32[]{:S(2)}, u32[]{:S(2)}) collective-permute-start(bf16[4224,128]{1,0:T(8,128)(2,1)S(1)} %shard_map.73.a), channel_id=1, source_target_pairs={{0,1},{1,0},{2,3},{3,2},{4,5},{5,4},{6,7},{7,6},{8,9},{9,8},{10,11... | collective-permute-start | bytes 3244040 | tf_op jit(solution)/shard_map/ppermute | solution.py:207
  69.7 4.7 %collective-permute-start.7 = (bf16[768,128]{1,0:T(8,128)(2,1)S(1)}, bf16[768,128]{1,0:T(8,128)(2,1)S(1)}, u32[]{:S(2)}, u32[]{:S(2)}) collective-permute-start(bf16[768,128]{1,0:T(8,128)(2,1)S(1)} %bitcast.42), channel_id=1, source_target_pairs={{0,4},{1,5},{2,0},{3,1},{4,6},{5,7},{6,2},{7,3},{8,12},{9,13},{10,... | collective-permute-start | bytes 589832 | tf_op jit(solution)/shard_map/ppermute | solution.py:207
  74.4 0.7 collective-permute-start.4
  75.1 4.2 %collective-permute-done.7.q_ref = bf16[768,128]{1,0:T(8,128)(2,1)S(1)} collective-permute-done((bf16[768,128]{1,0:T(8,128)(2,1)S(1)}, bf16[768,128]{1,0:T(8,128)(2,1)S(1)}, u32[]{:S(2)}, u32[]{:S(2)}) %collective-permute-start.7) | collective-permute-done | bytes 196640 | tf_op jit(solution)/shard_map/ppermute | solution.py:207
  79.3 6.2 %shard_map.75 = bf16[16,56,128]{2,1,0:T(8,128)(2,1)S(1)} custom-call(bf16[768,128]{1,0:T(8,128)(2,1)S(1)} %collective-permute-done.7.q_ref, bf16[4224,128]{1,0:T(8,128)(2,1)S(1)} %shard_map.73.a, bf16[4224,128]{1,0:T(8,128)(2,1)S(1)} %collective-permute-done.5.b), custom_call_target="tpu_custom_call" | custom-call | flops 1610612736 | bytes 2588672 | tf_op jit(solution)/shard_map/pallas_call | solution.py:177
  85.5 4.7 %collective-permute-start.8 = (bf16[16,56,128]{2,1,0:T(8,128)(2,1)S(1)}, bf16[16,56,128]{2,1,0:T(8,128)(2,1)S(1)}, u32[]{:S(2)}, u32[]{:S(2)}) collective-permute-start(bf16[16,56,128]{2,1,0:T(8,128)(2,1)S(1)} %shard_map.75), channel_id=1, source_target_pairs={{0,2},{1,3},{2,6},{3,7},{4,0},{5,1},{6,4},{7,5},{8,10},{9,11},{10,... | collective-permute-start | bytes 688136 | tf_op jit(solution)/shard_map/ppermute | solution.py:207
  90.1 6.2 %shard_map.74 = bf16[16,56,128]{2,1,0:T(8,128)(2,1)S(1)} custom-call(bf16[768,128]{1,0:T(8,128)(2,1)S(1)} %collective-permute-done.4.q_ref, bf16[4224,128]{1,0:T(8,128)(2,1)S(1)} %shard_map.73.a, bf16[4224,128]{1,0:T(8,128)(2,1)S(1)} %collective-permute-done.5.b), custom_call_target="tpu_custom_call" | custom-call | flops 1610612736 | bytes 2588672 | tf_op jit(solution)/shard_map/pallas_call | solution.py:177
  96.3 0.7 collective-permute-start.6
  97.0 1.1 shard_map.76
  98.1 3.7 %all-to-all-start.2 = ((bf16[16,56,128]{2,1,0:T(8,128)(2,1)}), bf16[16,56,128]{2,1,0:T(8,128)(2,1)S(1)}, u32[]{:S(2)}, u32[]{:S(2)}) async-start(bf16[16,56,128]{2,1,0:T(8,128)(2,1)} %shard_map.76), calls=%async_computation.2 | async-start | bytes 458752 | tf_op jit(solution)/shard_map/all_to_all | solution.py:276
  101.9 0.1 mul.39
  102.1 0.7 collective-permute-start.9
  102.8 15.1 %collective-permute-start.10 = (bf16[2,8,16,128]{3,2,1,0:T(8,128)(2,1)S(1)}, bf16[2,8,16,128]{3,2,1,0:T(8,128)(2,1)S(1)}, u32[]{:S(2)}, u32[]{:S(2)}) collective-permute-start(bf16[2,8,16,128]{3,2,1,0:T(8,128)(2,1)S(1)} %pad_maximum_fusion.7), channel_id=1, source_target_pairs={{0,2},{1,3},{2,6},{3,7},{4,0},{5,1},{6,4},{7,5},{8,10},{9,11},{10,... | collective-permute-start | bytes 196616 | tf_op jit(solution)/shard_map/ppermute | solution.py:207
  117.9 3.2 %collective-permute-done.10 = bf16[2,8,16,128]{3,2,1,0:T(8,128)(2,1)S(1)} collective-permute-done((bf16[2,8,16,128]{3,2,1,0:T(8,128)(2,1)S(1)}, bf16[2,8,16,128]{3,2,1,0:T(8,128)(2,1)S(1)}, u32[]{:S(2)}, u32[]{:S(2)}) %collective-permute-start.10) | collective-permute-done | bytes 65568 | tf_op jit(solution)/shard_map/ppermute | solution.py:207
  121.2 1.3 gather_fusion.1
  122.4 13.5 %all-to-all-start.3 = ((bf16[16,56,128]{2,1,0:T(8,128)(2,1)}), bf16[16,56,128]{2,1,0:T(8,128)(2,1)S(1)}, u32[]{:S(2)}, u32[]{:S(2)}) async-start(bf16[16,56,128]{2,1,0:T(8,128)(2,1)} %gather_fusion.1), calls=%async_computation.3 | async-start | bytes 458752 | tf_op jit(solution)/shard_map/all_to_all | solution.py:301
  136.3 0.1 iota.57
  137.0 1.7 %shard_map.77 = (f32[768,128]{1,0:T(8,128)S(1)}, f32[768,128]{1,0:T(8,128)S(1)}) custom-call(bf16[768,128]{1,0:T(8,128)(2,1)} %bitcast.18.q_ref, bf16[192,128]{1,0:T(8,128)(2,1)S(1)} %reshape.111.k_ref, bf16[192,128]{1,0:T(8,128)(2,1)S(1)} %reshape.112.v_ref, s32[192,192]{1,0:T(8,128)S(1)} %broadcast_in_dim.46.step_ref, ...), custom_call_target="tpu_custom_call" | custom-call | flops 75497472 | bytes 1376256 | tf_op jit(solution)/shard_map/pallas_call | solution.py:177
  138.8 14.8 %all-to-all-done.3.r_ref = bf16[16,56,128]{2,1,0:T(8,128)(2,1)S(1)} async-done(((bf16[16,56,128]{2,1,0:T(8,128)(2,1)}), bf16[16,56,128]{2,1,0:T(8,128)(2,1)S(1)}, u32[]{:S(2)}, u32[]{:S(2)}) %all-to-all-start.3) | async-done | bytes 229408 | tf_op jit(solution)/shard_map/all_to_all | solution.py:301
  153.6 1.0 shard_map.78
  (56 shorter events, 1.6 us)
Async XLA Ops:
  0.8 5.2 %copy-start = (bf16[1,3,64,512]{3,2,1,0:T(8,128)(2,1)S(1)}, bf16[1,3,64,512]{3,2,1,0:T(8,128)(2,1)}, u32[]{:S(2)}) copy-start(bf16[1,3,64,512]{3,2,1,0:T(8,128)(2,1)} %param.9) | copy-start | bytes 589828
  2.2 21.7 %collective-permute-start = (bf16[4,528,128]{2,1,0:T(8,128)(2,1)S(1)}, bf16[4,528,128]{2,1,0:T(8,128)(2,1)S(1)}, u32[]{:S(2)}, u32[]{:S(2)}) collective-permute-start(bf16[4,528,128]{2,1,0:T(8,128)(2,1)S(1)} %pad_maximum_fusion.1), channel_id=1, source_target_pairs={{0,2},{1,3},{2,0},{3,1},{4,6},{5,7},{6,4},{7,5},{8,10},{9,11},{10,... | collective-permute-start | bytes 1622024 | tf_op jit(solution)/shard_map/ppermute | solution.py:207
  6.8 35.5 %all-to-all-start = ((bf16[16,48,128]{2,1,0:T(8,128)(2,1)}), bf16[16,48,128]{2,1,0:T(8,128)(2,1)S(1)}, u32[]{:S(2)}, u32[]{:S(2)}) async-start(bf16[16,48,128]{2,1,0:T(8,128)(2,1)} %bitcast.12), calls=%async_computation | async-start | bytes 393216 | tf_op jit(solution)/shard_map/all_to_all | solution.py:231
  23.9 10.6 %copy-start.1 = (s32[16]{0:T(128)S(1)}, s32[16]{0:T(128)}, u32[]{:S(2)}) copy-start(s32[16]{0:T(128)} %param.13) | copy-start | bytes 196
  24.0 26.4 %collective-permute-start.3 = (bf16[2,528,128]{2,1,0:T(8,128)(2,1)S(1)}, bf16[2,528,128]{2,1,0:T(8,128)(2,1)S(1)}, u32[]{:S(2)}, u32[]{:S(2)}) collective-permute-start(bf16[2,528,128]{2,1,0:T(8,128)(2,1)S(1)} %pad_maximum_fusion.5), channel_id=1, source_target_pairs={{0,24},{1,25},{2,26},{3,27},{4,28},{5,29},{6,30},{7,31},{8,0},{9,1... | collective-permute-start | bytes 811016 | tf_op jit(solution)/shard_map/ppermute | solution.py:207
  26.5 23.9 %collective-permute-start.2 = (bf16[2,528,128]{2,1,0:T(8,128)(2,1)S(1)}, bf16[2,528,128]{2,1,0:T(8,128)(2,1)S(1)}, u32[]{:S(2)}, u32[]{:S(2)}) collective-permute-start(bf16[2,528,128]{2,1,0:T(8,128)(2,1)S(1)} %pad_maximum_fusion.4), channel_id=1, source_target_pairs={{0,16},{1,17},{2,18},{3,19},{4,20},{5,21},{6,22},{7,23},{8,24},{9,... | collective-permute-start | bytes 811016 | tf_op jit(solution)/shard_map/ppermute | solution.py:207
  30.9 19.5 %collective-permute-start.1 = (bf16[2,528,128]{2,1,0:T(8,128)(2,1)S(1)}, bf16[2,528,128]{2,1,0:T(8,128)(2,1)S(1)}, u32[]{:S(2)}, u32[]{:S(2)}) collective-permute-start(bf16[2,528,128]{2,1,0:T(8,128)(2,1)S(1)} %pad_maximum_fusion.3), channel_id=1, source_target_pairs={{0,8},{1,9},{2,10},{3,11},{4,12},{5,13},{6,14},{7,15},{8,16},{9,17... | collective-permute-start | bytes 811016 | tf_op jit(solution)/shard_map/ppermute | solution.py:207
  43.5 24.3 %all-to-all-start.1 = ((bf16[16,48,128]{2,1,0:T(8,128)(2,1)}), bf16[16,48,128]{2,1,0:T(8,128)(2,1)S(1)}, u32[]{:S(2)}, u32[]{:S(2)}) async-start(bf16[16,48,128]{2,1,0:T(8,128)(2,1)} %gather_fusion), calls=%async_computation.1 | async-start | bytes 393216 | tf_op jit(solution)/shard_map/all_to_all | solution.py:248
  67.8 11.5 %collective-permute-start.5 = (bf16[4224,128]{1,0:T(8,128)(2,1)S(1)}, bf16[4224,128]{1,0:T(8,128)(2,1)S(1)}, u32[]{:S(2)}, u32[]{:S(2)}) collective-permute-start(bf16[4224,128]{1,0:T(8,128)(2,1)S(1)} %shard_map.73.a), channel_id=1, source_target_pairs={{0,1},{1,0},{2,3},{3,2},{4,5},{5,4},{6,7},{7,6},{8,9},{9,8},{10,11... | collective-permute-start | bytes 3244040 | tf_op jit(solution)/shard_map/ppermute | solution.py:207
  69.7 9.6 %collective-permute-start.7 = (bf16[768,128]{1,0:T(8,128)(2,1)S(1)}, bf16[768,128]{1,0:T(8,128)(2,1)S(1)}, u32[]{:S(2)}, u32[]{:S(2)}) collective-permute-start(bf16[768,128]{1,0:T(8,128)(2,1)S(1)} %bitcast.42), channel_id=1, source_target_pairs={{0,4},{1,5},{2,0},{3,1},{4,6},{5,7},{6,2},{7,3},{8,12},{9,13},{10,... | collective-permute-start | bytes 589832 | tf_op jit(solution)/shard_map/ppermute | solution.py:207
  74.4 15.7 %collective-permute-start.4 = (bf16[768,128]{1,0:T(8,128)(2,1)S(1)}, bf16[768,128]{1,0:T(8,128)(2,1)S(1)}, u32[]{:S(2)}, u32[]{:S(2)}) collective-permute-start(bf16[768,128]{1,0:T(8,128)(2,1)S(1)} %bitcast.43), channel_id=1, source_target_pairs={{0,0},{1,1},{2,4},{3,5},{4,2},{5,3},{6,6},{7,7},{8,8},{9,9},{10,12... | collective-permute-start | bytes 589832 | tf_op jit(solution)/shard_map/ppermute | solution.py:207
  85.5 11.6 %collective-permute-start.8 = (bf16[16,56,128]{2,1,0:T(8,128)(2,1)S(1)}, bf16[16,56,128]{2,1,0:T(8,128)(2,1)S(1)}, u32[]{:S(2)}, u32[]{:S(2)}) collective-permute-start(bf16[16,56,128]{2,1,0:T(8,128)(2,1)S(1)} %shard_map.75), channel_id=1, source_target_pairs={{0,2},{1,3},{2,6},{3,7},{4,0},{5,1},{6,4},{7,5},{8,10},{9,11},{10,... | collective-permute-start | bytes 688136 | tf_op jit(solution)/shard_map/ppermute | solution.py:207
  96.3 0.7 collective-permute-start.6
  98.1 23.0 %all-to-all-start.2 = ((bf16[16,56,128]{2,1,0:T(8,128)(2,1)}), bf16[16,56,128]{2,1,0:T(8,128)(2,1)S(1)}, u32[]{:S(2)}, u32[]{:S(2)}) async-start(bf16[16,56,128]{2,1,0:T(8,128)(2,1)} %shard_map.76), calls=%async_computation.2 | async-start | bytes 458752 | tf_op jit(solution)/shard_map/all_to_all | solution.py:276
  101.8 35.0 %copy-start.2 = (s32[1,64]{1,0:T(1,128)S(1)}, s32[1,64]{1,0:T(1,128)}, u32[]{:S(2)}) copy-start(s32[1,64]{1,0:T(1,128)} %param.12) | copy-start | bytes 772
  102.1 15.8 %collective-permute-start.9 = (bf16[2,8,16,128]{3,2,1,0:T(8,128)(2,1)S(1)}, bf16[2,8,16,128]{3,2,1,0:T(8,128)(2,1)S(1)}, u32[]{:S(2)}, u32[]{:S(2)}) collective-permute-start(bf16[2,8,16,128]{3,2,1,0:T(8,128)(2,1)S(1)} %pad_maximum_fusion.7), channel_id=1, source_target_pairs={{0,0},{1,1},{2,4},{3,5},{4,2},{5,3},{6,6},{7,7},{8,8},{9,9},{10,12... | collective-permute-start | bytes 196616 | tf_op jit(solution)/shard_map/ppermute | solution.py:207
  102.8 18.3 %collective-permute-start.10 = (bf16[2,8,16,128]{3,2,1,0:T(8,128)(2,1)S(1)}, bf16[2,8,16,128]{3,2,1,0:T(8,128)(2,1)S(1)}, u32[]{:S(2)}, u32[]{:S(2)}) collective-permute-start(bf16[2,8,16,128]{3,2,1,0:T(8,128)(2,1)S(1)} %pad_maximum_fusion.7), channel_id=1, source_target_pairs={{0,2},{1,3},{2,6},{3,7},{4,0},{5,1},{6,4},{7,5},{8,10},{9,11},{10,... | collective-permute-start | bytes 196616 | tf_op jit(solution)/shard_map/ppermute | solution.py:207
  122.4 31.1 %all-to-all-start.3 = ((bf16[16,56,128]{2,1,0:T(8,128)(2,1)}), bf16[16,56,128]{2,1,0:T(8,128)(2,1)S(1)}, u32[]{:S(2)}, u32[]{:S(2)}) async-start(bf16[16,56,128]{2,1,0:T(8,128)(2,1)} %gather_fusion.1), calls=%async_computation.3 | async-start | bytes 458752 | tf_op jit(solution)/shard_map/all_to_all | solution.py:301

commit v3 on v2

--- a/solution.py
+++ b/solution.py
@@ -21,13 +21,12 @@
 SUF = 16
 PART = 2 * BLOCK + SUF
 HALF = 8 * BLOCK
-HELD = 8 * PART
 SORT_FLOPS = 40 * 10**9
 PIECES = 16
 PIECE = ROWS // PIECES
 EXTRA = 8
 SCALE2 = HD ** (-0.5) * math.log2(math.e)
-TILE = 256
+CHUNK = 1024
 
 
 def dot_t(a, b):
@@ -46,63 +45,29 @@
     return hi, mid, low
 
 
-def attend_tile(q, blocks, m, l, acc):
-    scores = [dot_t(q, k[...]) for k, _ in blocks]
-    top = functools.reduce(jnp.maximum, scores)
-    m_new = jnp.maximum(m, jnp.max(top, axis=-1, keepdims=True) * SCALE2)
-    fade = jnp.exp2(m - m_new)
-    l = l * fade
-    acc = acc * fade
-    for s, (_, v) in zip(scores, blocks):
-        w = jnp.exp2(s * SCALE2 - m_new)
-        l = l + jnp.sum(w, axis=-1, keepdims=True)
-        acc = acc + dot(w.astype(BF16), v[...])
-    return m_new, l, acc
+def attend(q, held):
+    m = jnp.full((ROWS, 1), NEG, F32)
+    l = jnp.zeros((ROWS, 1), F32)
+    acc = jnp.zeros((ROWS, HD), F32)
+    for keys, values in held:
+        for i in range(0, HALF, CHUNK):
+            at = pl.ds(i, CHUNK)
+            s = dot_t(q, keys[at])
+            m_new = jnp.maximum(m, jnp.max(s, axis=-1, keepdims=True) * SCALE2)
+            fade = jnp.exp2(m - m_new)
+            w = jnp.exp2(s * SCALE2 - m_new)
+            l = l * fade + jnp.sum(w, axis=-1, keepdims=True)
+            acc = acc * fade + dot(w.astype(BF16), values[at])
+            m = m_new
+    return acc / l, m + jnp.log2(l)
 
 
 def sort_kernel(*refs):
-    out = refs[-1]
-    for n, (got, i) in enumerate((got, i) for got in refs[:-1] for i in range(2)):
-        out[pl.ds(n * BLOCK, BLOCK)] = got[i, pl.ds(0, BLOCK)]
-        out[pl.ds(HALF + n * BLOCK, BLOCK)] = got[i, pl.ds(BLOCK, BLOCK)]
-        out[pl.ds(2 * HALF + n * SUF, SUF)] = got[i, pl.ds(2 * BLOCK, SUF)]
-
-
-def views(ref):
-    return [
-        (ref.at[pl.ds(i, BLOCK)], ref.at[pl.ds(HALF + i, BLOCK)]) for i in range(0, HALF, BLOCK)
-    ]
-
-
-def attend(q, refs, state):
-    blocks = [view for ref in refs for view in views(ref)]
-    for i in range(0, len(blocks), 4):
-        state = attend_tile(q, blocks[i : i + 4], *state)
-    return state
-
-
-def fresh_state():
-    return (
-        jnp.full((TILE, 1), NEG, F32),
-        jnp.zeros((TILE, 1), F32),
-        jnp.zeros((TILE, HD), F32),
-    )
-
-
-def tiles(body):
-    def step(r, carry):
-        body(pl.ds(pl.multiple_of(r * TILE, TILE), TILE))
-        return carry
-
-    lax.fori_loop(0, ROWS // TILE, step, 0)
-
-
-def spread_out(column):
-    return jnp.broadcast_to(column, (TILE, HD))
-
-
-def result(m, l, acc):
-    return acc / l, spread_out(m + jnp.log2(l))
+    *blocks, keys, rest = refs
+    for n, (got, i) in enumerate((got, i) for got in blocks for i in range(2)):
+        keys[pl.ds(n * BLOCK, BLOCK)] = got[i, pl.ds(0, BLOCK)]
+        rest[pl.ds(n * BLOCK, BLOCK)] = got[i, pl.ds(BLOCK, BLOCK)]
+        rest[pl.ds(HALF + n * SUF, SUF)] = got[i, pl.ds(2 * BLOCK, SUF)]
 
 
 def on_diagonal():
@@ -119,6 +84,12 @@
     return jnp.concatenate([o, parts], axis=0).astype(BF16)
 
 
+def pack_wide(o, lse):
+    line = jnp.sum(jnp.where(on_diagonal(), lse, 0.0), axis=0, keepdims=True)
+    row = lax.broadcasted_iota(jnp.int32, (EXTRA, HD), 0)
+    return jnp.concatenate([o, jnp.where(row == 0, line, 0.0)], axis=0)
+
+
 def unpack(piece):
     piece = piece.astype(F32)
     line = jnp.sum(piece[PIECE:], axis=0, keepdims=True)
@@ -126,14 +97,13 @@
     return piece[:PIECE], lse
 
 
-def attend_kernel(q_ref, a, b, out_ref, o_sc, lse_sc):
-    def body(at):
-        o_sc[at], lse_sc[at] = result(*attend(q_ref[at], (a, b), fresh_state()))
-
-    tiles(body)
+def attend_kernel(q_ref, k_a, v_a, k_b, v_b, out_ref, o_sc, lse_sc):
+    o_sc[...], lse = attend(q_ref[...], ((k_a, v_a), (k_b, v_b)))
+    lse_sc[...] = jnp.broadcast_to(lse, (ROWS, HD))
+    code = pack if out_ref.dtype == BF16 else pack_wide
     for p in range(PIECES):
         at = pl.ds(p * PIECE, PIECE)
-        out_ref[p] = pack(o_sc[at], lse_sc[at])
+        out_ref[p] = code(o_sc[at], lse_sc[at])
 
 
 def join(o1, lse1, o2, lse2):
@@ -244,31 +214,34 @@
     for k in (1, 2, 3):
         shift = lambda xx, zz, cc, k=k: ((xx + k) % 4, zz, cc)
         got.append(permute(payload((x + k) % 4), shift))
-    mine = call(sort_kernel, [sds(HELD, HD, dtype=BF16)], got, flops=SORT_FLOPS)
+    mine = call(
+        sort_kernel,
+        [sds(HALF, HD, dtype=BF16), sds(HALF + 8 * SUF, HD, dtype=BF16)],
+        got,
+        flops=SORT_FLOPS,
+    )
     home = lax.all_to_all(sorted_in, "prompt", 0, 0, tiled=True).reshape(ROWS, HD)
-    mine, home = lax.optimization_barrier((mine, home))
-    far = permute(mine, lambda xx, zz, cc: (xx, zz, cc ^ 1))
+    far = [permute(a, lambda xx, zz, cc: (xx, zz, cc ^ 1)) for a in mine]
 
     def cost(positions):
         return dict(flops=4 * ROWS * positions * HD, exps=ROWS * positions)
 
-    held = [mine, far]
-    packed = sds(PIECES, PIECE + EXTRA, HD, dtype=BF16)
+    held = [*mine, *far]
     wide = pltpu.VMEM((ROWS, HD), F32)
     partial = []
-    for there, back in ((there_0, there_0), (there_1, back_1)):
+    for there, back, kind in ((there_0, there_0, BF16), (there_1, back_1, F32)):
         part = call(
             attend_kernel,
-            [packed],
+            [sds(PIECES, PIECE + EXTRA, HD, dtype=kind)],
             [permute(home, there), *held],
             scratch=[wide, wide],
             **cost(4096),
         )
         partial.append(permute(part, back))
-    done = call(join_kernel, [packed], partial)
-
-    done, held = lax.optimization_barrier((done, held))
-    tail = jnp.stack([e[2 * HALF :].reshape(8, SUF, HD) for e in held])
+    done = call(join_kernel, [sds(PIECES, PIECE + EXTRA, HD, dtype=BF16)], partial)
+
+    tail = jnp.stack([e[1][HALF:].reshape(8, SUF, HD) for e in (mine, far)])
+    done, tail = lax.optimization_barrier((done, tail))
     tail = jnp.stack([permute(tail, there_0), permute(tail, back_1)])
     live = jnp.arange(STEPS, dtype=jnp.int32)[:, None] < suffix_lengths[0][None, :]
     live = jnp.broadcast_to(live.reshape(TOKENS, 1), (TOKENS, HD)).astype(jnp.int32)

time: 156 us -> 150 us (0.962)
  the two profiles are of different devices: /device:TPU:2 before, /device:TPU:32 now
where the time goes in v3:
time: 150 us; the launch traced here: 149 us
  starting transfers between devices  68.9 us (46%)
  waiting for transfers between devices  59.5 us (40%)
  Pallas kernels  12.9 us (9%)
  local copies, waits for them, and re-layouts  5.86 us (4%)
    ppermute x12, starting transfers between devices, permute(): return lax.ppermute(a, 'tp', pairs)  38.7 us
    all_to_all x1, waiting for transfers between devices, local(): back = lax.all_to_all(sorted_out, 'prompt', 0, 0, tiled=True)  17.2 us
    all_to_all x1, waiting for transfers between devices, local(): lax.all_to_all(sorted_in, 'prompt', 0, 0, tiled=True).reshape(ROWS, HD)  14.1 us
    pallas_call x6, Pallas kernels, call(): pl.pallas_call(kernel, out_shape=tuple(outs) if many else outs[0], in_spe...  12.9 us
    all_to_all x1, starting transfers between devices, local(): spread = lax.all_to_all(pieces, 'prompt', 0, 0, tiled=True)  12.5 us
    ppermute x12, waiting for transfers between devices, permute(): return lax.ppermute(a, 'tp', pairs)  11.4 us
    all_to_all x1, waiting for transfers between devices, local(): gone = lax.all_to_all(done, 'prompt', 0, 0, tiled=True)  8.67 us
    all_to_all x1, waiting for transfers between devices, local(): spread = lax.all_to_all(pieces, 'prompt', 0, 0, tiled=True)  8.13 us
  transfers between devices with their start and end apart: 16, of which 8 were waited for; matrix products, arithmetic and copies ran while one was open for 2% of the time, Pallas kernels for 7%

profile of v3, /device:TPU:32, one launch (start us, length us, event | category | flops | bytes accessed | tf_op | source)
XLA Modules:
  0.0 148.9 jit_solution(3928863911480439494)
XLA Ops:
  0.8 1.3 dynamic-slice_bitcast_fusion.2
  2.1 7.5 %collective-permute-start.1 = (bf16[4,528,128]{2,1,0:T(8,128)(2,1)S(1)}, bf16[4,528,128]{2,1,0:T(8,128)(2,1)S(1)}, u32[]{:S(2)}, u32[]{:S(2)}) collective-permute-start(bf16[4,528,128]{2,1,0:T(8,128)(2,1)S(1)} %pad_maximum_fusion.1), channel_id=1, source_target_pairs={{0,2},{1,3},{2,0},{3,1},{4,6},{5,7},{6,4},{7,5},{8,10},{9,11},{10,... | collective-permute-start | bytes 1622024 | tf_op jit(solution)/shard_map/ppermute | solution.py:177
  10.4 12.5 %all-to-all-start = ((bf16[16,48,128]{2,1,0:T(8,128)(2,1)}), bf16[16,48,128]{2,1,0:T(8,128)(2,1)S(1)}, u32[]{:S(2)}, u32[]{:S(2)}) async-start(bf16[16,48,128]{2,1,0:T(8,128)(2,1)} %bitcast.1), calls=%async_computation | async-start | bytes 393216 | tf_op jit(solution)/shard_map/all_to_all | solution.py:201
  23.2 3.4 %collective-permute-start.2 = (bf16[2,528,128]{2,1,0:T(8,128)(2,1)S(1)}, bf16[2,528,128]{2,1,0:T(8,128)(2,1)S(1)}, u32[]{:S(2)}, u32[]{:S(2)}) collective-permute-start(bf16[2,528,128]{2,1,0:T(8,128)(2,1)S(1)} %pad_maximum_fusion.3), channel_id=1, source_target_pairs={{0,8},{1,9},{2,10},{3,11},{4,12},{5,13},{6,14},{7,15},{8,16},{9,17... | collective-permute-start | bytes 811016 | tf_op jit(solution)/shard_map/ppermute | solution.py:177
  26.6 4.6 %collective-permute-start.3 = (bf16[2,528,128]{2,1,0:T(8,128)(2,1)S(1)}, bf16[2,528,128]{2,1,0:T(8,128)(2,1)S(1)}, u32[]{:S(2)}, u32[]{:S(2)}) collective-permute-start(bf16[2,528,128]{2,1,0:T(8,128)(2,1)S(1)} %pad_maximum_fusion.4), channel_id=1, source_target_pairs={{0,16},{1,17},{2,18},{3,19},{4,20},{5,21},{6,22},{7,23},{8,24},{9,... | collective-permute-start | bytes 811016 | tf_op jit(solution)/shard_map/ppermute | solution.py:177
  31.3 3.3 %collective-permute-start.4 = (bf16[2,528,128]{2,1,0:T(8,128)(2,1)S(1)}, bf16[2,528,128]{2,1,0:T(8,128)(2,1)S(1)}, u32[]{:S(2)}, u32[]{:S(2)}) collective-permute-start(bf16[2,528,128]{2,1,0:T(8,128)(2,1)S(1)} %pad_maximum_fusion.5), channel_id=1, source_target_pairs={{0,24},{1,25},{2,26},{3,27},{4,28},{5,29},{6,30},{7,31},{8,0},{9,1... | collective-permute-start | bytes 811016 | tf_op jit(solution)/shard_map/ppermute | solution.py:177
  34.8 8.1 %all-to-all-done = bf16[16,48,128]{2,1,0:T(8,128)(2,1)S(1)} async-done(((bf16[16,48,128]{2,1,0:T(8,128)(2,1)}), bf16[16,48,128]{2,1,0:T(8,128)(2,1)S(1)}, u32[]{:S(2)}, u32[]{:S(2)}) %all-to-all-start) | async-done | bytes 196640 | tf_op jit(solution)/shard_map/all_to_all | solution.py:201
  43.0 1.2 gather_fusion
  44.2 6.2 %all-to-all-start.1 = ((bf16[16,48,128]{2,1,0:T(8,128)(2,1)}), bf16[16,48,128]{2,1,0:T(8,128)(2,1)S(1)}, u32[]{:S(2)}, u32[]{:S(2)}) async-start(bf16[16,48,128]{2,1,0:T(8,128)(2,1)} %gather_fusion), calls=%async_computation.1 | async-start | bytes 393216 | tf_op jit(solution)/shard_map/all_to_all | solution.py:223
  50.6 1.9 %collective-permute-start.6 = (bf16[2176,128]{1,0:T(8,128)(2,1)S(1)}, bf16[2176,128]{1,0:T(8,128)(2,1)S(1)}, u32[]{:S(2)}, u32[]{:S(2)}) collective-permute-start(bf16[2176,128]{1,0:T(8,128)(2,1)S(1)} %get-tuple-element.16.v_a), channel_id=1, source_target_pairs={{0,1},{1,0},{2,3},{3,2},{4,5},{5,4},{6,7},{7,6},{8,9},{9,8},{10,11... | collective-permute-start | bytes 1671176 | tf_op jit(solution)/shard_map/ppermute | solution.py:177
  52.5 2.4 %collective-permute-start.5 = (bf16[2048,128]{1,0:T(8,128)(2,1)S(1)}, bf16[2048,128]{1,0:T(8,128)(2,1)S(1)}, u32[]{:S(2)}, u32[]{:S(2)}) collective-permute-start(bf16[2048,128]{1,0:T(8,128)(2,1)S(1)} %get-tuple-element.15.k_a), channel_id=1, source_target_pairs={{0,1},{1,0},{2,3},{3,2},{4,5},{5,4},{6,7},{7,6},{8,9},{9,8},{10,11... | collective-permute-start | bytes 1572872 | tf_op jit(solution)/shard_map/ppermute | solution.py:177
  54.9 14.1 %all-to-all-done.1 = bf16[16,48,128]{2,1,0:T(8,128)(2,1)S(1)} async-done(((bf16[16,48,128]{2,1,0:T(8,128)(2,1)}), bf16[16,48,128]{2,1,0:T(8,128)(2,1)S(1)}, u32[]{:S(2)}, u32[]{:S(2)}) %all-to-all-start.1) | async-done | bytes 196640 | tf_op jit(solution)/shard_map/all_to_all | solution.py:223
  69.0 1.9 %collective-permute-start.8 = (bf16[768,128]{1,0:T(8,128)(2,1)S(1)}, bf16[768,128]{1,0:T(8,128)(2,1)S(1)}, u32[]{:S(2)}, u32[]{:S(2)}) collective-permute-start(bf16[768,128]{1,0:T(8,128)(2,1)S(1)} %bitcast.42), channel_id=1, source_target_pairs={{0,4},{1,5},{2,0},{3,1},{4,6},{5,7},{6,2},{7,3},{8,12},{9,13},{10,... | collective-permute-start | bytes 589832 | tf_op jit(solution)/shard_map/ppermute | solution.py:177
  70.9 3.2 %collective-permute-start = (bf16[768,128]{1,0:T(8,128)(2,1)S(1)}, bf16[768,128]{1,0:T(8,128)(2,1)S(1)}, u32[]{:S(2)}, u32[]{:S(2)}) collective-permute-start(bf16[768,128]{1,0:T(8,128)(2,1)S(1)} %bitcast.43), channel_id=1, source_target_pairs={{0,0},{1,1},{2,4},{3,5},{4,2},{5,3},{6,6},{7,7},{8,8},{9,9},{10,12... | collective-permute-start | bytes 589832 | tf_op jit(solution)/shard_map/ppermute | solution.py:177
  74.1 3.4 %collective-permute-done.8.q_ref = bf16[768,128]{1,0:T(8,128)(2,1)S(1)} collective-permute-done((bf16[768,128]{1,0:T(8,128)(2,1)S(1)}, bf16[768,128]{1,0:T(8,128)(2,1)S(1)}, u32[]{:S(2)}, u32[]{:S(2)}) %collective-permute-start.8) | collective-permute-done | bytes 196640 | tf_op jit(solution)/shard_map/ppermute | solution.py:177
  77.5 4.5 %shard_map.75 = f32[16,56,128]{2,1,0:T(8,128)S(1)} custom-call(bf16[768,128]{1,0:T(8,128)(2,1)S(1)} %collective-permute-done.8.q_ref, bf16[2048,128]{1,0:T(8,128)(2,1)S(1)} %get-tuple-element.15.k_a, bf16[2176,128]{1,0:T(8,128)(2,1)S(1)} %get-tuple-element.16.v_a, bf16[2048,128]{1,0:T(8,128)(2,1)S(1)} %collective-permute-done.5.k_b, ...), custom_call_target="tpu_custom_call" | custom-call | flops 1610612736 | bytes 2818048 | tf_op jit(solution)/shard_map/pallas_call | solution.py:147
  82.1 1.9 %collective-permute-start.9 = (f32[16,56,128]{2,1,0:T(8,128)S(1)}, f32[16,56,128]{2,1,0:T(8,128)S(1)}, u32[]{:S(2)}, u32[]{:S(2)}) collective-permute-start(f32[16,56,128]{2,1,0:T(8,128)S(1)} %shard_map.75), channel_id=1, source_target_pairs={{0,2},{1,3},{2,6},{3,7},{4,0},{5,1},{6,4},{7,5},{8,10},{9,11},{10,... | collective-permute-start | bytes 1376264 | tf_op jit(solution)/shard_map/ppermute | solution.py:177
  84.0 4.6 %shard_map.74 = bf16[16,56,128]{2,1,0:T(8,128)(2,1)S(1)} custom-call(bf16[768,128]{1,0:T(8,128)(2,1)S(1)} %collective-permute-done.q_ref, bf16[2048,128]{1,0:T(8,128)(2,1)S(1)} %get-tuple-element.15.k_a, bf16[2176,128]{1,0:T(8,128)(2,1)S(1)} %get-tuple-element.16.v_a, bf16[2048,128]{1,0:T(8,128)(2,1)S(1)} %collective-permute-done.5.k_b, ...), custom_call_target="tpu_custom_call" | custom-call | flops 1610612736 | bytes 2588672 | tf_op jit(solution)/shard_map/pallas_call | solution.py:147
  88.6 3.4 %collective-permute-start.7 = (bf16[16,56,128]{2,1,0:T(8,128)(2,1)S(1)}, bf16[16,56,128]{2,1,0:T(8,128)(2,1)S(1)}, u32[]{:S(2)}, u32[]{:S(2)}) collective-permute-start(bf16[16,56,128]{2,1,0:T(8,128)(2,1)S(1)} %shard_map.74), channel_id=1, source_target_pairs={{0,0},{1,1},{2,4},{3,5},{4,2},{5,3},{6,6},{7,7},{8,8},{9,9},{10,12... | collective-permute-start | bytes 688136 | tf_op jit(solution)/shard_map/ppermute | solution.py:177
  92.0 4.6 %collective-permute-done.7.a_ref = bf16[16,56,128]{2,1,0:T(8,128)(2,1)S(1)} collective-permute-done((bf16[16,56,128]{2,1,0:T(8,128)(2,1)S(1)}, bf16[16,56,128]{2,1,0:T(8,128)(2,1)S(1)}, u32[]{:S(2)}, u32[]{:S(2)}) %collective-permute-start.7) | collective-permute-done | bytes 229408 | tf_op jit(solution)/shard_map/ppermute | solution.py:177
  96.6 1.1 shard_map.76
  97.7 5.6 %all-to-all-start.2 = ((bf16[16,56,128]{2,1,0:T(8,128)(2,1)}), bf16[16,56,128]{2,1,0:T(8,128)(2,1)S(1)}, u32[]{:S(2)}, u32[]{:S(2)}) async-start(bf16[16,56,128]{2,1,0:T(8,128)(2,1)} %shard_map.76), calls=%async_computation.2 | async-start | bytes 458752 | tf_op jit(solution)/shard_map/all_to_all | solution.py:249
  103.7 1.9 %collective-permute-start.11 = (bf16[2,8,16,128]{3,2,1,0:T(8,128)(2,1)S(1)}, bf16[2,8,16,128]{3,2,1,0:T(8,128)(2,1)S(1)}, u32[]{:S(2)}, u32[]{:S(2)}) collective-permute-start(bf16[2,8,16,128]{3,2,1,0:T(8,128)(2,1)S(1)} %pad_maximum_fusion.7), channel_id=1, source_target_pairs={{0,2},{1,3},{2,6},{3,7},{4,0},{5,1},{6,4},{7,5},{8,10},{9,11},{10,... | collective-permute-start | bytes 196616 | tf_op jit(solution)/shard_map/ppermute | solution.py:177
  105.6 3.2 %collective-permute-start.10 = (bf16[2,8,16,128]{3,2,1,0:T(8,128)(2,1)S(1)}, bf16[2,8,16,128]{3,2,1,0:T(8,128)(2,1)S(1)}, u32[]{:S(2)}, u32[]{:S(2)}) collective-permute-start(bf16[2,8,16,128]{3,2,1,0:T(8,128)(2,1)S(1)} %pad_maximum_fusion.7), channel_id=1, source_target_pairs={{0,0},{1,1},{2,4},{3,5},{4,2},{5,3},{6,6},{7,7},{8,8},{9,9},{10,12... | collective-permute-start | bytes 196616 | tf_op jit(solution)/shard_map/ppermute | solution.py:177
  108.9 1.2 collective-permute-done.11
  110.1 2.1 %collective-permute-done.10 = bf16[2,8,16,128]{3,2,1,0:T(8,128)(2,1)S(1)} collective-permute-done((bf16[2,8,16,128]{3,2,1,0:T(8,128)(2,1)S(1)}, bf16[2,8,16,128]{3,2,1,0:T(8,128)(2,1)S(1)}, u32[]{:S(2)}, u32[]{:S(2)}) %collective-permute-start.10) | collective-permute-done | bytes 65568 | tf_op jit(solution)/shard_map/ppermute | solution.py:177
  112.2 8.7 %all-to-all-done.2 = bf16[16,56,128]{2,1,0:T(8,128)(2,1)S(1)} async-done(((bf16[16,56,128]{2,1,0:T(8,128)(2,1)}), bf16[16,56,128]{2,1,0:T(8,128)(2,1)S(1)}, u32[]{:S(2)}, u32[]{:S(2)}) %all-to-all-start.2) | async-done | bytes 229408 | tf_op jit(solution)/shard_map/all_to_all | solution.py:249
  120.9 1.3 gather_fusion.1
  122.1 5.9 %all-to-all-start.3 = ((bf16[16,56,128]{2,1,0:T(8,128)(2,1)}), bf16[16,56,128]{2,1,0:T(8,128)(2,1)S(1)}, u32[]{:S(2)}, u32[]{:S(2)}) async-start(bf16[16,56,128]{2,1,0:T(8,128)(2,1)} %gather_fusion.1), calls=%async_computation.3 | async-start | bytes 458752 | tf_op jit(solution)/shard_map/all_to_all | solution.py:274
  129.0 1.7 %shard_map.77 = (f32[768,128]{1,0:T(8,128)S(1)}, f32[768,128]{1,0:T(8,128)S(1)}) custom-call(bf16[768,128]{1,0:T(8,128)(2,1)} %bitcast.18.q_ref, bf16[192,128]{1,0:T(8,128)(2,1)S(1)} %reshape.111.k_ref, bf16[192,128]{1,0:T(8,128)(2,1)S(1)} %reshape.112.v_ref, s32[192,192]{1,0:T(8,128)S(1)} %broadcast_in_dim.46.step_ref, ...), custom_call_target="tpu_custom_call" | custom-call | flops 75497472 | bytes 1376256 | tf_op jit(solution)/shard_map/pallas_call | solution.py:147
  130.7 17.2 %all-to-all-done.3.r_ref = bf16[16,56,128]{2,1,0:T(8,128)(2,1)S(1)} async-done(((bf16[16,56,128]{2,1,0:T(8,128)(2,1)}), bf16[16,56,128]{2,1,0:T(8,128)(2,1)S(1)}, u32[]{:S(2)}, u32[]{:S(2)}) %all-to-all-start.3) | async-done | bytes 229408 | tf_op jit(solution)/shard_map/all_to_all | solution.py:274
  147.9 1.0 shard_map.78
  (58 shorter events, 3.3 us)
Async XLA Ops:
  2.1 7.6 %copy-start = (bf16[1,3,64,512]{3,2,1,0:T(8,128)(2,1)S(1)}, bf16[1,3,64,512]{3,2,1,0:T(8,128)(2,1)}, u32[]{:S(2)}) copy-start(bf16[1,3,64,512]{3,2,1,0:T(8,128)(2,1)} %param.9) | copy-start | bytes 589828
  2.1 20.9 %collective-permute-start.1 = (bf16[4,528,128]{2,1,0:T(8,128)(2,1)S(1)}, bf16[4,528,128]{2,1,0:T(8,128)(2,1)S(1)}, u32[]{:S(2)}, u32[]{:S(2)}) collective-permute-start(bf16[4,528,128]{2,1,0:T(8,128)(2,1)S(1)} %pad_maximum_fusion.1), channel_id=1, source_target_pairs={{0,2},{1,3},{2,0},{3,1},{4,6},{5,7},{6,4},{7,5},{8,10},{9,11},{10,... | collective-permute-start | bytes 1622024 | tf_op jit(solution)/shard_map/ppermute | solution.py:177
  10.4 32.5 %all-to-all-start = ((bf16[16,48,128]{2,1,0:T(8,128)(2,1)}), bf16[16,48,128]{2,1,0:T(8,128)(2,1)S(1)}, u32[]{:S(2)}, u32[]{:S(2)}) async-start(bf16[16,48,128]{2,1,0:T(8,128)(2,1)} %bitcast.1), calls=%async_computation | async-start | bytes 393216 | tf_op jit(solution)/shard_map/all_to_all | solution.py:201
  23.2 11.5 %copy-start.1 = (s32[16]{0:T(128)S(1)}, s32[16]{0:T(128)}, u32[]{:S(2)}) copy-start(s32[16]{0:T(128)} %param.13) | copy-start | bytes 196
  23.2 27.3 %collective-permute-start.2 = (bf16[2,528,128]{2,1,0:T(8,128)(2,1)S(1)}, bf16[2,528,128]{2,1,0:T(8,128)(2,1)S(1)}, u32[]{:S(2)}, u32[]{:S(2)}) collective-permute-start(bf16[2,528,128]{2,1,0:T(8,128)(2,1)S(1)} %pad_maximum_fusion.3), channel_id=1, source_target_pairs={{0,8},{1,9},{2,10},{3,11},{4,12},{5,13},{6,14},{7,15},{8,16},{9,17... | collective-permute-start | bytes 811016 | tf_op jit(solution)/shard_map/ppermute | solution.py:177
  26.6 23.8 %collective-permute-start.3 = (bf16[2,528,128]{2,1,0:T(8,128)(2,1)S(1)}, bf16[2,528,128]{2,1,0:T(8,128)(2,1)S(1)}, u32[]{:S(2)}, u32[]{:S(2)}) collective-permute-start(bf16[2,528,128]{2,1,0:T(8,128)(2,1)S(1)} %pad_maximum_fusion.4), channel_id=1, source_target_pairs={{0,16},{1,17},{2,18},{3,19},{4,20},{5,21},{6,22},{7,23},{8,24},{9,... | collective-permute-start | bytes 811016 | tf_op jit(solution)/shard_map/ppermute | solution.py:177
  31.3 19.2 %collective-permute-start.4 = (bf16[2,528,128]{2,1,0:T(8,128)(2,1)S(1)}, bf16[2,528,128]{2,1,0:T(8,128)(2,1)S(1)}, u32[]{:S(2)}, u32[]{:S(2)}) collective-permute-start(bf16[2,528,128]{2,1,0:T(8,128)(2,1)S(1)} %pad_maximum_fusion.5), channel_id=1, source_target_pairs={{0,24},{1,25},{2,26},{3,27},{4,28},{5,29},{6,30},{7,31},{8,0},{9,1... | collective-permute-start | bytes 811016 | tf_op jit(solution)/shard_map/ppermute | solution.py:177
  44.2 24.8 %all-to-all-start.1 = ((bf16[16,48,128]{2,1,0:T(8,128)(2,1)}), bf16[16,48,128]{2,1,0:T(8,128)(2,1)S(1)}, u32[]{:S(2)}, u32[]{:S(2)}) async-start(bf16[16,48,128]{2,1,0:T(8,128)(2,1)} %gather_fusion), calls=%async_computation.1 | async-start | bytes 393216 | tf_op jit(solution)/shard_map/all_to_all | solution.py:223
  50.6 23.5 %collective-permute-start.6 = (bf16[2176,128]{1,0:T(8,128)(2,1)S(1)}, bf16[2176,128]{1,0:T(8,128)(2,1)S(1)}, u32[]{:S(2)}, u32[]{:S(2)}) collective-permute-start(bf16[2176,128]{1,0:T(8,128)(2,1)S(1)} %get-tuple-element.16.v_a), channel_id=1, source_target_pairs={{0,1},{1,0},{2,3},{3,2},{4,5},{5,4},{6,7},{7,6},{8,9},{9,8},{10,11... | collective-permute-start | bytes 1671176 | tf_op jit(solution)/shard_map/ppermute | solution.py:177
  52.5 21.6 %collective-permute-start.5 = (bf16[2048,128]{1,0:T(8,128)(2,1)S(1)}, bf16[2048,128]{1,0:T(8,128)(2,1)S(1)}, u32[]{:S(2)}, u32[]{:S(2)}) collective-permute-start(bf16[2048,128]{1,0:T(8,128)(2,1)S(1)} %get-tuple-element.15.k_a), channel_id=1, source_target_pairs={{0,1},{1,0},{2,3},{3,2},{4,5},{5,4},{6,7},{7,6},{8,9},{9,8},{10,11... | collective-permute-start | bytes 1572872 | tf_op jit(solution)/shard_map/ppermute | solution.py:177
  69.0 8.6 %collective-permute-start.8 = (bf16[768,128]{1,0:T(8,128)(2,1)S(1)}, bf16[768,128]{1,0:T(8,128)(2,1)S(1)}, u32[]{:S(2)}, u32[]{:S(2)}) collective-permute-start(bf16[768,128]{1,0:T(8,128)(2,1)S(1)} %bitcast.42), channel_id=1, source_target_pairs={{0,4},{1,5},{2,0},{3,1},{4,6},{5,7},{6,2},{7,3},{8,12},{9,13},{10,... | collective-permute-start | bytes 589832 | tf_op jit(solution)/shard_map/ppermute | solution.py:177
  70.9 13.1 %collective-permute-start = (bf16[768,128]{1,0:T(8,128)(2,1)S(1)}, bf16[768,128]{1,0:T(8,128)(2,1)S(1)}, u32[]{:S(2)}, u32[]{:S(2)}) collective-permute-start(bf16[768,128]{1,0:T(8,128)(2,1)S(1)} %bitcast.43), channel_id=1, source_target_pairs={{0,0},{1,1},{2,4},{3,5},{4,2},{5,3},{6,6},{7,7},{8,8},{9,9},{10,12... | collective-permute-start | bytes 589832 | tf_op jit(solution)/shard_map/ppermute | solution.py:177
  82.1 14.5 %collective-permute-start.9 = (f32[16,56,128]{2,1,0:T(8,128)S(1)}, f32[16,56,128]{2,1,0:T(8,128)S(1)}, u32[]{:S(2)}, u32[]{:S(2)}) collective-permute-start(f32[16,56,128]{2,1,0:T(8,128)S(1)} %shard_map.75), channel_id=1, source_target_pairs={{0,2},{1,3},{2,6},{3,7},{4,0},{5,1},{6,4},{7,5},{8,10},{9,11},{10,... | collective-permute-start | bytes 1376264 | tf_op jit(solution)/shard_map/ppermute | solution.py:177
  88.6 8.0 %collective-permute-start.7 = (bf16[16,56,128]{2,1,0:T(8,128)(2,1)S(1)}, bf16[16,56,128]{2,1,0:T(8,128)(2,1)S(1)}, u32[]{:S(2)}, u32[]{:S(2)}) collective-permute-start(bf16[16,56,128]{2,1,0:T(8,128)(2,1)S(1)} %shard_map.74), channel_id=1, source_target_pairs={{0,0},{1,1},{2,4},{3,5},{4,2},{5,3},{6,6},{7,7},{8,8},{9,9},{10,12... | collective-permute-start | bytes 688136 | tf_op jit(solution)/shard_map/ppermute | solution.py:177
  97.7 23.2 %all-to-all-start.2 = ((bf16[16,56,128]{2,1,0:T(8,128)(2,1)}), bf16[16,56,128]{2,1,0:T(8,128)(2,1)S(1)}, u32[]{:S(2)}, u32[]{:S(2)}) async-start(bf16[16,56,128]{2,1,0:T(8,128)(2,1)} %shard_map.76), calls=%async_computation.2 | async-start | bytes 458752 | tf_op jit(solution)/shard_map/all_to_all | solution.py:249
  103.7 6.4 %collective-permute-start.11 = (bf16[2,8,16,128]{3,2,1,0:T(8,128)(2,1)S(1)}, bf16[2,8,16,128]{3,2,1,0:T(8,128)(2,1)S(1)}, u32[]{:S(2)}, u32[]{:S(2)}) collective-permute-start(bf16[2,8,16,128]{3,2,1,0:T(8,128)(2,1)S(1)} %pad_maximum_fusion.7), channel_id=1, source_target_pairs={{0,2},{1,3},{2,6},{3,7},{4,0},{5,1},{6,4},{7,5},{8,10},{9,11},{10,... | collective-permute-start | bytes 196616 | tf_op jit(solution)/shard_map/ppermute | solution.py:177
  105.6 6.5 %collective-permute-start.10 = (bf16[2,8,16,128]{3,2,1,0:T(8,128)(2,1)S(1)}, bf16[2,8,16,128]{3,2,1,0:T(8,128)(2,1)S(1)}, u32[]{:S(2)}, u32[]{:S(2)}) collective-permute-start(bf16[2,8,16,128]{3,2,1,0:T(8,128)(2,1)S(1)} %pad_maximum_fusion.7), channel_id=1, source_target_pairs={{0,0},{1,1},{2,4},{3,5},{4,2},{5,3},{6,6},{7,7},{8,8},{9,9},{10,12... | collective-permute-start | bytes 196616 | tf_op jit(solution)/shard_map/ppermute | solution.py:177
  112.2 16.5 %copy-start.2 = (s32[1,64]{1,0:T(1,128)S(1)}, s32[1,64]{1,0:T(1,128)}, u32[]{:S(2)}) copy-start(s32[1,64]{1,0:T(1,128)} %param.12) | copy-start | bytes 772
  122.1 25.7 %all-to-all-start.3 = ((bf16[16,56,128]{2,1,0:T(8,128)(2,1)}), bf16[16,56,128]{2,1,0:T(8,128)(2,1)S(1)}, u32[]{:S(2)}, u32[]{:S(2)}) async-start(bf16[16,56,128]{2,1,0:T(8,128)(2,1)} %gather_fusion.1), calls=%async_computation.3 | async-start | bytes 458752 | tf_op jit(solution)/shard_map/all_to_all | solution.py:274

commit v4 on v3

--- a/solution.py
+++ b/solution.py
@@ -25,6 +25,10 @@
 PIECES = 16
 PIECE = ROWS // PIECES
 EXTRA = 8
+LANES = 128
+UNITS = ROWS // LANES
+PACKED = ROWS + 32
+PACKED_WIDE = ROWS + 8
 SCALE2 = HD ** (-0.5) * math.log2(math.e)
 CHUNK = 1024
 
@@ -70,40 +74,57 @@
         rest[pl.ds(HALF + n * SUF, SUF)] = got[i, pl.ds(2 * BLOCK, SUF)]
 
 
-def on_diagonal():
-    row = lax.broadcasted_iota(jnp.int32, (PIECE, HD), 0)
-    lane = lax.broadcasted_iota(jnp.int32, (PIECE, HD), 1)
-    return row == lane
+def on_diagonal(rows):
+    row = lax.broadcasted_iota(jnp.int32, (rows, LANES), 0)
+    return row == lax.broadcasted_iota(jnp.int32, (rows, LANES), 1)
+
+
+def unit(u):
+    return pl.ds(u * LANES, LANES)
+
+
+def to_line(column):
+    return jnp.sum(jnp.where(on_diagonal(column.shape[0]), column, 0.0), axis=0, keepdims=True)
+
+
+def to_column(line, rows):
+    return jnp.sum(jnp.where(on_diagonal(rows), line, 0.0), axis=1, keepdims=True)
+
+
+def store_lines(out_ref, lines):
+    lines = jnp.concatenate(lines + [jnp.zeros((8 - UNITS, LANES), F32)], axis=0)
+    if out_ref.dtype == BF16:
+        parts = [part.astype(F32) for part in split3(lines)]
+        lines = jnp.concatenate(parts + [jnp.zeros((8, LANES), F32)], axis=0).astype(BF16)
+    out_ref[pl.ds(ROWS, lines.shape[0])] = lines
+
+
+def load_lines(ref):
+    if ref.dtype == BF16:
+        parts = ref[pl.ds(ROWS, PACKED - ROWS)].astype(F32)
+        return parts[0:8] + parts[8:16] + parts[16:24]
+    return ref[pl.ds(ROWS, PACKED_WIDE - ROWS)]
 
 
 def pack(o, lse):
-    line = jnp.sum(jnp.where(on_diagonal(), lse, 0.0), axis=0, keepdims=True)
+    line = to_line(lse)
     hi, mid, low = (jnp.broadcast_to(part.astype(F32), (EXTRA, HD)) for part in split3(line))
     row = lax.broadcasted_iota(jnp.int32, (EXTRA, HD), 0)
     parts = jnp.where(row == 0, hi, jnp.where(row == 1, mid, jnp.where(row == 2, low, 0.0)))
     return jnp.concatenate([o, parts], axis=0).astype(BF16)
 
 
-def pack_wide(o, lse):
-    line = jnp.sum(jnp.where(on_diagonal(), lse, 0.0), axis=0, keepdims=True)
-    row = lax.broadcasted_iota(jnp.int32, (EXTRA, HD), 0)
-    return jnp.concatenate([o, jnp.where(row == 0, line, 0.0)], axis=0)
-
-
 def unpack(piece):
     piece = piece.astype(F32)
     line = jnp.sum(piece[PIECE:], axis=0, keepdims=True)
-    lse = jnp.sum(jnp.where(on_diagonal(), line, 0.0), axis=1, keepdims=True)
-    return piece[:PIECE], lse
-
-
-def attend_kernel(q_ref, k_a, v_a, k_b, v_b, out_ref, o_sc, lse_sc):
-    o_sc[...], lse = attend(q_ref[...], ((k_a, v_a), (k_b, v_b)))
-    lse_sc[...] = jnp.broadcast_to(lse, (ROWS, HD))
-    code = pack if out_ref.dtype == BF16 else pack_wide
-    for p in range(PIECES):
-        at = pl.ds(p * PIECE, PIECE)
-        out_ref[p] = code(o_sc[at], lse_sc[at])
+    return piece[:PIECE], to_column(line, PIECE)
+
+
+def attend_kernel(q_ref, k_a, v_a, k_b, v_b, out_ref, lse_sc):
+    o, lse = attend(q_ref[...], ((k_a, v_a), (k_b, v_b)))
+    out_ref[pl.ds(0, ROWS)] = o.astype(out_ref.dtype)
+    lse_sc[...] = jnp.broadcast_to(lse, (ROWS, LANES))
+    store_lines(out_ref, [to_line(lse_sc[unit(u)]) for u in range(UNITS)])
 
 
 def join(o1, lse1, o2, lse2):
@@ -113,9 +134,16 @@
     return (w1 * o1 + w2 * o2) / total, top + jnp.log2(total)
 
 
-def join_kernel(a_ref, b_ref, out_ref):
+def join_kernel(a_ref, b_ref, out_ref, o_sc, lse_sc):
+    lines_a, lines_b = load_lines(a_ref), load_lines(b_ref)
+    for u in range(UNITS):
+        lse_a, lse_b = (to_column(lines[u : u + 1], LANES) for lines in (lines_a, lines_b))
+        o, lse = join(a_ref[unit(u)].astype(F32), lse_a, b_ref[unit(u)].astype(F32), lse_b)
+        o_sc[unit(u)] = o
+        lse_sc[unit(u)] = jnp.broadcast_to(lse, (LANES, LANES))
     for p in range(PIECES):
-        out_ref[p] = pack(*join(*unpack(a_ref[p]), *unpack(b_ref[p])))
+        at = pl.ds(p * PIECE, PIECE)
+        out_ref[p] = pack(o_sc[at], lse_sc[at])
 
 
 def suffix_kernel(q_ref, k_ref, v_ref, step_ref, sample_ref, o_ref, lse_ref):
@@ -229,16 +257,21 @@
     held = [*mine, *far]
     wide = pltpu.VMEM((ROWS, HD), F32)
     partial = []
-    for there, back, kind in ((there_0, there_0, BF16), (there_1, back_1, F32)):
+    for there, back, kind, size in (
+        (there_0, there_0, BF16, PACKED),
+        (there_1, back_1, F32, PACKED_WIDE),
+    ):
         part = call(
             attend_kernel,
-            [sds(PIECES, PIECE + EXTRA, HD, dtype=kind)],
+            [sds(size, HD, dtype=kind)],
             [permute(home, there), *held],
-            scratch=[wide, wide],
+            scratch=[wide],
             **cost(4096),
         )
         partial.append(permute(part, back))
-    done = call(join_kernel, [sds(PIECES, PIECE + EXTRA, HD, dtype=BF16)], partial)
+    done = call(
+        join_kernel, [sds(PIECES, PIECE + EXTRA, HD, dtype=BF16)], partial, scratch=[wide, wide]
+    )
 
     tail = jnp.stack([e[1][HALF:].reshape(8, SUF, HD) for e in (mine, far)])
     done, tail = lax.optimization_barrier((done, tail))

time: 150 us -> 149 us (level)
  starting transfers between devices: 68.9 us -> 66.4 us
    all_to_all x1, waiting for transfers between devices: 8.67 us -> 10.3 us  [local(): gone = lax.all_to_all(done, 'prompt', 0, 0, tiled=True)]
where the time goes in v4:
time: 149 us; the launch traced here: 147 us
  starting transfers between devices  66.4 us (45%)
  waiting for transfers between devices  60.5 us (41%)
  Pallas kernels  12.9 us (9%)
  local copies, waits for them, and re-layouts  5.86 us (4%)
    ppermute x12, starting transfers between devices, permute(): return lax.ppermute(a, 'tp', pairs)  38.9 us
    all_to_all x1, waiting for transfers between devices, local(): back = lax.all_to_all(sorted_out, 'prompt', 0, 0, tiled=True)  17 us
    all_to_all x1, waiting for transfers between devices, local(): lax.all_to_all(sorted_in, 'prompt', 0, 0, tiled=True).reshape(ROWS, HD)  14.1 us
    pallas_call x6, Pallas kernels, call(): pl.pallas_call(kernel, out_shape=tuple(outs) if many else outs[0], in_spe...  12.9 us
    all_to_all x1, starting transfers between devices, local(): spread = lax.all_to_all(pieces, 'prompt', 0, 0, tiled=True)  12.5 us
    ppermute x12, waiting for transfers between devices, permute(): return lax.ppermute(a, 'tp', pairs)  11 us
    all_to_all x1, waiting for transfers between devices, local(): gone = lax.all_to_all(done, 'prompt', 0, 0, tiled=True)  10.3 us
    all_to_all x1, waiting for transfers between devices, local(): spread = lax.all_to_all(pieces, 'prompt', 0, 0, tiled=True)  8.13 us
  transfers between devices with their start and end apart: 16, of which 8 were waited for; matrix products, arithmetic and copies ran while one was open for 2% of the time, Pallas kernels for 7%

profile of v4, /device:TPU:32, one launch (start us, length us, event | category | flops | bytes accessed | tf_op | source)
XLA Modules:
  0.0 147.4 jit_solution(565802215338649600)
XLA Ops:
  0.8 1.3 dynamic-slice_bitcast_fusion.2
  2.1 7.5 %collective-permute-start.1 = (bf16[4,528,128]{2,1,0:T(8,128)(2,1)S(1)}, bf16[4,528,128]{2,1,0:T(8,128)(2,1)S(1)}, u32[]{:S(2)}, u32[]{:S(2)}) collective-permute-start(bf16[4,528,128]{2,1,0:T(8,128)(2,1)S(1)} %pad_maximum_fusion.1), channel_id=1, source_target_pairs={{0,2},{1,3},{2,0},{3,1},{4,6},{5,7},{6,4},{7,5},{8,10},{9,11},{10,... | collective-permute-start | bytes 1622024 | tf_op jit(solution)/shard_map/ppermute | solution.py:205
  10.4 12.5 %all-to-all-start = ((bf16[16,48,128]{2,1,0:T(8,128)(2,1)}), bf16[16,48,128]{2,1,0:T(8,128)(2,1)S(1)}, u32[]{:S(2)}, u32[]{:S(2)}) async-start(bf16[16,48,128]{2,1,0:T(8,128)(2,1)} %bitcast.1), calls=%async_computation | async-start | bytes 393216 | tf_op jit(solution)/shard_map/all_to_all | solution.py:229
  23.2 3.4 %collective-permute-start.2 = (bf16[2,528,128]{2,1,0:T(8,128)(2,1)S(1)}, bf16[2,528,128]{2,1,0:T(8,128)(2,1)S(1)}, u32[]{:S(2)}, u32[]{:S(2)}) collective-permute-start(bf16[2,528,128]{2,1,0:T(8,128)(2,1)S(1)} %pad_maximum_fusion.3), channel_id=1, source_target_pairs={{0,8},{1,9},{2,10},{3,11},{4,12},{5,13},{6,14},{7,15},{8,16},{9,17... | collective-permute-start | bytes 811016 | tf_op jit(solution)/shard_map/ppermute | solution.py:205
  26.6 4.6 %collective-permute-start.3 = (bf16[2,528,128]{2,1,0:T(8,128)(2,1)S(1)}, bf16[2,528,128]{2,1,0:T(8,128)(2,1)S(1)}, u32[]{:S(2)}, u32[]{:S(2)}) collective-permute-start(bf16[2,528,128]{2,1,0:T(8,128)(2,1)S(1)} %pad_maximum_fusion.4), channel_id=1, source_target_pairs={{0,16},{1,17},{2,18},{3,19},{4,20},{5,21},{6,22},{7,23},{8,24},{9,... | collective-permute-start | bytes 811016 | tf_op jit(solution)/shard_map/ppermute | solution.py:205
  31.3 3.3 %collective-permute-start.4 = (bf16[2,528,128]{2,1,0:T(8,128)(2,1)S(1)}, bf16[2,528,128]{2,1,0:T(8,128)(2,1)S(1)}, u32[]{:S(2)}, u32[]{:S(2)}) collective-permute-start(bf16[2,528,128]{2,1,0:T(8,128)(2,1)S(1)} %pad_maximum_fusion.5), channel_id=1, source_target_pairs={{0,24},{1,25},{2,26},{3,27},{4,28},{5,29},{6,30},{7,31},{8,0},{9,1... | collective-permute-start | bytes 811016 | tf_op jit(solution)/shard_map/ppermute | solution.py:205
  34.8 8.1 %all-to-all-done = bf16[16,48,128]{2,1,0:T(8,128)(2,1)S(1)} async-done(((bf16[16,48,128]{2,1,0:T(8,128)(2,1)}), bf16[16,48,128]{2,1,0:T(8,128)(2,1)S(1)}, u32[]{:S(2)}, u32[]{:S(2)}) %all-to-all-start) | async-done | bytes 196640 | tf_op jit(solution)/shard_map/all_to_all | solution.py:229
  43.0 1.2 gather_fusion
  44.2 6.2 %all-to-all-start.1 = ((bf16[16,48,128]{2,1,0:T(8,128)(2,1)}), bf16[16,48,128]{2,1,0:T(8,128)(2,1)S(1)}, u32[]{:S(2)}, u32[]{:S(2)}) async-start(bf16[16,48,128]{2,1,0:T(8,128)(2,1)} %gather_fusion), calls=%async_computation.1 | async-start | bytes 393216 | tf_op jit(solution)/shard_map/all_to_all | solution.py:251
  50.6 1.9 %collective-permute-start.6 = (bf16[2176,128]{1,0:T(8,128)(2,1)S(1)}, bf16[2176,128]{1,0:T(8,128)(2,1)S(1)}, u32[]{:S(2)}, u32[]{:S(2)}) collective-permute-start(bf16[2176,128]{1,0:T(8,128)(2,1)S(1)} %get-tuple-element.16.v_a), channel_id=1, source_target_pairs={{0,1},{1,0},{2,3},{3,2},{4,5},{5,4},{6,7},{7,6},{8,9},{9,8},{10,11... | collective-permute-start | bytes 1671176 | tf_op jit(solution)/shard_map/ppermute | solution.py:205
  52.5 2.4 %collective-permute-start.5 = (bf16[2048,128]{1,0:T(8,128)(2,1)S(1)}, bf16[2048,128]{1,0:T(8,128)(2,1)S(1)}, u32[]{:S(2)}, u32[]{:S(2)}) collective-permute-start(bf16[2048,128]{1,0:T(8,128)(2,1)S(1)} %get-tuple-element.15.k_a), channel_id=1, source_target_pairs={{0,1},{1,0},{2,3},{3,2},{4,5},{5,4},{6,7},{7,6},{8,9},{9,8},{10,11... | collective-permute-start | bytes 1572872 | tf_op jit(solution)/shard_map/ppermute | solution.py:205
  54.9 14.1 %all-to-all-done.1 = bf16[16,48,128]{2,1,0:T(8,128)(2,1)S(1)} async-done(((bf16[16,48,128]{2,1,0:T(8,128)(2,1)}), bf16[16,48,128]{2,1,0:T(8,128)(2,1)S(1)}, u32[]{:S(2)}, u32[]{:S(2)}) %all-to-all-start.1) | async-done | bytes 196640 | tf_op jit(solution)/shard_map/all_to_all | solution.py:251
  69.0 1.9 %collective-permute-start.8 = (bf16[768,128]{1,0:T(8,128)(2,1)S(1)}, bf16[768,128]{1,0:T(8,128)(2,1)S(1)}, u32[]{:S(2)}, u32[]{:S(2)}) collective-permute-start(bf16[768,128]{1,0:T(8,128)(2,1)S(1)} %bitcast.42), channel_id=1, source_target_pairs={{0,4},{1,5},{2,0},{3,1},{4,6},{5,7},{6,2},{7,3},{8,12},{9,13},{10,... | collective-permute-start | bytes 589832 | tf_op jit(solution)/shard_map/ppermute | solution.py:205
  70.9 3.2 %collective-permute-start = (bf16[768,128]{1,0:T(8,128)(2,1)S(1)}, bf16[768,128]{1,0:T(8,128)(2,1)S(1)}, u32[]{:S(2)}, u32[]{:S(2)}) collective-permute-start(bf16[768,128]{1,0:T(8,128)(2,1)S(1)} %bitcast.43), channel_id=1, source_target_pairs={{0,0},{1,1},{2,4},{3,5},{4,2},{5,3},{6,6},{7,7},{8,8},{9,9},{10,12... | collective-permute-start | bytes 589832 | tf_op jit(solution)/shard_map/ppermute | solution.py:205
  74.1 3.4 %collective-permute-done.8.q_ref = bf16[768,128]{1,0:T(8,128)(2,1)S(1)} collective-permute-done((bf16[768,128]{1,0:T(8,128)(2,1)S(1)}, bf16[768,128]{1,0:T(8,128)(2,1)S(1)}, u32[]{:S(2)}, u32[]{:S(2)}) %collective-permute-start.8) | collective-permute-done | bytes 196640 | tf_op jit(solution)/shard_map/ppermute | solution.py:205
  77.5 4.5 %shard_map.75 = f32[776,128]{1,0:T(8,128)S(1)} custom-call(bf16[768,128]{1,0:T(8,128)(2,1)S(1)} %collective-permute-done.8.q_ref, bf16[2048,128]{1,0:T(8,128)(2,1)S(1)} %get-tuple-element.15.k_a, bf16[2176,128]{1,0:T(8,128)(2,1)S(1)} %get-tuple-element.16.v_a, bf16[2048,128]{1,0:T(8,128)(2,1)S(1)} %collective-permute-done.5.k_b, ...), custom_call_target="tpu_custom_call" | custom-call | flops 1610612736 | bytes 2756608 | tf_op jit(solution)/shard_map/pallas_call | solution.py:175
  82.1 1.9 %collective-permute-start.9 = (f32[776,128]{1,0:T(8,128)S(1)}, f32[776,128]{1,0:T(8,128)S(1)}, u32[]{:S(2)}, u32[]{:S(2)}) collective-permute-start(f32[776,128]{1,0:T(8,128)S(1)} %shard_map.75), channel_id=1, source_target_pairs={{0,2},{1,3},{2,6},{3,7},{4,0},{5,1},{6,4},{7,5},{8,10},{9,11},{10,... | collective-permute-start | bytes 1191944 | tf_op jit(solution)/shard_map/ppermute | solution.py:205
  84.0 4.5 %shard_map.74 = bf16[800,128]{1,0:T(8,128)(2,1)S(1)} custom-call(bf16[768,128]{1,0:T(8,128)(2,1)S(1)} %collective-permute-done.q_ref, bf16[2048,128]{1,0:T(8,128)(2,1)S(1)} %get-tuple-element.15.k_a, bf16[2176,128]{1,0:T(8,128)(2,1)S(1)} %get-tuple-element.16.v_a, bf16[2048,128]{1,0:T(8,128)(2,1)S(1)} %collective-permute-done.5.k_b, ...), custom_call_target="tpu_custom_call" | custom-call | flops 1610612736 | bytes 2564096 | tf_op jit(solution)/shard_map/pallas_call | solution.py:175
  88.5 3.4 %collective-permute-start.7 = (bf16[800,128]{1,0:T(8,128)(2,1)S(1)}, bf16[800,128]{1,0:T(8,128)(2,1)S(1)}, u32[]{:S(2)}, u32[]{:S(2)}) collective-permute-start(bf16[800,128]{1,0:T(8,128)(2,1)S(1)} %shard_map.74), channel_id=1, source_target_pairs={{0,0},{1,1},{2,4},{3,5},{4,2},{5,3},{6,6},{7,7},{8,8},{9,9},{10,12... | collective-permute-start | bytes 614408 | tf_op jit(solution)/shard_map/ppermute | solution.py:205
  92.0 4.2 %collective-permute-done.7.a_ref = bf16[800,128]{1,0:T(8,128)(2,1)S(1)} collective-permute-done((bf16[800,128]{1,0:T(8,128)(2,1)S(1)}, bf16[800,128]{1,0:T(8,128)(2,1)S(1)}, u32[]{:S(2)}, u32[]{:S(2)}) %collective-permute-start.7) | collective-permute-done | bytes 204832 | tf_op jit(solution)/shard_map/ppermute | solution.py:205
  96.2 1.1 shard_map.76
  97.3 4.1 %all-to-all-start.2 = ((bf16[16,56,128]{2,1,0:T(8,128)(2,1)}), bf16[16,56,128]{2,1,0:T(8,128)(2,1)S(1)}, u32[]{:S(2)}, u32[]{:S(2)}) async-start(bf16[16,56,128]{2,1,0:T(8,128)(2,1)} %shard_map.76), calls=%async_computation.2 | async-start | bytes 458752 | tf_op jit(solution)/shard_map/all_to_all | solution.py:282
  101.8 1.9 %collective-permute-start.11 = (bf16[2,8,16,128]{3,2,1,0:T(8,128)(2,1)S(1)}, bf16[2,8,16,128]{3,2,1,0:T(8,128)(2,1)S(1)}, u32[]{:S(2)}, u32[]{:S(2)}) collective-permute-start(bf16[2,8,16,128]{3,2,1,0:T(8,128)(2,1)S(1)} %pad_maximum_fusion.7), channel_id=1, source_target_pairs={{0,2},{1,3},{2,6},{3,7},{4,0},{5,1},{6,4},{7,5},{8,10},{9,11},{10,... | collective-permute-start | bytes 196616 | tf_op jit(solution)/shard_map/ppermute | solution.py:205
  103.8 3.4 %collective-permute-start.10 = (bf16[2,8,16,128]{3,2,1,0:T(8,128)(2,1)S(1)}, bf16[2,8,16,128]{3,2,1,0:T(8,128)(2,1)S(1)}, u32[]{:S(2)}, u32[]{:S(2)}) collective-permute-start(bf16[2,8,16,128]{3,2,1,0:T(8,128)(2,1)S(1)} %pad_maximum_fusion.7), channel_id=1, source_target_pairs={{0,0},{1,1},{2,4},{3,5},{4,2},{5,3},{6,6},{7,7},{8,8},{9,9},{10,12... | collective-permute-start | bytes 196616 | tf_op jit(solution)/shard_map/ppermute | solution.py:205
  107.2 1.1 collective-permute-done.11
  108.3 2.1 %collective-permute-done.10 = bf16[2,8,16,128]{3,2,1,0:T(8,128)(2,1)S(1)} collective-permute-done((bf16[2,8,16,128]{3,2,1,0:T(8,128)(2,1)S(1)}, bf16[2,8,16,128]{3,2,1,0:T(8,128)(2,1)S(1)}, u32[]{:S(2)}, u32[]{:S(2)}) %collective-permute-start.10) | collective-permute-done | bytes 65568 | tf_op jit(solution)/shard_map/ppermute | solution.py:205
  110.5 10.3 %all-to-all-done.2 = bf16[16,56,128]{2,1,0:T(8,128)(2,1)S(1)} async-done(((bf16[16,56,128]{2,1,0:T(8,128)(2,1)}), bf16[16,56,128]{2,1,0:T(8,128)(2,1)S(1)}, u32[]{:S(2)}, u32[]{:S(2)}) %all-to-all-start.2) | async-done | bytes 229408 | tf_op jit(solution)/shard_map/all_to_all | solution.py:282
  120.8 1.3 gather_fusion.1
  122.1 4.7 %all-to-all-start.3 = ((bf16[16,56,128]{2,1,0:T(8,128)(2,1)}), bf16[16,56,128]{2,1,0:T(8,128)(2,1)S(1)}, u32[]{:S(2)}, u32[]{:S(2)}) async-start(bf16[16,56,128]{2,1,0:T(8,128)(2,1)} %gather_fusion.1), calls=%async_computation.3 | async-start | bytes 458752 | tf_op jit(solution)/shard_map/all_to_all | solution.py:307
  127.7 1.7 %shard_map.77 = (f32[768,128]{1,0:T(8,128)S(1)}, f32[768,128]{1,0:T(8,128)S(1)}) custom-call(bf16[768,128]{1,0:T(8,128)(2,1)} %bitcast.18.q_ref, bf16[192,128]{1,0:T(8,128)(2,1)S(1)} %reshape.111.k_ref, bf16[192,128]{1,0:T(8,128)(2,1)S(1)} %reshape.112.v_ref, s32[192,192]{1,0:T(8,128)S(1)} %broadcast_in_dim.46.step_ref, ...), custom_call_target="tpu_custom_call" | custom-call | flops 75497472 | bytes 1376256 | tf_op jit(solution)/shard_map/pallas_call | solution.py:175
  129.4 17.0 %all-to-all-done.3.r_ref = bf16[16,56,128]{2,1,0:T(8,128)(2,1)S(1)} async-done(((bf16[16,56,128]{2,1,0:T(8,128)(2,1)}), bf16[16,56,128]{2,1,0:T(8,128)(2,1)S(1)}, u32[]{:S(2)}, u32[]{:S(2)}) %all-to-all-start.3) | async-done | bytes 229408 | tf_op jit(solution)/shard_map/all_to_all | solution.py:307
  146.4 1.0 shard_map.78
  (58 shorter events, 3.3 us)
Async XLA Ops:
  2.1 7.6 %copy-start = (bf16[1,3,64,512]{3,2,1,0:T(8,128)(2,1)S(1)}, bf16[1,3,64,512]{3,2,1,0:T(8,128)(2,1)}, u32[]{:S(2)}) copy-start(bf16[1,3,64,512]{3,2,1,0:T(8,128)(2,1)} %param.9) | copy-start | bytes 589828
  2.1 20.9 %collective-permute-start.1 = (bf16[4,528,128]{2,1,0:T(8,128)(2,1)S(1)}, bf16[4,528,128]{2,1,0:T(8,128)(2,1)S(1)}, u32[]{:S(2)}, u32[]{:S(2)}) collective-permute-start(bf16[4,528,128]{2,1,0:T(8,128)(2,1)S(1)} %pad_maximum_fusion.1), channel_id=1, source_target_pairs={{0,2},{1,3},{2,0},{3,1},{4,6},{5,7},{6,4},{7,5},{8,10},{9,11},{10,... | collective-permute-start | bytes 1622024 | tf_op jit(solution)/shard_map/ppermute | solution.py:205
  10.4 32.5 %all-to-all-start = ((bf16[16,48,128]{2,1,0:T(8,128)(2,1)}), bf16[16,48,128]{2,1,0:T(8,128)(2,1)S(1)}, u32[]{:S(2)}, u32[]{:S(2)}) async-start(bf16[16,48,128]{2,1,0:T(8,128)(2,1)} %bitcast.1), calls=%async_computation | async-start | bytes 393216 | tf_op jit(solution)/shard_map/all_to_all | solution.py:229
  23.2 11.5 %copy-start.1 = (s32[16]{0:T(128)S(1)}, s32[16]{0:T(128)}, u32[]{:S(2)}) copy-start(s32[16]{0:T(128)} %param.13) | copy-start | bytes 196
  23.2 27.3 %collective-permute-start.2 = (bf16[2,528,128]{2,1,0:T(8,128)(2,1)S(1)}, bf16[2,528,128]{2,1,0:T(8,128)(2,1)S(1)}, u32[]{:S(2)}, u32[]{:S(2)}) collective-permute-start(bf16[2,528,128]{2,1,0:T(8,128)(2,1)S(1)} %pad_maximum_fusion.3), channel_id=1, source_target_pairs={{0,8},{1,9},{2,10},{3,11},{4,12},{5,13},{6,14},{7,15},{8,16},{9,17... | collective-permute-start | bytes 811016 | tf_op jit(solution)/shard_map/ppermute | solution.py:205
  26.6 23.8 %collective-permute-start.3 = (bf16[2,528,128]{2,1,0:T(8,128)(2,1)S(1)}, bf16[2,528,128]{2,1,0:T(8,128)(2,1)S(1)}, u32[]{:S(2)}, u32[]{:S(2)}) collective-permute-start(bf16[2,528,128]{2,1,0:T(8,128)(2,1)S(1)} %pad_maximum_fusion.4), channel_id=1, source_target_pairs={{0,16},{1,17},{2,18},{3,19},{4,20},{5,21},{6,22},{7,23},{8,24},{9,... | collective-permute-start | bytes 811016 | tf_op jit(solution)/shard_map/ppermute | solution.py:205
  31.3 19.1 %collective-permute-start.4 = (bf16[2,528,128]{2,1,0:T(8,128)(2,1)S(1)}, bf16[2,528,128]{2,1,0:T(8,128)(2,1)S(1)}, u32[]{:S(2)}, u32[]{:S(2)}) collective-permute-start(bf16[2,528,128]{2,1,0:T(8,128)(2,1)S(1)} %pad_maximum_fusion.5), channel_id=1, source_target_pairs={{0,24},{1,25},{2,26},{3,27},{4,28},{5,29},{6,30},{7,31},{8,0},{9,1... | collective-permute-start | bytes 811016 | tf_op jit(solution)/shard_map/ppermute | solution.py:205
  44.2 24.8 %all-to-all-start.1 = ((bf16[16,48,128]{2,1,0:T(8,128)(2,1)}), bf16[16,48,128]{2,1,0:T(8,128)(2,1)S(1)}, u32[]{:S(2)}, u32[]{:S(2)}) async-start(bf16[16,48,128]{2,1,0:T(8,128)(2,1)} %gather_fusion), calls=%async_computation.1 | async-start | bytes 393216 | tf_op jit(solution)/shard_map/all_to_all | solution.py:251
  50.6 23.5 %collective-permute-start.6 = (bf16[2176,128]{1,0:T(8,128)(2,1)S(1)}, bf16[2176,128]{1,0:T(8,128)(2,1)S(1)}, u32[]{:S(2)}, u32[]{:S(2)}) collective-permute-start(bf16[2176,128]{1,0:T(8,128)(2,1)S(1)} %get-tuple-element.16.v_a), channel_id=1, source_target_pairs={{0,1},{1,0},{2,3},{3,2},{4,5},{5,4},{6,7},{7,6},{8,9},{9,8},{10,11... | collective-permute-start | bytes 1671176 | tf_op jit(solution)/shard_map/ppermute | solution.py:205
  52.5 21.6 %collective-permute-start.5 = (bf16[2048,128]{1,0:T(8,128)(2,1)S(1)}, bf16[2048,128]{1,0:T(8,128)(2,1)S(1)}, u32[]{:S(2)}, u32[]{:S(2)}) collective-permute-start(bf16[2048,128]{1,0:T(8,128)(2,1)S(1)} %get-tuple-element.15.k_a), channel_id=1, source_target_pairs={{0,1},{1,0},{2,3},{3,2},{4,5},{5,4},{6,7},{7,6},{8,9},{9,8},{10,11... | collective-permute-start | bytes 1572872 | tf_op jit(solution)/shard_map/ppermute | solution.py:205
  69.0 8.6 %collective-permute-start.8 = (bf16[768,128]{1,0:T(8,128)(2,1)S(1)}, bf16[768,128]{1,0:T(8,128)(2,1)S(1)}, u32[]{:S(2)}, u32[]{:S(2)}) collective-permute-start(bf16[768,128]{1,0:T(8,128)(2,1)S(1)} %bitcast.42), channel_id=1, source_target_pairs={{0,4},{1,5},{2,0},{3,1},{4,6},{5,7},{6,2},{7,3},{8,12},{9,13},{10,... | collective-permute-start | bytes 589832 | tf_op jit(solution)/shard_map/ppermute | solution.py:205
  70.9 13.1 %collective-permute-start = (bf16[768,128]{1,0:T(8,128)(2,1)S(1)}, bf16[768,128]{1,0:T(8,128)(2,1)S(1)}, u32[]{:S(2)}, u32[]{:S(2)}) collective-permute-start(bf16[768,128]{1,0:T(8,128)(2,1)S(1)} %bitcast.43), channel_id=1, source_target_pairs={{0,0},{1,1},{2,4},{3,5},{4,2},{5,3},{6,6},{7,7},{8,8},{9,9},{10,12... | collective-permute-start | bytes 589832 | tf_op jit(solution)/shard_map/ppermute | solution.py:205
  82.1 14.1 %collective-permute-start.9 = (f32[776,128]{1,0:T(8,128)S(1)}, f32[776,128]{1,0:T(8,128)S(1)}, u32[]{:S(2)}, u32[]{:S(2)}) collective-permute-start(f32[776,128]{1,0:T(8,128)S(1)} %shard_map.75), channel_id=1, source_target_pairs={{0,2},{1,3},{2,6},{3,7},{4,0},{5,1},{6,4},{7,5},{8,10},{9,11},{10,... | collective-permute-start | bytes 1191944 | tf_op jit(solution)/shard_map/ppermute | solution.py:205
  88.5 7.7 %collective-permute-start.7 = (bf16[800,128]{1,0:T(8,128)(2,1)S(1)}, bf16[800,128]{1,0:T(8,128)(2,1)S(1)}, u32[]{:S(2)}, u32[]{:S(2)}) collective-permute-start(bf16[800,128]{1,0:T(8,128)(2,1)S(1)} %shard_map.74), channel_id=1, source_target_pairs={{0,0},{1,1},{2,4},{3,5},{4,2},{5,3},{6,6},{7,7},{8,8},{9,9},{10,12... | collective-permute-start | bytes 614408 | tf_op jit(solution)/shard_map/ppermute | solution.py:205
  97.3 23.6 %all-to-all-start.2 = ((bf16[16,56,128]{2,1,0:T(8,128)(2,1)}), bf16[16,56,128]{2,1,0:T(8,128)(2,1)S(1)}, u32[]{:S(2)}, u32[]{:S(2)}) async-start(bf16[16,56,128]{2,1,0:T(8,128)(2,1)} %shard_map.76), calls=%async_computation.2 | async-start | bytes 458752 | tf_op jit(solution)/shard_map/all_to_all | solution.py:282
  101.8 6.5 %collective-permute-start.11 = (bf16[2,8,16,128]{3,2,1,0:T(8,128)(2,1)S(1)}, bf16[2,8,16,128]{3,2,1,0:T(8,128)(2,1)S(1)}, u32[]{:S(2)}, u32[]{:S(2)}) collective-permute-start(bf16[2,8,16,128]{3,2,1,0:T(8,128)(2,1)S(1)} %pad_maximum_fusion.7), channel_id=1, source_target_pairs={{0,2},{1,3},{2,6},{3,7},{4,0},{5,1},{6,4},{7,5},{8,10},{9,11},{10,... | collective-permute-start | bytes 196616 | tf_op jit(solution)/shard_map/ppermute | solution.py:205
  103.8 6.7 %collective-permute-start.10 = (bf16[2,8,16,128]{3,2,1,0:T(8,128)(2,1)S(1)}, bf16[2,8,16,128]{3,2,1,0:T(8,128)(2,1)S(1)}, u32[]{:S(2)}, u32[]{:S(2)}) collective-permute-start(bf16[2,8,16,128]{3,2,1,0:T(8,128)(2,1)S(1)} %pad_maximum_fusion.7), channel_id=1, source_target_pairs={{0,0},{1,1},{2,4},{3,5},{4,2},{5,3},{6,6},{7,7},{8,8},{9,9},{10,12... | collective-permute-start | bytes 196616 | tf_op jit(solution)/shard_map/ppermute | solution.py:205
  110.5 16.9 %copy-start.2 = (s32[1,64]{1,0:T(1,128)S(1)}, s32[1,64]{1,0:T(1,128)}, u32[]{:S(2)}) copy-start(s32[1,64]{1,0:T(1,128)} %param.12) | copy-start | bytes 772
  122.1 24.3 %all-to-all-start.3 = ((bf16[16,56,128]{2,1,0:T(8,128)(2,1)}), bf16[16,56,128]{2,1,0:T(8,128)(2,1)S(1)}, u32[]{:S(2)}, u32[]{:S(2)}) async-start(bf16[16,56,128]{2,1,0:T(8,128)(2,1)} %gather_fusion.1), calls=%async_computation.3 | async-start | bytes 458752 | tf_op jit(solution)/shard_map/all_to_all | solution.py:307

commit v5 on v4

--- a/solution.py
+++ b/solution.py
@@ -31,6 +31,7 @@
 PACKED_WIDE = ROWS + 8
 SCALE2 = HD ** (-0.5) * math.log2(math.e)
 CHUNK = 1024
+FIRST = 10
 
 
 def dot_t(a, b):
@@ -66,6 +67,13 @@
     return acc / l, m + jnp.log2(l)
 
 
+def deal_kernel(x_ref, kept, came, *outs):
+    for k, out in enumerate(outs):
+        to = lax.rem(x_ref[0] + k, 4)
+        out[0] = kept[to]
+        out[1] = came[to]
+
+
 def sort_kernel(*refs):
     *blocks, keys, rest = refs
     for n, (got, i) in enumerate((got, i) for got in blocks for i in range(2)):
@@ -169,13 +177,14 @@
         out_ref[tok, pl.ds((p // per_head) * HD, HD)] = merged.astype(BF16)
 
 
-def call(kernel, outs, args, scratch=(), flops=0, exps=0):
+def call(kernel, outs, args, scratch=(), flops=0, exps=0, scalars=0):
     moved = sum(math.prod(a.shape) * a.dtype.itemsize for a in (*args, *outs))
+    smem = pl.BlockSpec(memory_space=pltpu.SMEM)
     many = len(outs) > 1
     return pl.pallas_call(
         kernel,
         out_shape=tuple(outs) if many else outs[0],
-        in_specs=[VMEM] * len(args),
+        in_specs=[smem] * scalars + [VMEM] * (len(args) - scalars),
         out_specs=(VMEM,) * len(outs) if many else VMEM,
         scratch_shapes=list(scratch),
         compiler_params=pltpu.CompilerParams(vmem_limit_bytes=40 * 2**20),
@@ -185,6 +194,15 @@
 
 def sds(*shape, dtype=F32):
     return jax.ShapeDtypeStruct(shape, dtype)
+
+
+def exchange(a):
+    order = [(i + FIRST) % PIECES for i in range(PIECES)]
+    return lax.all_to_all(a, "prompt", 0, 0, tiled=True, axis_index_groups=[order])
+
+
+def in_order(index):
+    return (jnp.roll(index, -FIRST) + PIECES - FIRST) % PIECES
 
 
 def local(
@@ -226,29 +244,31 @@
 
     rows = jnp.transpose(queries[0].reshape(TOKENS, HEADS, HD), (1, 0, 2))
     pieces = rows.reshape(PIECES, PIECE, HD)
-    spread = lax.all_to_all(pieces, "prompt", 0, 0, tiled=True)
+    spread = exchange(pieces)
     index = jnp.arange(PIECES, dtype=jnp.int32)
     server = jnp.sum(jnp.where(assignment[None, :] == index[:, None], index[None, :], 0), axis=1)
-    sorted_in = jnp.take(spread, server, axis=0, mode="clip")
+    sorted_in = jnp.take(spread, in_order(server), axis=0, mode="clip")
     kept = of_parity(z % 2)
     came = permute(of_parity(1 - z % 2), lambda xx, zz, cc: (xx, zz ^ 1, cc))
 
-    def payload(to):
-        return jnp.stack(
-            [lax.dynamic_index_in_dim(a, to, 0, keepdims=False) for a in (kept, came)]
-        )
-
-    got = [payload(x)]
+    dealt = call(
+        deal_kernel,
+        [sds(2, PART, HD, dtype=BF16)] * 4,
+        [x.reshape(1), kept, came],
+        flops=SORT_FLOPS,
+        scalars=1,
+    )
+    got = [dealt[0]]
     for k in (1, 2, 3):
         shift = lambda xx, zz, cc, k=k: ((xx + k) % 4, zz, cc)
-        got.append(permute(payload((x + k) % 4), shift))
+        got.append(permute(dealt[k], shift))
     mine = call(
         sort_kernel,
         [sds(HALF, HD, dtype=BF16), sds(HALF + 8 * SUF, HD, dtype=BF16)],
         got,
         flops=SORT_FLOPS,
     )
-    home = lax.all_to_all(sorted_in, "prompt", 0, 0, tiled=True).reshape(ROWS, HD)
+    home = exchange(sorted_in).reshape(ROWS, HD)
     far = [permute(a, lambda xx, zz, cc: (xx, zz, cc ^ 1)) for a in mine]
 
     def cost(positions):
@@ -279,9 +299,9 @@
     live = jnp.arange(STEPS, dtype=jnp.int32)[:, None] < suffix_lengths[0][None, :]
     live = jnp.broadcast_to(live.reshape(TOKENS, 1), (TOKENS, HD)).astype(jnp.int32)
 
-    gone = lax.all_to_all(done, "prompt", 0, 0, tiled=True)
+    gone = exchange(done)
     gone, tail = lax.optimization_barrier((gone, tail))
-    sorted_out = jnp.take(gone, assignment, axis=0, mode="clip")
+    sorted_out = jnp.take(gone, in_order(assignment), axis=0, mode="clip")
     sorted_out, tail = lax.optimization_barrier((sorted_out, tail))
     suf_k = tail[:, :, :, : 2 * STEPS].reshape(TOKENS, HD)
     suf_v = tail[:, :, :, 2 * STEPS : 4 * STEPS].reshape(TOKENS, HD)
@@ -304,7 +324,7 @@
         flops=4 * ROWS * TOKENS * HD,
         exps=ROWS * TOKENS,
     )
-    back = lax.all_to_all(sorted_out, "prompt", 0, 0, tiled=True)
+    back = exchange(sorted_out)
     out = call(
         merge_kernel, [sds(TOKENS, HEADS * HD, dtype=BF16)], [back, o_s, lse_s, live]
     )

time: 149 us -> 141 us (0.946)
  the two profiles are of different devices: /device:TPU:32 before, /device:TPU:6 now
where the time goes in v5:
time: 141 us; the launch traced here: 140 us
  starting transfers between devices  94.7 us (67%)
  waiting for transfers between devices  24.5 us (17%)
  Pallas kernels  13 us (9%)
  local copies, waits for them, and re-layouts  5.93 us (4%)
    all_to_all x4, starting transfers between devices, exchange(): lax.all_to_all(a, 'prompt', 0, 0, tiled=True, axis_index_groups=[order])  63.2 us
    ppermute x12, starting transfers between devices, permute(): return lax.ppermute(a, 'tp', pairs)  31.4 us
    pallas_call x7, Pallas kernels, call(): pl.pallas_call(kernel, out_shape=tuple(outs) if many else outs[0], in_spe...  13 us
    all_to_all x4, waiting for transfers between devices, exchange(): lax.all_to_all(a, 'prompt', 0, 0, tiled=True, axis_index_groups=[order])  12.3 us
    ppermute x12, waiting for transfers between devices, permute(): return lax.ppermute(a, 'tp', pairs)  12.2 us
  transfers between devices with their start and end apart: 16, of which 6 were waited for; matrix products, arithmetic and copies ran while one was open for 3% of the time, Pallas kernels for 8%

profile of v5, /device:TPU:6, one launch (start us, length us, event | category | flops | bytes accessed | tf_op | source)
XLA Modules:
  0.0 139.8 jit_solution(13071000540403106021)
XLA Ops:
  0.0 0.7 pad_maximum_fusion.4
  0.8 1.3 dynamic-slice_bitcast_fusion
  2.2 4.0 %collective-permute-start.1 = (bf16[4,528,128]{2,1,0:T(8,128)(2,1)S(1)}, bf16[4,528,128]{2,1,0:T(8,128)(2,1)S(1)}, u32[]{:S(2)}, u32[]{:S(2)}) collective-permute-start(bf16[4,528,128]{2,1,0:T(8,128)(2,1)S(1)} %pad_maximum_fusion.1), channel_id=1, source_target_pairs={{0,2},{1,3},{2,0},{3,1},{4,6},{5,7},{6,4},{7,5},{8,10},{9,11},{10,... | collective-permute-start | bytes 1622024 | tf_op jit(solution)/shard_map/ppermute | solution.py:223
  6.2 0.7 copy.25
  6.9 19.9 %all-to-all-start = ((bf16[16,48,128]{2,1,0:T(8,128)(2,1)}), bf16[16,48,128]{2,1,0:T(8,128)(2,1)S(1)}, u32[]{:S(2)}, u32[]{:S(2)}) async-start(bf16[16,48,128]{2,1,0:T(8,128)(2,1)} %bitcast.1), calls=%async_computation | async-start | bytes 393216 | tf_op jit(solution)/shard_map/all_to_all | solution.py:201
  27.1 2.4 %collective-permute-start.2 = (bf16[2,528,128]{2,1,0:T(8,128)(2,1)S(1)}, bf16[2,528,128]{2,1,0:T(8,128)(2,1)S(1)}, u32[]{:S(2)}, u32[]{:S(2)}) collective-permute-start(bf16[2,528,128]{2,1,0:T(8,128)(2,1)S(1)} %get-tuple-element.20), channel_id=1, source_target_pairs={{0,8},{1,9},{2,10},{3,11},{4,12},{5,13},{6,14},{7,15},{8,16},{9,17... | collective-permute-start | bytes 811016 | tf_op jit(solution)/shard_map/ppermute | solution.py:223
  29.5 4.3 %collective-permute-start.3 = (bf16[2,528,128]{2,1,0:T(8,128)(2,1)S(1)}, bf16[2,528,128]{2,1,0:T(8,128)(2,1)S(1)}, u32[]{:S(2)}, u32[]{:S(2)}) collective-permute-start(bf16[2,528,128]{2,1,0:T(8,128)(2,1)S(1)} %get-tuple-element.21), channel_id=1, source_target_pairs={{0,16},{1,17},{2,18},{3,19},{4,20},{5,21},{6,22},{7,23},{8,24},{9,... | collective-permute-start | bytes 811016 | tf_op jit(solution)/shard_map/ppermute | solution.py:223
  33.8 1.9 %collective-permute-start.4 = (bf16[2,528,128]{2,1,0:T(8,128)(2,1)S(1)}, bf16[2,528,128]{2,1,0:T(8,128)(2,1)S(1)}, u32[]{:S(2)}, u32[]{:S(2)}) collective-permute-start(bf16[2,528,128]{2,1,0:T(8,128)(2,1)S(1)} %get-tuple-element.22), channel_id=1, source_target_pairs={{0,24},{1,25},{2,26},{3,27},{4,28},{5,29},{6,30},{7,31},{8,0},{9,1... | collective-permute-start | bytes 811016 | tf_op jit(solution)/shard_map/ppermute | solution.py:223
  35.9 3.9 %all-to-all-done = bf16[16,48,128]{2,1,0:T(8,128)(2,1)S(1)} async-done(((bf16[16,48,128]{2,1,0:T(8,128)(2,1)}), bf16[16,48,128]{2,1,0:T(8,128)(2,1)S(1)}, u32[]{:S(2)}, u32[]{:S(2)}) %all-to-all-start) | async-done | bytes 196640 | tf_op jit(solution)/shard_map/all_to_all | solution.py:201
  39.8 1.2 gather_fusion
  41.0 14.4 %all-to-all-start.1 = ((bf16[16,48,128]{2,1,0:T(8,128)(2,1)}), bf16[16,48,128]{2,1,0:T(8,128)(2,1)S(1)}, u32[]{:S(2)}, u32[]{:S(2)}) async-start(bf16[16,48,128]{2,1,0:T(8,128)(2,1)} %gather_fusion), calls=%async_computation.1 | async-start | bytes 393216 | tf_op jit(solution)/shard_map/all_to_all | solution.py:201
  55.6 1.9 %collective-permute-start.6 = (bf16[2176,128]{1,0:T(8,128)(2,1)S(1)}, bf16[2176,128]{1,0:T(8,128)(2,1)S(1)}, u32[]{:S(2)}, u32[]{:S(2)}) collective-permute-start(bf16[2176,128]{1,0:T(8,128)(2,1)S(1)} %get-tuple-element.24.v_a), channel_id=1, source_target_pairs={{0,1},{1,0},{2,3},{3,2},{4,5},{5,4},{6,7},{7,6},{8,9},{9,8},{10,11... | collective-permute-start | bytes 1671176 | tf_op jit(solution)/shard_map/ppermute | solution.py:223
  57.5 2.4 %collective-permute-start.5 = (bf16[2048,128]{1,0:T(8,128)(2,1)S(1)}, bf16[2048,128]{1,0:T(8,128)(2,1)S(1)}, u32[]{:S(2)}, u32[]{:S(2)}) collective-permute-start(bf16[2048,128]{1,0:T(8,128)(2,1)S(1)} %get-tuple-element.23.k_a), channel_id=1, source_target_pairs={{0,1},{1,0},{2,3},{3,2},{4,5},{5,4},{6,7},{7,6},{8,9},{9,8},{10,11... | collective-permute-start | bytes 1572872 | tf_op jit(solution)/shard_map/ppermute | solution.py:223
  59.9 2.3 %all-to-all-done.1 = bf16[16,48,128]{2,1,0:T(8,128)(2,1)S(1)} async-done(((bf16[16,48,128]{2,1,0:T(8,128)(2,1)}), bf16[16,48,128]{2,1,0:T(8,128)(2,1)S(1)}, u32[]{:S(2)}, u32[]{:S(2)}) %all-to-all-start.1) | async-done | bytes 196640 | tf_op jit(solution)/shard_map/all_to_all | solution.py:201
  62.2 3.5 %collective-permute-start.8 = (bf16[768,128]{1,0:T(8,128)(2,1)S(1)}, bf16[768,128]{1,0:T(8,128)(2,1)S(1)}, u32[]{:S(2)}, u32[]{:S(2)}) collective-permute-start(bf16[768,128]{1,0:T(8,128)(2,1)S(1)} %bitcast.55), channel_id=1, source_target_pairs={{0,4},{1,5},{2,0},{3,1},{4,6},{5,7},{6,2},{7,3},{8,12},{9,13},{10,... | collective-permute-start | bytes 589832 | tf_op jit(solution)/shard_map/ppermute | solution.py:223
  65.7 0.7 collective-permute-start
  66.4 3.4 %collective-permute-done.8.q_ref = bf16[768,128]{1,0:T(8,128)(2,1)S(1)} collective-permute-done((bf16[768,128]{1,0:T(8,128)(2,1)S(1)}, bf16[768,128]{1,0:T(8,128)(2,1)S(1)}, u32[]{:S(2)}, u32[]{:S(2)}) %collective-permute-start.8) | collective-permute-done | bytes 196640 | tf_op jit(solution)/shard_map/ppermute | solution.py:223
  69.7 4.5 %shard_map.76 = f32[776,128]{1,0:T(8,128)S(1)} custom-call(bf16[768,128]{1,0:T(8,128)(2,1)S(1)} %collective-permute-done.8.q_ref, bf16[2048,128]{1,0:T(8,128)(2,1)S(1)} %get-tuple-element.23.k_a, bf16[2176,128]{1,0:T(8,128)(2,1)S(1)} %get-tuple-element.24.v_a, bf16[2048,128]{1,0:T(8,128)(2,1)S(1)} %collective-permute-done.5.k_b, ...), custom_call_target="tpu_custom_call" | custom-call | flops 1610612736 | bytes 2756608 | tf_op jit(solution)/shard_map/pallas_call | solution.py:184
  74.3 3.5 %collective-permute-start.9 = (f32[776,128]{1,0:T(8,128)S(1)}, f32[776,128]{1,0:T(8,128)S(1)}, u32[]{:S(2)}, u32[]{:S(2)}) collective-permute-start(f32[776,128]{1,0:T(8,128)S(1)} %shard_map.76), channel_id=1, source_target_pairs={{0,2},{1,3},{2,6},{3,7},{4,0},{5,1},{6,4},{7,5},{8,10},{9,11},{10,... | collective-permute-start | bytes 1191944 | tf_op jit(solution)/shard_map/ppermute | solution.py:223
  77.7 4.6 %shard_map.75 = bf16[800,128]{1,0:T(8,128)(2,1)S(1)} custom-call(bf16[768,128]{1,0:T(8,128)(2,1)S(1)} %collective-permute-done.q_ref, bf16[2048,128]{1,0:T(8,128)(2,1)S(1)} %get-tuple-element.23.k_a, bf16[2176,128]{1,0:T(8,128)(2,1)S(1)} %get-tuple-element.24.v_a, bf16[2048,128]{1,0:T(8,128)(2,1)S(1)} %collective-permute-done.5.k_b, ...), custom_call_target="tpu_custom_call" | custom-call | flops 1610612736 | bytes 2564096 | tf_op jit(solution)/shard_map/pallas_call | solution.py:184
  82.3 0.9 collective-permute-start.7
  83.6 5.0 %collective-permute-done.9.b_ref = f32[776,128]{1,0:T(8,128)S(1)} collective-permute-done((f32[776,128]{1,0:T(8,128)S(1)}, f32[776,128]{1,0:T(8,128)S(1)}, u32[]{:S(2)}, u32[]{:S(2)}) %collective-permute-start.9) | collective-permute-done | bytes 397344 | tf_op jit(solution)/shard_map/ppermute | solution.py:223
  88.6 1.1 shard_map.77
  89.7 14.4 %all-to-all-start.2 = ((bf16[16,56,128]{2,1,0:T(8,128)(2,1)}), bf16[16,56,128]{2,1,0:T(8,128)(2,1)S(1)}, u32[]{:S(2)}, u32[]{:S(2)}) async-start(bf16[16,56,128]{2,1,0:T(8,128)(2,1)} %shard_map.77), calls=%async_computation.2 | async-start | bytes 458752 | tf_op jit(solution)/shard_map/all_to_all | solution.py:201
  104.4 5.4 %collective-permute-start.11 = (bf16[2,8,16,128]{3,2,1,0:T(8,128)(2,1)S(1)}, bf16[2,8,16,128]{3,2,1,0:T(8,128)(2,1)S(1)}, u32[]{:S(2)}, u32[]{:S(2)}) collective-permute-start(bf16[2,8,16,128]{3,2,1,0:T(8,128)(2,1)S(1)} %pad_maximum_fusion.3), channel_id=1, source_target_pairs={{0,2},{1,3},{2,6},{3,7},{4,0},{5,1},{6,4},{7,5},{8,10},{9,11},{10,... | collective-permute-start | bytes 196616 | tf_op jit(solution)/shard_map/ppermute | solution.py:223
  109.7 0.7 collective-permute-start.10
  110.4 3.8 %collective-permute-done.11 = bf16[2,8,16,128]{3,2,1,0:T(8,128)(2,1)S(1)} collective-permute-done((bf16[2,8,16,128]{3,2,1,0:T(8,128)(2,1)S(1)}, bf16[2,8,16,128]{3,2,1,0:T(8,128)(2,1)S(1)}, u32[]{:S(2)}, u32[]{:S(2)}) %collective-permute-start.11) | collective-permute-done | bytes 65568 | tf_op jit(solution)/shard_map/ppermute | solution.py:223
  114.2 1.3 gather_fusion.1
  115.5 14.4 %all-to-all-start.3 = ((bf16[16,56,128]{2,1,0:T(8,128)(2,1)}), bf16[16,56,128]{2,1,0:T(8,128)(2,1)S(1)}, u32[]{:S(2)}, u32[]{:S(2)}) async-start(bf16[16,56,128]{2,1,0:T(8,128)(2,1)} %gather_fusion.1), calls=%async_computation.3 | async-start | bytes 458752 | tf_op jit(solution)/shard_map/all_to_all | solution.py:201
  130.8 1.7 %shard_map.78 = (f32[768,128]{1,0:T(8,128)S(1)}, f32[768,128]{1,0:T(8,128)S(1)}) custom-call(bf16[768,128]{1,0:T(8,128)(2,1)} %bitcast.25.q_ref, bf16[192,128]{1,0:T(8,128)(2,1)S(1)} %reshape.239.k_ref, bf16[192,128]{1,0:T(8,128)(2,1)S(1)} %reshape.240.v_ref, s32[192,192]{1,0:T(8,128)S(1)} %broadcast_in_dim.40.step_ref, ...), custom_call_target="tpu_custom_call" | custom-call | flops 75497472 | bytes 1376256 | tf_op jit(solution)/shard_map/pallas_call | solution.py:184
  132.6 6.2 %all-to-all-done.3.r_ref = bf16[16,56,128]{2,1,0:T(8,128)(2,1)S(1)} async-done(((bf16[16,56,128]{2,1,0:T(8,128)(2,1)}), bf16[16,56,128]{2,1,0:T(8,128)(2,1)S(1)}, u32[]{:S(2)}, u32[]{:S(2)}) %all-to-all-start.3) | async-done | bytes 229408 | tf_op jit(solution)/shard_map/all_to_all | solution.py:201
  138.8 1.0 shard_map.79
  (59 shorter events, 2.1 us)
Async XLA Ops:
  2.1 4.0 %copy-start = (bf16[1,3,64,512]{3,2,1,0:T(8,128)(2,1)S(1)}, bf16[1,3,64,512]{3,2,1,0:T(8,128)(2,1)}, u32[]{:S(2)}) copy-start(bf16[1,3,64,512]{3,2,1,0:T(8,128)(2,1)} %param.9) | copy-start | bytes 589828
  2.1 24.7 %copy-start.2 = (s32[16]{0:T(128)S(1)}, s32[16]{0:T(128)}, u32[]{:S(2)}) copy-start(s32[16]{0:T(128)} %param.13) | copy-start | bytes 196
  2.2 24.9 %collective-permute-start.1 = (bf16[4,528,128]{2,1,0:T(8,128)(2,1)S(1)}, bf16[4,528,128]{2,1,0:T(8,128)(2,1)S(1)}, u32[]{:S(2)}, u32[]{:S(2)}) collective-permute-start(bf16[4,528,128]{2,1,0:T(8,128)(2,1)S(1)} %pad_maximum_fusion.1), channel_id=1, source_target_pairs={{0,2},{1,3},{2,0},{3,1},{4,6},{5,7},{6,4},{7,5},{8,10},{9,11},{10,... | collective-permute-start | bytes 1622024 | tf_op jit(solution)/shard_map/ppermute | solution.py:223
  6.9 32.9 %all-to-all-start = ((bf16[16,48,128]{2,1,0:T(8,128)(2,1)}), bf16[16,48,128]{2,1,0:T(8,128)(2,1)S(1)}, u32[]{:S(2)}, u32[]{:S(2)}) async-start(bf16[16,48,128]{2,1,0:T(8,128)(2,1)} %bitcast.1), calls=%async_computation | async-start | bytes 393216 | tf_op jit(solution)/shard_map/all_to_all | solution.py:201
  27.1 28.4 %collective-permute-start.2 = (bf16[2,528,128]{2,1,0:T(8,128)(2,1)S(1)}, bf16[2,528,128]{2,1,0:T(8,128)(2,1)S(1)}, u32[]{:S(2)}, u32[]{:S(2)}) collective-permute-start(bf16[2,528,128]{2,1,0:T(8,128)(2,1)S(1)} %get-tuple-element.20), channel_id=1, source_target_pairs={{0,8},{1,9},{2,10},{3,11},{4,12},{5,13},{6,14},{7,15},{8,16},{9,17... | collective-permute-start | bytes 811016 | tf_op jit(solution)/shard_map/ppermute | solution.py:223
  29.5 26.0 %collective-permute-start.3 = (bf16[2,528,128]{2,1,0:T(8,128)(2,1)S(1)}, bf16[2,528,128]{2,1,0:T(8,128)(2,1)S(1)}, u32[]{:S(2)}, u32[]{:S(2)}) collective-permute-start(bf16[2,528,128]{2,1,0:T(8,128)(2,1)S(1)} %get-tuple-element.21), channel_id=1, source_target_pairs={{0,16},{1,17},{2,18},{3,19},{4,20},{5,21},{6,22},{7,23},{8,24},{9,... | collective-permute-start | bytes 811016 | tf_op jit(solution)/shard_map/ppermute | solution.py:223
  33.8 21.7 %collective-permute-start.4 = (bf16[2,528,128]{2,1,0:T(8,128)(2,1)S(1)}, bf16[2,528,128]{2,1,0:T(8,128)(2,1)S(1)}, u32[]{:S(2)}, u32[]{:S(2)}) collective-permute-start(bf16[2,528,128]{2,1,0:T(8,128)(2,1)S(1)} %get-tuple-element.22), channel_id=1, source_target_pairs={{0,24},{1,25},{2,26},{3,27},{4,28},{5,29},{6,30},{7,31},{8,0},{9,1... | collective-permute-start | bytes 811016 | tf_op jit(solution)/shard_map/ppermute | solution.py:223
  41.0 21.1 %all-to-all-start.1 = ((bf16[16,48,128]{2,1,0:T(8,128)(2,1)}), bf16[16,48,128]{2,1,0:T(8,128)(2,1)S(1)}, u32[]{:S(2)}, u32[]{:S(2)}) async-start(bf16[16,48,128]{2,1,0:T(8,128)(2,1)} %gather_fusion), calls=%async_computation.1 | async-start | bytes 393216 | tf_op jit(solution)/shard_map/all_to_all | solution.py:201
  55.6 10.8 %collective-permute-start.6 = (bf16[2176,128]{1,0:T(8,128)(2,1)S(1)}, bf16[2176,128]{1,0:T(8,128)(2,1)S(1)}, u32[]{:S(2)}, u32[]{:S(2)}) collective-permute-start(bf16[2176,128]{1,0:T(8,128)(2,1)S(1)} %get-tuple-element.24.v_a), channel_id=1, source_target_pairs={{0,1},{1,0},{2,3},{3,2},{4,5},{5,4},{6,7},{7,6},{8,9},{9,8},{10,11... | collective-permute-start | bytes 1671176 | tf_op jit(solution)/shard_map/ppermute | solution.py:223
  57.5 8.9 %collective-permute-start.5 = (bf16[2048,128]{1,0:T(8,128)(2,1)S(1)}, bf16[2048,128]{1,0:T(8,128)(2,1)S(1)}, u32[]{:S(2)}, u32[]{:S(2)}) collective-permute-start(bf16[2048,128]{1,0:T(8,128)(2,1)S(1)} %get-tuple-element.23.k_a), channel_id=1, source_target_pairs={{0,1},{1,0},{2,3},{3,2},{4,5},{5,4},{6,7},{7,6},{8,9},{9,8},{10,11... | collective-permute-start | bytes 1572872 | tf_op jit(solution)/shard_map/ppermute | solution.py:223
  62.2 7.6 %collective-permute-start.8 = (bf16[768,128]{1,0:T(8,128)(2,1)S(1)}, bf16[768,128]{1,0:T(8,128)(2,1)S(1)}, u32[]{:S(2)}, u32[]{:S(2)}) collective-permute-start(bf16[768,128]{1,0:T(8,128)(2,1)S(1)} %bitcast.55), channel_id=1, source_target_pairs={{0,4},{1,5},{2,0},{3,1},{4,6},{5,7},{6,2},{7,3},{8,12},{9,13},{10,... | collective-permute-start | bytes 589832 | tf_op jit(solution)/shard_map/ppermute | solution.py:223
  65.7 12.1 %collective-permute-start = (bf16[768,128]{1,0:T(8,128)(2,1)S(1)}, bf16[768,128]{1,0:T(8,128)(2,1)S(1)}, u32[]{:S(2)}, u32[]{:S(2)}) collective-permute-start(bf16[768,128]{1,0:T(8,128)(2,1)S(1)} %bitcast.56), channel_id=1, source_target_pairs={{0,0},{1,1},{2,4},{3,5},{4,2},{5,3},{6,6},{7,7},{8,8},{9,9},{10,12... | collective-permute-start | bytes 589832 | tf_op jit(solution)/shard_map/ppermute | solution.py:223
  74.3 14.4 %collective-permute-start.9 = (f32[776,128]{1,0:T(8,128)S(1)}, f32[776,128]{1,0:T(8,128)S(1)}, u32[]{:S(2)}, u32[]{:S(2)}) collective-permute-start(f32[776,128]{1,0:T(8,128)S(1)} %shard_map.76), channel_id=1, source_target_pairs={{0,2},{1,3},{2,6},{3,7},{4,0},{5,1},{6,4},{7,5},{8,10},{9,11},{10,... | collective-permute-start | bytes 1191944 | tf_op jit(solution)/shard_map/ppermute | solution.py:223
  82.3 1.3 collective-permute-start.7
  89.7 24.6 %all-to-all-start.2 = ((bf16[16,56,128]{2,1,0:T(8,128)(2,1)}), bf16[16,56,128]{2,1,0:T(8,128)(2,1)S(1)}, u32[]{:S(2)}, u32[]{:S(2)}) async-start(bf16[16,56,128]{2,1,0:T(8,128)(2,1)} %shard_map.77), calls=%async_computation.2 | async-start | bytes 458752 | tf_op jit(solution)/shard_map/all_to_all | solution.py:201
  104.4 9.8 %collective-permute-start.11 = (bf16[2,8,16,128]{3,2,1,0:T(8,128)(2,1)S(1)}, bf16[2,8,16,128]{3,2,1,0:T(8,128)(2,1)S(1)}, u32[]{:S(2)}, u32[]{:S(2)}) collective-permute-start(bf16[2,8,16,128]{3,2,1,0:T(8,128)(2,1)S(1)} %pad_maximum_fusion.3), channel_id=1, source_target_pairs={{0,2},{1,3},{2,6},{3,7},{4,0},{5,1},{6,4},{7,5},{8,10},{9,11},{10,... | collective-permute-start | bytes 196616 | tf_op jit(solution)/shard_map/ppermute | solution.py:223
  109.7 4.5 %collective-permute-start.10 = (bf16[2,8,16,128]{3,2,1,0:T(8,128)(2,1)S(1)}, bf16[2,8,16,128]{3,2,1,0:T(8,128)(2,1)S(1)}, u32[]{:S(2)}, u32[]{:S(2)}) collective-permute-start(bf16[2,8,16,128]{3,2,1,0:T(8,128)(2,1)S(1)} %pad_maximum_fusion.3), channel_id=1, source_target_pairs={{0,0},{1,1},{2,4},{3,5},{4,2},{5,3},{6,6},{7,7},{8,8},{9,9},{10,12... | collective-permute-start | bytes 196616 | tf_op jit(solution)/shard_map/ppermute | solution.py:223
  114.2 16.3 %copy-start.1 = (s32[1,64]{1,0:T(1,128)S(1)}, s32[1,64]{1,0:T(1,128)}, u32[]{:S(2)}) copy-start(s32[1,64]{1,0:T(1,128)} %param.12) | copy-start | bytes 772
  115.5 23.2 %all-to-all-start.3 = ((bf16[16,56,128]{2,1,0:T(8,128)(2,1)}), bf16[16,56,128]{2,1,0:T(8,128)(2,1)S(1)}, u32[]{:S(2)}, u32[]{:S(2)}) async-start(bf16[16,56,128]{2,1,0:T(8,128)(2,1)} %gather_fusion.1), calls=%async_computation.3 | async-start | bytes 458752 | tf_op jit(solution)/shard_map/all_to_all | solution.py:201

commit v6 on v5

--- a/solution.py
+++ b/solution.py
@@ -133,6 +133,9 @@
     out_ref[pl.ds(0, ROWS)] = o.astype(out_ref.dtype)
     lse_sc[...] = jnp.broadcast_to(lse, (ROWS, LANES))
     store_lines(out_ref, [to_line(lse_sc[unit(u)]) for u in range(UNITS)])
+    if out_ref.shape[0] > PACKED:
+        for n, v in enumerate((v_a, v_b)):
+            out_ref[pl.ds(PACKED + n * 8 * SUF, 8 * SUF)] = v[pl.ds(HALF, 8 * SUF)]
 
 
 def join(o1, lse1, o2, lse2):
@@ -278,8 +281,8 @@
     wide = pltpu.VMEM((ROWS, HD), F32)
     partial = []
     for there, back, kind, size in (
+        (there_1, back_1, BF16, PACKED + 16 * SUF),
         (there_0, there_0, BF16, PACKED),
-        (there_1, back_1, F32, PACKED_WIDE),
     ):
         part = call(
             attend_kernel,
@@ -295,7 +298,7 @@
 
     tail = jnp.stack([e[1][HALF:].reshape(8, SUF, HD) for e in (mine, far)])
     done, tail = lax.optimization_barrier((done, tail))
-    tail = jnp.stack([permute(tail, there_0), permute(tail, back_1)])
+    tail = jnp.stack([permute(tail, there_0), partial[0][PACKED:].reshape(tail.shape)])
     live = jnp.arange(STEPS, dtype=jnp.int32)[:, None] < suffix_lengths[0][None, :]
     live = jnp.broadcast_to(live.reshape(TOKENS, 1), (TOKENS, HD)).astype(jnp.int32)
 

time: 141 us -> 136 us (0.965)
  the two profiles are of different devices: /device:TPU:6 before, /device:TPU:56 now
where the time goes in v6:
time: 136 us; the launch traced here: 135 us
  starting transfers between devices  94.8 us (70%)
  waiting for transfers between devices  19.9 us (15%)
  Pallas kernels  13 us (10%)
  local copies, waits for them, and re-layouts  5.92 us (4%)
    all_to_all x4, starting transfers between devices, exchange(): lax.all_to_all(a, 'prompt', 0, 0, tiled=True, axis_index_groups=[order])  62.8 us
    ppermute x11, starting transfers between devices, permute(): return lax.ppermute(a, 'tp', pairs)  32 us
    pallas_call x7, Pallas kernels, call(): pl.pallas_call(kernel, out_shape=tuple(outs) if many else outs[0], in_spe...  13 us
    ppermute x11, waiting for transfers between devices, permute(): return lax.ppermute(a, 'tp', pairs)  10.7 us
    all_to_all x4, waiting for transfers between devices, exchange(): lax.all_to_all(a, 'prompt', 0, 0, tiled=True, axis_index_groups=[order])  9.16 us
  transfers between devices with their start and end apart: 15, of which 6 were waited for; matrix products, arithmetic and copies ran while one was open for 3% of the time, Pallas kernels for 8%

profile of v6, /device:TPU:56, one launch (start us, length us, event | category | flops | bytes accessed | tf_op | source)
XLA Modules:
  0.0 135.3 jit_solution(16730456334305662333)
XLA Ops:
  0.0 0.7 pad_maximum_fusion.4
  0.8 1.3 dynamic-slice_bitcast_fusion
  2.1 2.1 %collective-permute-start.1 = (bf16[4,528,128]{2,1,0:T(8,128)(2,1)S(1)}, bf16[4,528,128]{2,1,0:T(8,128)(2,1)S(1)}, u32[]{:S(2)}, u32[]{:S(2)}) collective-permute-start(bf16[4,528,128]{2,1,0:T(8,128)(2,1)S(1)} %pad_maximum_fusion.1), channel_id=1, source_target_pairs={{0,2},{1,3},{2,0},{3,1},{4,6},{5,7},{6,4},{7,5},{8,10},{9,11},{10,... | collective-permute-start | bytes 1622024 | tf_op jit(solution)/shard_map/ppermute | solution.py:226
  4.4 0.7 copy.25
  5.1 18.4 %all-to-all-start = ((bf16[16,48,128]{2,1,0:T(8,128)(2,1)}), bf16[16,48,128]{2,1,0:T(8,128)(2,1)S(1)}, u32[]{:S(2)}, u32[]{:S(2)}) async-start(bf16[16,48,128]{2,1,0:T(8,128)(2,1)} %bitcast.1), calls=%async_computation | async-start | bytes 393216 | tf_op jit(solution)/shard_map/all_to_all | solution.py:204
  23.7 3.4 %collective-permute-start.2 = (bf16[2,528,128]{2,1,0:T(8,128)(2,1)S(1)}, bf16[2,528,128]{2,1,0:T(8,128)(2,1)S(1)}, u32[]{:S(2)}, u32[]{:S(2)}) collective-permute-start(bf16[2,528,128]{2,1,0:T(8,128)(2,1)S(1)} %get-tuple-element.20), channel_id=1, source_target_pairs={{0,8},{1,9},{2,10},{3,11},{4,12},{5,13},{6,14},{7,15},{8,16},{9,17... | collective-permute-start | bytes 811016 | tf_op jit(solution)/shard_map/ppermute | solution.py:226
  27.1 4.6 %collective-permute-start.3 = (bf16[2,528,128]{2,1,0:T(8,128)(2,1)S(1)}, bf16[2,528,128]{2,1,0:T(8,128)(2,1)S(1)}, u32[]{:S(2)}, u32[]{:S(2)}) collective-permute-start(bf16[2,528,128]{2,1,0:T(8,128)(2,1)S(1)} %get-tuple-element.21), channel_id=1, source_target_pairs={{0,16},{1,17},{2,18},{3,19},{4,20},{5,21},{6,22},{7,23},{8,24},{9,... | collective-permute-start | bytes 811016 | tf_op jit(solution)/shard_map/ppermute | solution.py:226
  31.8 3.3 %collective-permute-start.4 = (bf16[2,528,128]{2,1,0:T(8,128)(2,1)S(1)}, bf16[2,528,128]{2,1,0:T(8,128)(2,1)S(1)}, u32[]{:S(2)}, u32[]{:S(2)}) collective-permute-start(bf16[2,528,128]{2,1,0:T(8,128)(2,1)S(1)} %get-tuple-element.22), channel_id=1, source_target_pairs={{0,24},{1,25},{2,26},{3,27},{4,28},{5,29},{6,30},{7,31},{8,0},{9,1... | collective-permute-start | bytes 811016 | tf_op jit(solution)/shard_map/ppermute | solution.py:226
  35.3 1.7 %all-to-all-done = bf16[16,48,128]{2,1,0:T(8,128)(2,1)S(1)} async-done(((bf16[16,48,128]{2,1,0:T(8,128)(2,1)}), bf16[16,48,128]{2,1,0:T(8,128)(2,1)S(1)}, u32[]{:S(2)}, u32[]{:S(2)}) %all-to-all-start) | async-done | bytes 196640 | tf_op jit(solution)/shard_map/all_to_all | solution.py:204
  37.0 1.2 gather_fusion
  38.2 14.7 %all-to-all-start.1 = ((bf16[16,48,128]{2,1,0:T(8,128)(2,1)}), bf16[16,48,128]{2,1,0:T(8,128)(2,1)S(1)}, u32[]{:S(2)}, u32[]{:S(2)}) async-start(bf16[16,48,128]{2,1,0:T(8,128)(2,1)} %gather_fusion), calls=%async_computation.1 | async-start | bytes 393216 | tf_op jit(solution)/shard_map/all_to_all | solution.py:204
  53.0 1.9 %collective-permute-start.6 = (bf16[2176,128]{1,0:T(8,128)(2,1)S(1)}, bf16[2176,128]{1,0:T(8,128)(2,1)S(1)}, u32[]{:S(2)}, u32[]{:S(2)}) collective-permute-start(bf16[2176,128]{1,0:T(8,128)(2,1)S(1)} %get-tuple-element.24.v_a), channel_id=1, source_target_pairs={{0,1},{1,0},{2,3},{3,2},{4,5},{5,4},{6,7},{7,6},{8,9},{9,8},{10,11... | collective-permute-start | bytes 1671176 | tf_op jit(solution)/shard_map/ppermute | solution.py:226
  54.9 2.4 %collective-permute-start.5 = (bf16[2048,128]{1,0:T(8,128)(2,1)S(1)}, bf16[2048,128]{1,0:T(8,128)(2,1)S(1)}, u32[]{:S(2)}, u32[]{:S(2)}) collective-permute-start(bf16[2048,128]{1,0:T(8,128)(2,1)S(1)} %get-tuple-element.23.k_a), channel_id=1, source_target_pairs={{0,1},{1,0},{2,3},{3,2},{4,5},{5,4},{6,7},{7,6},{8,9},{9,8},{10,11... | collective-permute-start | bytes 1572872 | tf_op jit(solution)/shard_map/ppermute | solution.py:226
  57.4 3.2 %all-to-all-done.1 = bf16[16,48,128]{2,1,0:T(8,128)(2,1)S(1)} async-done(((bf16[16,48,128]{2,1,0:T(8,128)(2,1)}), bf16[16,48,128]{2,1,0:T(8,128)(2,1)S(1)}, u32[]{:S(2)}, u32[]{:S(2)}) %all-to-all-start.1) | async-done | bytes 196640 | tf_op jit(solution)/shard_map/all_to_all | solution.py:204
  60.5 2.4 %collective-permute-start = (bf16[768,128]{1,0:T(8,128)(2,1)S(1)}, bf16[768,128]{1,0:T(8,128)(2,1)S(1)}, u32[]{:S(2)}, u32[]{:S(2)}) collective-permute-start(bf16[768,128]{1,0:T(8,128)(2,1)S(1)} %bitcast.56), channel_id=1, source_target_pairs={{0,4},{1,5},{2,0},{3,1},{4,6},{5,7},{6,2},{7,3},{8,12},{9,13},{10,... | collective-permute-start | bytes 589832 | tf_op jit(solution)/shard_map/ppermute | solution.py:226
  63.0 3.7 %collective-permute-start.8 = (bf16[768,128]{1,0:T(8,128)(2,1)S(1)}, bf16[768,128]{1,0:T(8,128)(2,1)S(1)}, u32[]{:S(2)}, u32[]{:S(2)}) collective-permute-start(bf16[768,128]{1,0:T(8,128)(2,1)S(1)} %bitcast.57), channel_id=1, source_target_pairs={{0,0},{1,1},{2,4},{3,5},{4,2},{5,3},{6,6},{7,7},{8,8},{9,9},{10,12... | collective-permute-start | bytes 589832 | tf_op jit(solution)/shard_map/ppermute | solution.py:226
  66.7 2.4 %collective-permute-done.q_ref = bf16[768,128]{1,0:T(8,128)(2,1)S(1)} collective-permute-done((bf16[768,128]{1,0:T(8,128)(2,1)S(1)}, bf16[768,128]{1,0:T(8,128)(2,1)S(1)}, u32[]{:S(2)}, u32[]{:S(2)}) %collective-permute-start) | collective-permute-done | bytes 196640 | tf_op jit(solution)/shard_map/ppermute | solution.py:226
  69.1 4.5 %shard_map.75 = bf16[1056,128]{1,0:T(8,128)(2,1)S(1)} custom-call(bf16[768,128]{1,0:T(8,128)(2,1)S(1)} %collective-permute-done.q_ref, bf16[2048,128]{1,0:T(8,128)(2,1)S(1)} %get-tuple-element.23.k_a, bf16[2176,128]{1,0:T(8,128)(2,1)S(1)} %get-tuple-element.24.v_a, bf16[2048,128]{1,0:T(8,128)(2,1)S(1)} %collective-permute-done.5.k_b, ...), custom_call_target="tpu_custom_call" | custom-call | flops 1610612736 | bytes 2629632 | tf_op jit(solution)/shard_map/pallas_call | solution.py:187
  73.6 2.7 %collective-permute-start.7 = (bf16[1056,128]{1,0:T(8,128)(2,1)S(1)}, bf16[1056,128]{1,0:T(8,128)(2,1)S(1)}, u32[]{:S(2)}, u32[]{:S(2)}) collective-permute-start(bf16[1056,128]{1,0:T(8,128)(2,1)S(1)} %shard_map.75), channel_id=1, source_target_pairs={{0,2},{1,3},{2,6},{3,7},{4,0},{5,1},{6,4},{7,5},{8,10},{9,11},{10,... | collective-permute-start | bytes 811016 | tf_op jit(solution)/shard_map/ppermute | solution.py:226
  76.3 4.5 %shard_map.76 = bf16[800,128]{1,0:T(8,128)(2,1)S(1)} custom-call(bf16[768,128]{1,0:T(8,128)(2,1)S(1)} %collective-permute-done.8.q_ref, bf16[2048,128]{1,0:T(8,128)(2,1)S(1)} %get-tuple-element.23.k_a, bf16[2176,128]{1,0:T(8,128)(2,1)S(1)} %get-tuple-element.24.v_a, bf16[2048,128]{1,0:T(8,128)(2,1)S(1)} %collective-permute-done.5.k_b, ...), custom_call_target="tpu_custom_call" | custom-call | flops 1610612736 | bytes 2564096 | tf_op jit(solution)/shard_map/pallas_call | solution.py:187
  80.8 3.5 %collective-permute-start.9 = (bf16[800,128]{1,0:T(8,128)(2,1)S(1)}, bf16[800,128]{1,0:T(8,128)(2,1)S(1)}, u32[]{:S(2)}, u32[]{:S(2)}) collective-permute-start(bf16[800,128]{1,0:T(8,128)(2,1)S(1)} %shard_map.76), channel_id=1, source_target_pairs={{0,0},{1,1},{2,4},{3,5},{4,2},{5,3},{6,6},{7,7},{8,8},{9,9},{10,12... | collective-permute-start | bytes 614408 | tf_op jit(solution)/shard_map/ppermute | solution.py:226
  84.4 4.1 %collective-permute-done.9.b_ref = bf16[800,128]{1,0:T(8,128)(2,1)S(1)} collective-permute-done((bf16[800,128]{1,0:T(8,128)(2,1)S(1)}, bf16[800,128]{1,0:T(8,128)(2,1)S(1)}, u32[]{:S(2)}, u32[]{:S(2)}) %collective-permute-start.9) | collective-permute-done | bytes 204832 | tf_op jit(solution)/shard_map/ppermute | solution.py:226
  88.5 1.1 shard_map.77
  89.6 15.2 %all-to-all-start.2 = ((bf16[16,56,128]{2,1,0:T(8,128)(2,1)}), bf16[16,56,128]{2,1,0:T(8,128)(2,1)S(1)}, u32[]{:S(2)}, u32[]{:S(2)}) async-start(bf16[16,56,128]{2,1,0:T(8,128)(2,1)} %shard_map.77), calls=%async_computation.2 | async-start | bytes 458752 | tf_op jit(solution)/shard_map/all_to_all | solution.py:204
  105.2 1.9 %collective-permute-start.10 = (bf16[2,8,16,128]{3,2,1,0:T(8,128)(2,1)S(1)}, bf16[2,8,16,128]{3,2,1,0:T(8,128)(2,1)S(1)}, u32[]{:S(2)}, u32[]{:S(2)}) collective-permute-start(bf16[2,8,16,128]{3,2,1,0:T(8,128)(2,1)S(1)} %pad_maximum_fusion.3), channel_id=1, source_target_pairs={{0,0},{1,1},{2,4},{3,5},{4,2},{5,3},{6,6},{7,7},{8,8},{9,9},{10,12... | collective-permute-start | bytes 196616 | tf_op jit(solution)/shard_map/ppermute | solution.py:226
  107.1 4.2 %collective-permute-done.10 = bf16[2,8,16,128]{3,2,1,0:T(8,128)(2,1)S(1)} collective-permute-done((bf16[2,8,16,128]{3,2,1,0:T(8,128)(2,1)S(1)}, bf16[2,8,16,128]{3,2,1,0:T(8,128)(2,1)S(1)}, u32[]{:S(2)}, u32[]{:S(2)}) %collective-permute-start.10) | collective-permute-done | bytes 65568 | tf_op jit(solution)/shard_map/ppermute | solution.py:226
  111.3 1.3 gather_fusion.1
  112.6 14.5 %all-to-all-start.3 = ((bf16[16,56,128]{2,1,0:T(8,128)(2,1)}), bf16[16,56,128]{2,1,0:T(8,128)(2,1)S(1)}, u32[]{:S(2)}, u32[]{:S(2)}) async-start(bf16[16,56,128]{2,1,0:T(8,128)(2,1)} %gather_fusion.1), calls=%async_computation.3 | async-start | bytes 458752 | tf_op jit(solution)/shard_map/all_to_all | solution.py:204
  127.5 0.1 iota.57
  128.2 1.7 %shard_map.78 = (f32[768,128]{1,0:T(8,128)S(1)}, f32[768,128]{1,0:T(8,128)S(1)}) custom-call(bf16[768,128]{1,0:T(8,128)(2,1)} %bitcast.25.q_ref, bf16[192,128]{1,0:T(8,128)(2,1)S(1)} %reshape.239.k_ref, bf16[192,128]{1,0:T(8,128)(2,1)S(1)} %reshape.240.v_ref, s32[192,192]{1,0:T(8,128)S(1)} %broadcast_in_dim.40.step_ref, ...), custom_call_target="tpu_custom_call" | custom-call | flops 75497472 | bytes 1376256 | tf_op jit(solution)/shard_map/pallas_call | solution.py:187
  129.9 4.3 %all-to-all-done.3.r_ref = bf16[16,56,128]{2,1,0:T(8,128)(2,1)S(1)} async-done(((bf16[16,56,128]{2,1,0:T(8,128)(2,1)}), bf16[16,56,128]{2,1,0:T(8,128)(2,1)S(1)}, u32[]{:S(2)}, u32[]{:S(2)}) %all-to-all-start.3) | async-done | bytes 229408 | tf_op jit(solution)/shard_map/all_to_all | solution.py:204
  134.3 1.0 shard_map.79
  (58 shorter events, 2.0 us)
Async XLA Ops:
  2.1 2.2 %copy-start = (bf16[1,3,64,512]{3,2,1,0:T(8,128)(2,1)S(1)}, bf16[1,3,64,512]{3,2,1,0:T(8,128)(2,1)}, u32[]{:S(2)}) copy-start(bf16[1,3,64,512]{3,2,1,0:T(8,128)(2,1)} %param.9) | copy-start | bytes 589828
  2.1 21.3 %copy-start.2 = (s32[16]{0:T(128)S(1)}, s32[16]{0:T(128)}, u32[]{:S(2)}) copy-start(s32[16]{0:T(128)} %param.13) | copy-start | bytes 196
  2.1 21.5 %collective-permute-start.1 = (bf16[4,528,128]{2,1,0:T(8,128)(2,1)S(1)}, bf16[4,528,128]{2,1,0:T(8,128)(2,1)S(1)}, u32[]{:S(2)}, u32[]{:S(2)}) collective-permute-start(bf16[4,528,128]{2,1,0:T(8,128)(2,1)S(1)} %pad_maximum_fusion.1), channel_id=1, source_target_pairs={{0,2},{1,3},{2,0},{3,1},{4,6},{5,7},{6,4},{7,5},{8,10},{9,11},{10,... | collective-permute-start | bytes 1622024 | tf_op jit(solution)/shard_map/ppermute | solution.py:226
  5.1 31.9 %all-to-all-start = ((bf16[16,48,128]{2,1,0:T(8,128)(2,1)}), bf16[16,48,128]{2,1,0:T(8,128)(2,1)S(1)}, u32[]{:S(2)}, u32[]{:S(2)}) async-start(bf16[16,48,128]{2,1,0:T(8,128)(2,1)} %bitcast.1), calls=%async_computation | async-start | bytes 393216 | tf_op jit(solution)/shard_map/all_to_all | solution.py:204
  23.7 29.2 %collective-permute-start.2 = (bf16[2,528,128]{2,1,0:T(8,128)(2,1)S(1)}, bf16[2,528,128]{2,1,0:T(8,128)(2,1)S(1)}, u32[]{:S(2)}, u32[]{:S(2)}) collective-permute-start(bf16[2,528,128]{2,1,0:T(8,128)(2,1)S(1)} %get-tuple-element.20), channel_id=1, source_target_pairs={{0,8},{1,9},{2,10},{3,11},{4,12},{5,13},{6,14},{7,15},{8,16},{9,17... | collective-permute-start | bytes 811016 | tf_op jit(solution)/shard_map/ppermute | solution.py:226
  27.1 25.8 %collective-permute-start.3 = (bf16[2,528,128]{2,1,0:T(8,128)(2,1)S(1)}, bf16[2,528,128]{2,1,0:T(8,128)(2,1)S(1)}, u32[]{:S(2)}, u32[]{:S(2)}) collective-permute-start(bf16[2,528,128]{2,1,0:T(8,128)(2,1)S(1)} %get-tuple-element.21), channel_id=1, source_target_pairs={{0,16},{1,17},{2,18},{3,19},{4,20},{5,21},{6,22},{7,23},{8,24},{9,... | collective-permute-start | bytes 811016 | tf_op jit(solution)/shard_map/ppermute | solution.py:226
  31.8 21.1 %collective-permute-start.4 = (bf16[2,528,128]{2,1,0:T(8,128)(2,1)S(1)}, bf16[2,528,128]{2,1,0:T(8,128)(2,1)S(1)}, u32[]{:S(2)}, u32[]{:S(2)}) collective-permute-start(bf16[2,528,128]{2,1,0:T(8,128)(2,1)S(1)} %get-tuple-element.22), channel_id=1, source_target_pairs={{0,24},{1,25},{2,26},{3,27},{4,28},{5,29},{6,30},{7,31},{8,0},{9,1... | collective-permute-start | bytes 811016 | tf_op jit(solution)/shard_map/ppermute | solution.py:226
  38.2 22.3 %all-to-all-start.1 = ((bf16[16,48,128]{2,1,0:T(8,128)(2,1)}), bf16[16,48,128]{2,1,0:T(8,128)(2,1)S(1)}, u32[]{:S(2)}, u32[]{:S(2)}) async-start(bf16[16,48,128]{2,1,0:T(8,128)(2,1)} %gather_fusion), calls=%async_computation.1 | async-start | bytes 393216 | tf_op jit(solution)/shard_map/all_to_all | solution.py:204
  53.0 13.7 %collective-permute-start.6 = (bf16[2176,128]{1,0:T(8,128)(2,1)S(1)}, bf16[2176,128]{1,0:T(8,128)(2,1)S(1)}, u32[]{:S(2)}, u32[]{:S(2)}) collective-permute-start(bf16[2176,128]{1,0:T(8,128)(2,1)S(1)} %get-tuple-element.24.v_a), channel_id=1, source_target_pairs={{0,1},{1,0},{2,3},{3,2},{4,5},{5,4},{6,7},{7,6},{8,9},{9,8},{10,11... | collective-permute-start | bytes 1671176 | tf_op jit(solution)/shard_map/ppermute | solution.py:226
  54.9 11.7 %collective-permute-start.5 = (bf16[2048,128]{1,0:T(8,128)(2,1)S(1)}, bf16[2048,128]{1,0:T(8,128)(2,1)S(1)}, u32[]{:S(2)}, u32[]{:S(2)}) collective-permute-start(bf16[2048,128]{1,0:T(8,128)(2,1)S(1)} %get-tuple-element.23.k_a), channel_id=1, source_target_pairs={{0,1},{1,0},{2,3},{3,2},{4,5},{5,4},{6,7},{7,6},{8,9},{9,8},{10,11... | collective-permute-start | bytes 1572872 | tf_op jit(solution)/shard_map/ppermute | solution.py:226
  60.5 8.6 %collective-permute-start = (bf16[768,128]{1,0:T(8,128)(2,1)S(1)}, bf16[768,128]{1,0:T(8,128)(2,1)S(1)}, u32[]{:S(2)}, u32[]{:S(2)}) collective-permute-start(bf16[768,128]{1,0:T(8,128)(2,1)S(1)} %bitcast.56), channel_id=1, source_target_pairs={{0,4},{1,5},{2,0},{3,1},{4,6},{5,7},{6,2},{7,3},{8,12},{9,13},{10,... | collective-permute-start | bytes 589832 | tf_op jit(solution)/shard_map/ppermute | solution.py:226
  63.0 13.3 %collective-permute-start.8 = (bf16[768,128]{1,0:T(8,128)(2,1)S(1)}, bf16[768,128]{1,0:T(8,128)(2,1)S(1)}, u32[]{:S(2)}, u32[]{:S(2)}) collective-permute-start(bf16[768,128]{1,0:T(8,128)(2,1)S(1)} %bitcast.57), channel_id=1, source_target_pairs={{0,0},{1,1},{2,4},{3,5},{4,2},{5,3},{6,6},{7,7},{8,8},{9,9},{10,12... | collective-permute-start | bytes 589832 | tf_op jit(solution)/shard_map/ppermute | solution.py:226
  73.6 14.9 %collective-permute-start.7 = (bf16[1056,128]{1,0:T(8,128)(2,1)S(1)}, bf16[1056,128]{1,0:T(8,128)(2,1)S(1)}, u32[]{:S(2)}, u32[]{:S(2)}) collective-permute-start(bf16[1056,128]{1,0:T(8,128)(2,1)S(1)} %shard_map.75), channel_id=1, source_target_pairs={{0,2},{1,3},{2,6},{3,7},{4,0},{5,1},{6,4},{7,5},{8,10},{9,11},{10,... | collective-permute-start | bytes 811016 | tf_op jit(solution)/shard_map/ppermute | solution.py:226
  80.8 7.7 %collective-permute-start.9 = (bf16[800,128]{1,0:T(8,128)(2,1)S(1)}, bf16[800,128]{1,0:T(8,128)(2,1)S(1)}, u32[]{:S(2)}, u32[]{:S(2)}) collective-permute-start(bf16[800,128]{1,0:T(8,128)(2,1)S(1)} %shard_map.76), channel_id=1, source_target_pairs={{0,0},{1,1},{2,4},{3,5},{4,2},{5,3},{6,6},{7,7},{8,8},{9,9},{10,12... | collective-permute-start | bytes 614408 | tf_op jit(solution)/shard_map/ppermute | solution.py:226
  89.6 21.8 %all-to-all-start.2 = ((bf16[16,56,128]{2,1,0:T(8,128)(2,1)}), bf16[16,56,128]{2,1,0:T(8,128)(2,1)S(1)}, u32[]{:S(2)}, u32[]{:S(2)}) async-start(bf16[16,56,128]{2,1,0:T(8,128)(2,1)} %shard_map.77), calls=%async_computation.2 | async-start | bytes 458752 | tf_op jit(solution)/shard_map/all_to_all | solution.py:204
  105.2 6.1 %collective-permute-start.10 = (bf16[2,8,16,128]{3,2,1,0:T(8,128)(2,1)S(1)}, bf16[2,8,16,128]{3,2,1,0:T(8,128)(2,1)S(1)}, u32[]{:S(2)}, u32[]{:S(2)}) collective-permute-start(bf16[2,8,16,128]{3,2,1,0:T(8,128)(2,1)S(1)} %pad_maximum_fusion.3), channel_id=1, source_target_pairs={{0,0},{1,1},{2,4},{3,5},{4,2},{5,3},{6,6},{7,7},{8,8},{9,9},{10,12... | collective-permute-start | bytes 196616 | tf_op jit(solution)/shard_map/ppermute | solution.py:226
  112.6 15.3 %copy-start.1 = (s32[1,64]{1,0:T(1,128)S(1)}, s32[1,64]{1,0:T(1,128)}, u32[]{:S(2)}) copy-start(s32[1,64]{1,0:T(1,128)} %param.12) | copy-start | bytes 772
  112.6 21.7 %all-to-all-start.3 = ((bf16[16,56,128]{2,1,0:T(8,128)(2,1)}), bf16[16,56,128]{2,1,0:T(8,128)(2,1)S(1)}, u32[]{:S(2)}, u32[]{:S(2)}) async-start(bf16[16,56,128]{2,1,0:T(8,128)(2,1)} %gather_fusion.1), calls=%async_computation.3 | async-start | bytes 458752 | tf_op jit(solution)/shard_map/all_to_all | solution.py:204

commit v7 on v6

--- a/solution.py
+++ b/solution.py
@@ -234,16 +234,16 @@
     def back_1(xx, zz, cc):
         return xx, turn(zz ^ 2), cc
 
-    fresh = jnp.stack([sample_step_keys[0], suffix_values[0]])
-    fresh = jnp.transpose(fresh, (3, 0, 1, 2, 4)).reshape(8, 4 * STEPS, HD)
-    fresh = jnp.pad(fresh, ((0, 0), (0, SUF - 4 * STEPS), (0, 0)))
+    fresh = jnp.stack([sample_step_keys[0], suffix_values[0]]).reshape(4 * STEPS, 4, 2, HD)
 
     def of_parity(which):
         parts = [
             lax.dynamic_index_in_dim(a.reshape(4, 2, -1, HD), which, 1, keepdims=False)
-            for a in (keys, values, fresh)
+            for a in (keys, values)
         ]
-        return jnp.concatenate(parts, axis=1)
+        tokens = jnp.where(which == 0, fresh[:, :, 0], fresh[:, :, 1])
+        tokens = jnp.pad(jnp.transpose(tokens, (1, 0, 2)), ((0, 0), (0, SUF - 4 * STEPS), (0, 0)))
+        return jnp.concatenate([*parts, tokens], axis=1)
 
     rows = jnp.transpose(queries[0].reshape(TOKENS, HEADS, HD), (1, 0, 2))
     pieces = rows.reshape(PIECES, PIECE, HD)

time: 136 us -> 136 us (level)
  the two profiles are of different devices: /device:TPU:56 before, /device:TPU:32 now
where the time goes in v7:
time: 136 us; the launch traced here: 135 us
  starting transfers between devices  98 us (72%)
  waiting for transfers between devices  16.4 us (12%)
  Pallas kernels  13 us (10%)
  local copies, waits for them, and re-layouts  5.94 us (4%)
    all_to_all x4, starting transfers between devices, exchange(): lax.all_to_all(a, 'prompt', 0, 0, tiled=True, axis_index_groups=[order])  61.6 us
    ppermute x11, starting transfers between devices, permute(): return lax.ppermute(a, 'tp', pairs)  36.4 us
    pallas_call x7, Pallas kernels, call(): pl.pallas_call(kernel, out_shape=tuple(outs) if many else outs[0], in_spe...  13 us
    ppermute x11, waiting for transfers between devices, permute(): return lax.ppermute(a, 'tp', pairs)  11.6 us
    all_to_all x4, waiting for transfers between devices, exchange(): lax.all_to_all(a, 'prompt', 0, 0, tiled=True, axis_index_groups=[order])  4.78 us
  transfers between devices with their start and end apart: 15, of which 6 were waited for; matrix products, arithmetic and copies ran while one was open for 3% of the time, Pallas kernels for 8%

profile of v7, /device:TPU:32, one launch (start us, length us, event | category | flops | bytes accessed | tf_op | source)
XLA Modules:
  0.0 135.0 jit_solution(6637499303766693582)
XLA Ops:
  0.0 0.7 pad_maximum_fusion.2
  0.8 1.3 dynamic-slice_bitcast_fusion
  2.2 7.5 %collective-permute-start.1 = (bf16[4,528,128]{2,1,0:T(8,128)(2,1)S(1)}, bf16[4,528,128]{2,1,0:T(8,128)(2,1)S(1)}, u32[]{:S(2)}, u32[]{:S(2)}) collective-permute-start(bf16[4,528,128]{2,1,0:T(8,128)(2,1)S(1)} %fusion.3), channel_id=1, source_target_pairs={{0,2},{1,3},{2,0},{3,1},{4,6},{5,7},{6,4},{7,5},{8,10},{9,11},{10,... | collective-permute-start | bytes 1622024 | tf_op jit(solution)/shard_map/ppermute | solution.py:226
  9.8 0.7 copy.20
  10.5 15.5 %all-to-all-start = ((bf16[16,48,128]{2,1,0:T(8,128)(2,1)}), bf16[16,48,128]{2,1,0:T(8,128)(2,1)S(1)}, u32[]{:S(2)}, u32[]{:S(2)}) async-start(bf16[16,48,128]{2,1,0:T(8,128)(2,1)} %bitcast.1), calls=%async_computation | async-start | bytes 393216 | tf_op jit(solution)/shard_map/all_to_all | solution.py:204
  26.2 3.4 %collective-permute-start.2 = (bf16[2,528,128]{2,1,0:T(8,128)(2,1)S(1)}, bf16[2,528,128]{2,1,0:T(8,128)(2,1)S(1)}, u32[]{:S(2)}, u32[]{:S(2)}) collective-permute-start(bf16[2,528,128]{2,1,0:T(8,128)(2,1)S(1)} %get-tuple-element.20), channel_id=1, source_target_pairs={{0,8},{1,9},{2,10},{3,11},{4,12},{5,13},{6,14},{7,15},{8,16},{9,17... | collective-permute-start | bytes 811016 | tf_op jit(solution)/shard_map/ppermute | solution.py:226
  29.6 4.6 %collective-permute-start.3 = (bf16[2,528,128]{2,1,0:T(8,128)(2,1)S(1)}, bf16[2,528,128]{2,1,0:T(8,128)(2,1)S(1)}, u32[]{:S(2)}, u32[]{:S(2)}) collective-permute-start(bf16[2,528,128]{2,1,0:T(8,128)(2,1)S(1)} %get-tuple-element.21), channel_id=1, source_target_pairs={{0,16},{1,17},{2,18},{3,19},{4,20},{5,21},{6,22},{7,23},{8,24},{9,... | collective-permute-start | bytes 811016 | tf_op jit(solution)/shard_map/ppermute | solution.py:226
  34.3 3.3 %collective-permute-start.4 = (bf16[2,528,128]{2,1,0:T(8,128)(2,1)S(1)}, bf16[2,528,128]{2,1,0:T(8,128)(2,1)S(1)}, u32[]{:S(2)}, u32[]{:S(2)}) collective-permute-start(bf16[2,528,128]{2,1,0:T(8,128)(2,1)S(1)} %get-tuple-element.22), channel_id=1, source_target_pairs={{0,24},{1,25},{2,26},{3,27},{4,28},{5,29},{6,30},{7,31},{8,0},{9,1... | collective-permute-start | bytes 811016 | tf_op jit(solution)/shard_map/ppermute | solution.py:226
  37.8 1.2 all-to-all-done
  39.0 1.2 gather_fusion
  40.2 15.1 %all-to-all-start.1 = ((bf16[16,48,128]{2,1,0:T(8,128)(2,1)}), bf16[16,48,128]{2,1,0:T(8,128)(2,1)S(1)}, u32[]{:S(2)}, u32[]{:S(2)}) async-start(bf16[16,48,128]{2,1,0:T(8,128)(2,1)} %gather_fusion), calls=%async_computation.1 | async-start | bytes 393216 | tf_op jit(solution)/shard_map/all_to_all | solution.py:204
  55.5 1.9 %collective-permute-start.6 = (bf16[2176,128]{1,0:T(8,128)(2,1)S(1)}, bf16[2176,128]{1,0:T(8,128)(2,1)S(1)}, u32[]{:S(2)}, u32[]{:S(2)}) collective-permute-start(bf16[2176,128]{1,0:T(8,128)(2,1)S(1)} %get-tuple-element.24.v_a), channel_id=1, source_target_pairs={{0,1},{1,0},{2,3},{3,2},{4,5},{5,4},{6,7},{7,6},{8,9},{9,8},{10,11... | collective-permute-start | bytes 1671176 | tf_op jit(solution)/shard_map/ppermute | solution.py:226
  57.4 2.4 %collective-permute-start.5 = (bf16[2048,128]{1,0:T(8,128)(2,1)S(1)}, bf16[2048,128]{1,0:T(8,128)(2,1)S(1)}, u32[]{:S(2)}, u32[]{:S(2)}) collective-permute-start(bf16[2048,128]{1,0:T(8,128)(2,1)S(1)} %get-tuple-element.23.k_a), channel_id=1, source_target_pairs={{0,1},{1,0},{2,3},{3,2},{4,5},{5,4},{6,7},{7,6},{8,9},{9,8},{10,11... | collective-permute-start | bytes 1572872 | tf_op jit(solution)/shard_map/ppermute | solution.py:226
  59.8 2.0 %all-to-all-done.1 = bf16[16,48,128]{2,1,0:T(8,128)(2,1)S(1)} async-done(((bf16[16,48,128]{2,1,0:T(8,128)(2,1)}), bf16[16,48,128]{2,1,0:T(8,128)(2,1)S(1)}, u32[]{:S(2)}, u32[]{:S(2)}) %all-to-all-start.1) | async-done | bytes 196640 | tf_op jit(solution)/shard_map/all_to_all | solution.py:204
  61.8 2.1 %collective-permute-start = (bf16[768,128]{1,0:T(8,128)(2,1)S(1)}, bf16[768,128]{1,0:T(8,128)(2,1)S(1)}, u32[]{:S(2)}, u32[]{:S(2)}) collective-permute-start(bf16[768,128]{1,0:T(8,128)(2,1)S(1)} %bitcast.58), channel_id=1, source_target_pairs={{0,4},{1,5},{2,0},{3,1},{4,6},{5,7},{6,2},{7,3},{8,12},{9,13},{10,... | collective-permute-start | bytes 589832 | tf_op jit(solution)/shard_map/ppermute | solution.py:226
  64.0 3.5 %collective-permute-start.8 = (bf16[768,128]{1,0:T(8,128)(2,1)S(1)}, bf16[768,128]{1,0:T(8,128)(2,1)S(1)}, u32[]{:S(2)}, u32[]{:S(2)}) collective-permute-start(bf16[768,128]{1,0:T(8,128)(2,1)S(1)} %bitcast.59), channel_id=1, source_target_pairs={{0,0},{1,1},{2,4},{3,5},{4,2},{5,3},{6,6},{7,7},{8,8},{9,9},{10,12... | collective-permute-start | bytes 589832 | tf_op jit(solution)/shard_map/ppermute | solution.py:226
  67.6 2.8 %collective-permute-done.q_ref = bf16[768,128]{1,0:T(8,128)(2,1)S(1)} collective-permute-done((bf16[768,128]{1,0:T(8,128)(2,1)S(1)}, bf16[768,128]{1,0:T(8,128)(2,1)S(1)}, u32[]{:S(2)}, u32[]{:S(2)}) %collective-permute-start) | collective-permute-done | bytes 196640 | tf_op jit(solution)/shard_map/ppermute | solution.py:226
  70.4 4.5 %shard_map.75 = bf16[1056,128]{1,0:T(8,128)(2,1)S(1)} custom-call(bf16[768,128]{1,0:T(8,128)(2,1)S(1)} %collective-permute-done.q_ref, bf16[2048,128]{1,0:T(8,128)(2,1)S(1)} %get-tuple-element.23.k_a, bf16[2176,128]{1,0:T(8,128)(2,1)S(1)} %get-tuple-element.24.v_a, bf16[2048,128]{1,0:T(8,128)(2,1)S(1)} %collective-permute-done.5.k_b, ...), custom_call_target="tpu_custom_call" | custom-call | flops 1610612736 | bytes 2629632 | tf_op jit(solution)/shard_map/pallas_call | solution.py:187
  74.9 2.6 %collective-permute-start.7 = (bf16[1056,128]{1,0:T(8,128)(2,1)S(1)}, bf16[1056,128]{1,0:T(8,128)(2,1)S(1)}, u32[]{:S(2)}, u32[]{:S(2)}) collective-permute-start(bf16[1056,128]{1,0:T(8,128)(2,1)S(1)} %shard_map.75), channel_id=1, source_target_pairs={{0,2},{1,3},{2,6},{3,7},{4,0},{5,1},{6,4},{7,5},{8,10},{9,11},{10,... | collective-permute-start | bytes 811016 | tf_op jit(solution)/shard_map/ppermute | solution.py:226
  77.5 4.6 %shard_map.76 = bf16[800,128]{1,0:T(8,128)(2,1)S(1)} custom-call(bf16[768,128]{1,0:T(8,128)(2,1)S(1)} %collective-permute-done.8.q_ref, bf16[2048,128]{1,0:T(8,128)(2,1)S(1)} %get-tuple-element.23.k_a, bf16[2176,128]{1,0:T(8,128)(2,1)S(1)} %get-tuple-element.24.v_a, bf16[2048,128]{1,0:T(8,128)(2,1)S(1)} %collective-permute-done.5.k_b, ...), custom_call_target="tpu_custom_call" | custom-call | flops 1610612736 | bytes 2564096 | tf_op jit(solution)/shard_map/pallas_call | solution.py:187
  82.1 3.0 %collective-permute-start.9 = (bf16[800,128]{1,0:T(8,128)(2,1)S(1)}, bf16[800,128]{1,0:T(8,128)(2,1)S(1)}, u32[]{:S(2)}, u32[]{:S(2)}) collective-permute-start(bf16[800,128]{1,0:T(8,128)(2,1)S(1)} %shard_map.76), channel_id=1, source_target_pairs={{0,0},{1,1},{2,4},{3,5},{4,2},{5,3},{6,6},{7,7},{8,8},{9,9},{10,12... | collective-permute-start | bytes 614408 | tf_op jit(solution)/shard_map/ppermute | solution.py:226
  85.2 4.6 %collective-permute-done.9.b_ref = bf16[800,128]{1,0:T(8,128)(2,1)S(1)} collective-permute-done((bf16[800,128]{1,0:T(8,128)(2,1)S(1)}, bf16[800,128]{1,0:T(8,128)(2,1)S(1)}, u32[]{:S(2)}, u32[]{:S(2)}) %collective-permute-start.9) | collective-permute-done | bytes 204832 | tf_op jit(solution)/shard_map/ppermute | solution.py:226
  89.7 1.1 shard_map.77
  90.8 16.4 %all-to-all-start.2 = ((bf16[16,56,128]{2,1,0:T(8,128)(2,1)}), bf16[16,56,128]{2,1,0:T(8,128)(2,1)S(1)}, u32[]{:S(2)}, u32[]{:S(2)}) async-start(bf16[16,56,128]{2,1,0:T(8,128)(2,1)} %shard_map.77), calls=%async_computation.2 | async-start | bytes 458752 | tf_op jit(solution)/shard_map/all_to_all | solution.py:204
  107.6 1.9 %collective-permute-start.10 = (bf16[2,8,16,128]{3,2,1,0:T(8,128)(2,1)S(1)}, bf16[2,8,16,128]{3,2,1,0:T(8,128)(2,1)S(1)}, u32[]{:S(2)}, u32[]{:S(2)}) collective-permute-start(bf16[2,8,16,128]{3,2,1,0:T(8,128)(2,1)S(1)} %pad_maximum_fusion.1), channel_id=1, source_target_pairs={{0,0},{1,1},{2,4},{3,5},{4,2},{5,3},{6,6},{7,7},{8,8},{9,9},{10,12... | collective-permute-start | bytes 196616 | tf_op jit(solution)/shard_map/ppermute | solution.py:226
  109.6 4.2 %collective-permute-done.10 = bf16[2,8,16,128]{3,2,1,0:T(8,128)(2,1)S(1)} collective-permute-done((bf16[2,8,16,128]{3,2,1,0:T(8,128)(2,1)S(1)}, bf16[2,8,16,128]{3,2,1,0:T(8,128)(2,1)S(1)}, u32[]{:S(2)}, u32[]{:S(2)}) %collective-permute-start.10) | collective-permute-done | bytes 65568 | tf_op jit(solution)/shard_map/ppermute | solution.py:226
  113.8 1.3 gather_fusion.1
  115.1 14.6 %all-to-all-start.3 = ((bf16[16,56,128]{2,1,0:T(8,128)(2,1)}), bf16[16,56,128]{2,1,0:T(8,128)(2,1)S(1)}, u32[]{:S(2)}, u32[]{:S(2)}) async-start(bf16[16,56,128]{2,1,0:T(8,128)(2,1)} %gather_fusion.1), calls=%async_computation.3 | async-start | bytes 458752 | tf_op jit(solution)/shard_map/all_to_all | solution.py:204
  129.9 0.1 iota.57
  130.7 1.7 %shard_map.78 = (f32[768,128]{1,0:T(8,128)S(1)}, f32[768,128]{1,0:T(8,128)S(1)}) custom-call(bf16[768,128]{1,0:T(8,128)(2,1)} %bitcast.25.q_ref, bf16[192,128]{1,0:T(8,128)(2,1)S(1)} %reshape.238.k_ref, bf16[192,128]{1,0:T(8,128)(2,1)S(1)} %reshape.239.v_ref, s32[192,192]{1,0:T(8,128)S(1)} %broadcast_in_dim.40.step_ref, ...), custom_call_target="tpu_custom_call" | custom-call | flops 75497472 | bytes 1376256 | tf_op jit(solution)/shard_map/pallas_call | solution.py:187
  132.4 1.6 %all-to-all-done.3.r_ref = bf16[16,56,128]{2,1,0:T(8,128)(2,1)S(1)} async-done(((bf16[16,56,128]{2,1,0:T(8,128)(2,1)}), bf16[16,56,128]{2,1,0:T(8,128)(2,1)S(1)}, u32[]{:S(2)}, u32[]{:S(2)}) %all-to-all-start.3) | async-done | bytes 229408 | tf_op jit(solution)/shard_map/all_to_all | solution.py:204
  134.1 1.0 shard_map.79
  (57 shorter events, 2.0 us)
Async XLA Ops:
  2.1 7.6 %copy-start = (bf16[1,3,64,512]{3,2,1,0:T(8,128)(2,1)S(1)}, bf16[1,3,64,512]{3,2,1,0:T(8,128)(2,1)}, u32[]{:S(2)}) copy-start(bf16[1,3,64,512]{3,2,1,0:T(8,128)(2,1)} %param.9) | copy-start | bytes 589828
  2.1 23.8 %copy-start.2 = (s32[16]{0:T(128)S(1)}, s32[16]{0:T(128)}, u32[]{:S(2)}) copy-start(s32[16]{0:T(128)} %param.13) | copy-start | bytes 196
  2.2 23.9 %collective-permute-start.1 = (bf16[4,528,128]{2,1,0:T(8,128)(2,1)S(1)}, bf16[4,528,128]{2,1,0:T(8,128)(2,1)S(1)}, u32[]{:S(2)}, u32[]{:S(2)}) collective-permute-start(bf16[4,528,128]{2,1,0:T(8,128)(2,1)S(1)} %fusion.3), channel_id=1, source_target_pairs={{0,2},{1,3},{2,0},{3,1},{4,6},{5,7},{6,4},{7,5},{8,10},{9,11},{10,... | collective-permute-start | bytes 1622024 | tf_op jit(solution)/shard_map/ppermute | solution.py:226
  10.5 28.5 %all-to-all-start = ((bf16[16,48,128]{2,1,0:T(8,128)(2,1)}), bf16[16,48,128]{2,1,0:T(8,128)(2,1)S(1)}, u32[]{:S(2)}, u32[]{:S(2)}) async-start(bf16[16,48,128]{2,1,0:T(8,128)(2,1)} %bitcast.1), calls=%async_computation | async-start | bytes 393216 | tf_op jit(solution)/shard_map/all_to_all | solution.py:204
  26.2 29.2 %collective-permute-start.2 = (bf16[2,528,128]{2,1,0:T(8,128)(2,1)S(1)}, bf16[2,528,128]{2,1,0:T(8,128)(2,1)S(1)}, u32[]{:S(2)}, u32[]{:S(2)}) collective-permute-start(bf16[2,528,128]{2,1,0:T(8,128)(2,1)S(1)} %get-tuple-element.20), channel_id=1, source_target_pairs={{0,8},{1,9},{2,10},{3,11},{4,12},{5,13},{6,14},{7,15},{8,16},{9,17... | collective-permute-start | bytes 811016 | tf_op jit(solution)/shard_map/ppermute | solution.py:226
  29.6 25.8 %collective-permute-start.3 = (bf16[2,528,128]{2,1,0:T(8,128)(2,1)S(1)}, bf16[2,528,128]{2,1,0:T(8,128)(2,1)S(1)}, u32[]{:S(2)}, u32[]{:S(2)}) collective-permute-start(bf16[2,528,128]{2,1,0:T(8,128)(2,1)S(1)} %get-tuple-element.21), channel_id=1, source_target_pairs={{0,16},{1,17},{2,18},{3,19},{4,20},{5,21},{6,22},{7,23},{8,24},{9,... | collective-permute-start | bytes 811016 | tf_op jit(solution)/shard_map/ppermute | solution.py:226
  34.3 21.1 %collective-permute-start.4 = (bf16[2,528,128]{2,1,0:T(8,128)(2,1)S(1)}, bf16[2,528,128]{2,1,0:T(8,128)(2,1)S(1)}, u32[]{:S(2)}, u32[]{:S(2)}) collective-permute-start(bf16[2,528,128]{2,1,0:T(8,128)(2,1)S(1)} %get-tuple-element.22), channel_id=1, source_target_pairs={{0,24},{1,25},{2,26},{3,27},{4,28},{5,29},{6,30},{7,31},{8,0},{9,1... | collective-permute-start | bytes 811016 | tf_op jit(solution)/shard_map/ppermute | solution.py:226
  40.2 21.6 %all-to-all-start.1 = ((bf16[16,48,128]{2,1,0:T(8,128)(2,1)}), bf16[16,48,128]{2,1,0:T(8,128)(2,1)S(1)}, u32[]{:S(2)}, u32[]{:S(2)}) async-start(bf16[16,48,128]{2,1,0:T(8,128)(2,1)} %gather_fusion), calls=%async_computation.1 | async-start | bytes 393216 | tf_op jit(solution)/shard_map/all_to_all | solution.py:204
  55.5 12.1 %collective-permute-start.6 = (bf16[2176,128]{1,0:T(8,128)(2,1)S(1)}, bf16[2176,128]{1,0:T(8,128)(2,1)S(1)}, u32[]{:S(2)}, u32[]{:S(2)}) collective-permute-start(bf16[2176,128]{1,0:T(8,128)(2,1)S(1)} %get-tuple-element.24.v_a), channel_id=1, source_target_pairs={{0,1},{1,0},{2,3},{3,2},{4,5},{5,4},{6,7},{7,6},{8,9},{9,8},{10,11... | collective-permute-start | bytes 1671176 | tf_op jit(solution)/shard_map/ppermute | solution.py:226
  57.4 10.2 %collective-permute-start.5 = (bf16[2048,128]{1,0:T(8,128)(2,1)S(1)}, bf16[2048,128]{1,0:T(8,128)(2,1)S(1)}, u32[]{:S(2)}, u32[]{:S(2)}) collective-permute-start(bf16[2048,128]{1,0:T(8,128)(2,1)S(1)} %get-tuple-element.23.k_a), channel_id=1, source_target_pairs={{0,1},{1,0},{2,3},{3,2},{4,5},{5,4},{6,7},{7,6},{8,9},{9,8},{10,11... | collective-permute-start | bytes 1572872 | tf_op jit(solution)/shard_map/ppermute | solution.py:226
  61.8 8.6 %collective-permute-start = (bf16[768,128]{1,0:T(8,128)(2,1)S(1)}, bf16[768,128]{1,0:T(8,128)(2,1)S(1)}, u32[]{:S(2)}, u32[]{:S(2)}) collective-permute-start(bf16[768,128]{1,0:T(8,128)(2,1)S(1)} %bitcast.58), channel_id=1, source_target_pairs={{0,4},{1,5},{2,0},{3,1},{4,6},{5,7},{6,2},{7,3},{8,12},{9,13},{10,... | collective-permute-start | bytes 589832 | tf_op jit(solution)/shard_map/ppermute | solution.py:226
  64.0 13.6 %collective-permute-start.8 = (bf16[768,128]{1,0:T(8,128)(2,1)S(1)}, bf16[768,128]{1,0:T(8,128)(2,1)S(1)}, u32[]{:S(2)}, u32[]{:S(2)}) collective-permute-start(bf16[768,128]{1,0:T(8,128)(2,1)S(1)} %bitcast.59), channel_id=1, source_target_pairs={{0,0},{1,1},{2,4},{3,5},{4,2},{5,3},{6,6},{7,7},{8,8},{9,9},{10,12... | collective-permute-start | bytes 589832 | tf_op jit(solution)/shard_map/ppermute | solution.py:226
  74.9 14.8 %collective-permute-start.7 = (bf16[1056,128]{1,0:T(8,128)(2,1)S(1)}, bf16[1056,128]{1,0:T(8,128)(2,1)S(1)}, u32[]{:S(2)}, u32[]{:S(2)}) collective-permute-start(bf16[1056,128]{1,0:T(8,128)(2,1)S(1)} %shard_map.75), channel_id=1, source_target_pairs={{0,2},{1,3},{2,6},{3,7},{4,0},{5,1},{6,4},{7,5},{8,10},{9,11},{10,... | collective-permute-start | bytes 811016 | tf_op jit(solution)/shard_map/ppermute | solution.py:226
  82.1 7.7 %collective-permute-start.9 = (bf16[800,128]{1,0:T(8,128)(2,1)S(1)}, bf16[800,128]{1,0:T(8,128)(2,1)S(1)}, u32[]{:S(2)}, u32[]{:S(2)}) collective-permute-start(bf16[800,128]{1,0:T(8,128)(2,1)S(1)} %shard_map.76), channel_id=1, source_target_pairs={{0,0},{1,1},{2,4},{3,5},{4,2},{5,3},{6,6},{7,7},{8,8},{9,9},{10,12... | collective-permute-start | bytes 614408 | tf_op jit(solution)/shard_map/ppermute | solution.py:226
  90.8 23.0 %all-to-all-start.2 = ((bf16[16,56,128]{2,1,0:T(8,128)(2,1)}), bf16[16,56,128]{2,1,0:T(8,128)(2,1)S(1)}, u32[]{:S(2)}, u32[]{:S(2)}) async-start(bf16[16,56,128]{2,1,0:T(8,128)(2,1)} %shard_map.77), calls=%async_computation.2 | async-start | bytes 458752 | tf_op jit(solution)/shard_map/all_to_all | solution.py:204
  107.6 6.1 %collective-permute-start.10 = (bf16[2,8,16,128]{3,2,1,0:T(8,128)(2,1)S(1)}, bf16[2,8,16,128]{3,2,1,0:T(8,128)(2,1)S(1)}, u32[]{:S(2)}, u32[]{:S(2)}) collective-permute-start(bf16[2,8,16,128]{3,2,1,0:T(8,128)(2,1)S(1)} %pad_maximum_fusion.1), channel_id=1, source_target_pairs={{0,0},{1,1},{2,4},{3,5},{4,2},{5,3},{6,6},{7,7},{8,8},{9,9},{10,12... | collective-permute-start | bytes 196616 | tf_op jit(solution)/shard_map/ppermute | solution.py:226
  115.1 15.4 %copy-start.1 = (s32[1,64]{1,0:T(1,128)S(1)}, s32[1,64]{1,0:T(1,128)}, u32[]{:S(2)}) copy-start(s32[1,64]{1,0:T(1,128)} %param.12) | copy-start | bytes 772
  115.1 18.9 %all-to-all-start.3 = ((bf16[16,56,128]{2,1,0:T(8,128)(2,1)}), bf16[16,56,128]{2,1,0:T(8,128)(2,1)S(1)}, u32[]{:S(2)}, u32[]{:S(2)}) async-start(bf16[16,56,128]{2,1,0:T(8,128)(2,1)} %gather_fusion.1), calls=%async_computation.3 | async-start | bytes 458752 | tf_op jit(solution)/shard_map/all_to_all | solution.py:204
